TPU v7x, 256 devices: a whole 4x4x8 slice. The times are simulated.
256 devices in a mesh: seq: 16 (over z, y_lo), chan: 16 (over x, y_hi, core).
Axes of the slice: x: 4, y: 4 (y_hi: 2, y_lo: 2; y = y_hi * 2 + y_lo), z: 8, core: 2. Of those that a mesh axis runs over, the one named last changes fastest.
Arguments:
- hidden_in: bfloat16 [8192, 4096], P('seq', 'chan'), may hold values from -6 to 6
- in_weight: bfloat16 [3, 4096, 2048], P(None, None, 'chan'), may hold values from -0.09375 to 0.09375
- conv_taps: float32 [3, 3, 2048], P(None, None, 'chan'), may hold values from -3 to 3
- decay_rate: float32 [16, 2048], P(None, 'chan'), may hold values from 0.0002 to 0.05
- mode_angle: float32 [16, 2048], P(None, 'chan'), may hold values from -3.140625 to 3.140625
- residue: float32 [2, 16, 2048], P(None, None, 'chan'), may hold values from -0.2 to 0.2
- skip_gain: float32 [2048], P('chan'), may hold values from -5 to 5
- out_grad: float32 [2048, 8192], P('chan', 'seq'), may hold values from -6 to 6
Outputs:
- mixed_out: float32 [2048, 8192], P('chan', 'seq')
- input_grad: float32 [8192, 4096], P('seq', 'chan')
- weight_grad: float32 [3, 4096, 2048], P(None, 'seq', 'chan')
- taps_grad: float32 [3, 3, 2048], P(None, None, 'chan')
- residue_grad: float32 [2, 16, 2048], P(None, None, 'chan')
- skip_grad: float32 [2048], P('chan')
All inputs are finite; a program needn't handle non-finite values.
Results may differ from a plain program's by a relative error of at most 0.0029.
Values may be sent and summed in bfloat16 or wider, within the bound.
No kernel may reach another device: no remote copies, remote signals or barrier semaphores. Data moves between devices by JAX's collectives and lax.ppermute only.
A program may use at most 128 MiB of HBM per device.

v0:
```python
import math

import jax
import jax.numpy as jnp
from jax import lax
from jax.sharding import PartitionSpec as P

HIGH = lax.Precision.HIGHEST


def from_behind(x, axis, by):
    length = lax.axis_size(axis)
    pairs = [(i, i + by) for i in range(length) if 0 <= i + by < length]
    return lax.ppermute(x, axis, pairs)


def make_tables(length):
    padlen = 2 * length
    second = 128
    first_size = padlen // second
    index_one = jnp.arange(first_size, dtype=jnp.int32)
    index_two = jnp.arange(second, dtype=jnp.int32)
    phase_one = (index_one[:, None] * index_one[None, :] % first_size).astype(jnp.float32) * (
        2.0 * math.pi / first_size
    )
    phase_two = (index_two[:, None] * index_two[None, :] % second).astype(jnp.float32) * (
        2.0 * math.pi / second
    )
    phase_twist = (index_one[:, None] * index_two[None, :] % padlen).astype(jnp.float32) * (
        2.0 * math.pi / padlen
    )
    return (
        jnp.cos(phase_one),
        jnp.sin(phase_one),
        jnp.cos(phase_twist),
        jnp.sin(phase_twist),
        jnp.cos(phase_two),
        jnp.sin(phase_two),
    )


def forward_transform(signal, tables):
    cos_one, sin_one, twist_cos, twist_sin, cos_two, sin_two = tables
    half_rows = cos_one.shape[0] // 2
    blocks = signal.reshape(signal.shape[0], half_rows, 128)
    real_a = jnp.einsum("ka,gab->gkb", cos_one[:, :half_rows], blocks, precision=HIGH)
    imag_a = -jnp.einsum("ka,gab->gkb", sin_one[:, :half_rows], blocks, precision=HIGH)
    real_b = real_a * twist_cos + imag_a * twist_sin
    imag_b = imag_a * twist_cos - real_a * twist_sin
    out_re = jnp.einsum("gkb,bm->gkm", real_b, cos_two, precision=HIGH) + jnp.einsum(
        "gkb,bm->gkm", imag_b, sin_two, precision=HIGH
    )
    out_im = jnp.einsum("gkb,bm->gkm", imag_b, cos_two, precision=HIGH) - jnp.einsum(
        "gkb,bm->gkm", real_b, sin_two, precision=HIGH
    )
    return (out_re, out_im)


def inverse_transform(spec_re, spec_im, tables):
    cos_one, sin_one, twist_cos, twist_sin, cos_two, sin_two = tables
    half_rows = cos_one.shape[0] // 2
    real_c = jnp.einsum("gkm,bm->gkb", spec_re, cos_two, precision=HIGH) - jnp.einsum(
        "gkm,bm->gkb", spec_im, sin_two, precision=HIGH
    )
    imag_c = jnp.einsum("gkm,bm->gkb", spec_im, cos_two, precision=HIGH) + jnp.einsum(
        "gkm,bm->gkb", spec_re, sin_two, precision=HIGH
    )
    real_d = real_c * twist_cos - imag_c * twist_sin
    imag_d = imag_c * twist_cos + real_c * twist_sin
    signal = jnp.einsum("ak,gkb->gab", cos_one[:half_rows], real_d, precision=HIGH) - jnp.einsum(
        "ak,gkb->gab", sin_one[:half_rows], imag_d, precision=HIGH
    )
    padlen = cos_one.shape[0] * 128
    return signal.reshape(signal.shape[0], padlen // 2) / padlen


def mode_basis(decay_rate, mode_angle, positions):
    fading = jnp.exp(-decay_rate[:, :, None] * positions)
    return (
        fading * jnp.cos(mode_angle[:, :, None] * positions),
        fading * jnp.sin(mode_angle[:, :, None] * positions),
    )


def residue_sums(grad_resp, decay_cos, decay_sin):
    return jnp.stack(
        [
            jnp.sum(grad_resp[None] * decay_cos, axis=2),
            -jnp.sum(grad_resp[None] * decay_sin, axis=2),
        ]
    )


def on_device(
    hidden_in, in_weight, conv_taps, decay_rate, mode_angle, residue, skip_gain, out_grad
):
    tok_rows = hidden_in.shape[0]
    seq_count = lax.axis_size("seq")
    length = tok_rows * seq_count
    gathered = lax.all_gather(hidden_in, "chan", axis=1, tiled=True)
    proj = jnp.einsum("td,kdc->kct", gathered, in_weight, preferred_element_type=jnp.float32)
    rim_cols = from_behind(proj[:, :, tok_rows - 2 :], "seq", 1)
    extended = jnp.concatenate([rim_cols, proj], axis=2)
    branches = sum(
        (
            conv_taps[:, offset, :, None] * extended[:, :, 2 - offset : 2 - offset + tok_rows]
            for offset in range(3)
        )
    )
    query_branch = branches[0]
    key_branch = branches[1]
    value_branch = branches[2]
    product = key_branch * value_branch
    tables = make_tables(length)
    offset_start = lax.axis_index("seq") * tok_rows
    positions = (offset_start + jnp.arange(tok_rows, dtype=jnp.int32)).astype(jnp.float32)
    decay_cos, decay_sin = mode_basis(decay_rate, mode_angle, positions)
    filter_seq = jnp.sum(
        residue[0][:, :, None] * decay_cos - residue[1][:, :, None] * decay_sin, axis=0
    )
    prod_cols, filter_cols = (
        lax.all_to_all(product, "seq", split_axis=0, concat_axis=1, tiled=True),
        lax.all_to_all(filter_seq, "seq", split_axis=0, concat_axis=1, tiled=True),
    )
    prod_re, prod_im = forward_transform(prod_cols, tables)
    filt_re, filt_im = forward_transform(filter_cols, tables)
    conv_cols = inverse_transform(
        prod_re * filt_re - prod_im * filt_im, prod_re * filt_im + prod_im * filt_re, tables
    )
    conv_back = lax.all_to_all(conv_cols, "seq", split_axis=1, concat_axis=0, tiled=True)
    long_out = conv_back + skip_gain[:, None] * product
    mixed_out = query_branch * long_out
    grad_long = out_grad * query_branch
    grad_query = out_grad * long_out
    grad_cols = lax.all_to_all(grad_long, "seq", split_axis=0, concat_axis=1, tiled=True)
    grad_re, grad_im = forward_transform(grad_cols, tables)
    prod_grad_cols = inverse_transform(
        filt_re * grad_re + filt_im * grad_im, filt_re * grad_im - filt_im * grad_re, tables
    )
    resp_grad_cols = inverse_transform(
        grad_re * prod_re + grad_im * prod_im, grad_im * prod_re - grad_re * prod_im, tables
    )
    skip_grad = jnp.sum(grad_long * product, axis=1)
    prod_grad_back, resp_grad_back = (
        lax.all_to_all(prod_grad_cols, "seq", split_axis=1, concat_axis=0, tiled=True),
        lax.all_to_all(resp_grad_cols, "seq", split_axis=1, concat_axis=0, tiled=True),
    )
    local_residue = residue_sums(resp_grad_back, decay_cos, decay_sin)
    grad_prod = prod_grad_back + skip_gain[:, None] * grad_long
    grad_branches = jnp.stack([grad_query, grad_prod * value_branch, grad_prod * key_branch])
    next_rim = from_behind(grad_branches[:, :, :2], "seq", -1)
    extended_back = jnp.concatenate([grad_branches, next_rim], axis=2)
    grad_proj = sum(
        (
            conv_taps[:, offset, :, None] * extended_back[:, :, offset : offset + tok_rows]
            for offset in range(3)
        )
    )
    local_taps = jnp.stack(
        [
            jnp.sum(grad_branches * extended[:, :, 2 - offset : 2 - offset + tok_rows], axis=2)
            for offset in range(3)
        ],
        axis=1,
    )
    residue_grad, taps_grad, skip_grad = lax.psum((local_residue, local_taps, skip_grad), "seq")
    grad_low = grad_proj.astype(jnp.bfloat16)
    input_term = jnp.einsum("kct,kdc->td", grad_low, in_weight, preferred_element_type=jnp.float32)
    input_grad = lax.psum_scatter(input_term, "chan", scatter_dimension=1, tiled=True)
    weight_term = jnp.einsum("td,kct->kdc", gathered, grad_low, preferred_element_type=jnp.float32)
    weight_grad = lax.psum_scatter(weight_term, "seq", scatter_dimension=1, tiled=True)
    return (mixed_out, input_grad, weight_grad, taps_grad, residue_grad, skip_grad)


def solution(mesh):
    in_specs = (
        P("seq", "chan"),
        P(None, None, "chan"),
        P(None, None, "chan"),
        P(None, "chan"),
        P(None, "chan"),
        P(None, None, "chan"),
        P("chan"),
        P("chan", "seq"),
    )
    out_specs = (
        P("chan", "seq"),
        P("seq", "chan"),
        P(None, "seq", "chan"),
        P(None, None, "chan"),
        P(None, None, "chan"),
        P("chan"),
    )
    return jax.shard_map(
        on_device, mesh=mesh, in_specs=in_specs, out_specs=out_specs, check_vma=False
    )
```

profile of v0, /device:TPU:1, one launch (start us, length us, event | category | flops | bytes accessed | tf_op | source)
XLA Modules:
  0.0 540.1 jit_solution(7193601367311828785)
XLA Ops:
  8.8 70.2 %all-gather.2.cloned.1.call-done = bf16[512,4096]{1,0:T(8,128)(2,1)} async-done(((bf16[512,256]{1,0:T(8,128)(2,1)}), bf16[512,4096]{1,0:T(8,128)(2,1)}) %all-gather.2.cloned.1.call-update) | async-done | bytes 4194320 | tf_op jit(solution)/shard_map/all_gather | solution.py:100
  79.0 4.0 fusion.3
  83.2 2.2 collective-permute-start
  85.4 4.0 collective-permute-done
  91.9 10.8 %all-to-all-start = ((f32[16,8,512]{2,1,0:T(8,128)}), f32[16,8,512]{2,1,0:T(8,128)S(1)}, u32[]{:S(2)}, u32[]{:S(2)}) async-start(f32[16,8,512]{2,1,0:T(8,128)} %multiply_bitcast_fusion.1), calls=%async_computation | async-start | bytes 524288 | tf_op jit(solution)/shard_map/all_to_all | solution.py:122
  102.7 2.5 multiply_reduce_fusion.5
  105.2 7.5 %all-to-all-done = f32[16,8,512]{2,1,0:T(8,128)S(1)} async-done(((f32[16,8,512]{2,1,0:T(8,128)}), f32[16,8,512]{2,1,0:T(8,128)S(1)}, u32[]{:S(2)}, u32[]{:S(2)}) %all-to-all-start) | async-done | bytes 262176 | tf_op jit(solution)/shard_map/all_to_all | solution.py:122
  112.7 4.4 all-to-all-start.3
  120.9 5.6 %all-to-all-done.3 = f32[16,8,512]{2,1,0:T(8,128)} async-done(((f32[16,8,512]{2,1,0:T(8,128)}), f32[16,8,512]{2,1,0:T(8,128)}, u32[]{:S(2)}, u32[]{:S(2)}) %all-to-all-start.3) | async-done | bytes 262176 | tf_op jit(solution)/shard_map/all_to_all | solution.py:135
  130.0 1.9 fusion.5
  131.9 1.9 convolution_bitcast_fusion.2
  146.3 2.0 multiply_add_fusion.1
  155.9 3.5 all-to-all-start.5
  162.1 7.0 %all-to-all-done.5 = f32[8,16,512]{2,0,1:T(8,128)S(1)} async-done(((f32[8,16,512]{2,0,1:T(8,128)}), f32[8,16,512]{2,0,1:T(8,128)S(1)}, u32[]{:S(2)}, u32[]{:S(2)}) %all-to-all-start.5) | async-done | bytes 262176 | tf_op jit(solution)/shard_map/all_to_all | solution.py:146
  169.1 19.1 %multiply_reduce_fusion.1 = (f32[16,128]{1,0:T(8,128)}, f32[16,128]{1,0:T(8,128)}, f32[128,512]{1,0:T(8,128)S(1)}) fusion(f32[128,512]{1,0:T(8,128)S(1)} %bitcast.224, f32[16,128]{1,0:T(8,128)} %param.12, f32[512]{0:T(512)S(1)} %add_convert_fusion, f32[16,128]{1,0:T(8,128)} %neg.37, f32[16,128]{1,0:T(8,128)} %get-tuple-element.51, ...), kind=kLoop, calls=%fused_computation.10 | loop fusion | flops 12513280 | bytes 575488 | tf_op jit(solution)/shard_map/reduce_sum | solution.py:88
  188.3 12.3 %all_to_all.90 = f32[16,8,512]{2,1,0:T(8,128)S(1)} all-to-all(f32[16,8,512]{2,1,0:T(8,128)S(1)} %bitcast.225), channel_id=1, replica_groups=mesh['seq'=16,'chan'=16] {'seq'}, dimensions={0} | all-to-all | bytes 524288 | tf_op jit(solution)/shard_map/all_to_all | solution.py:123
  209.8 2.3 multiply_add_fusion.2
  221.3 4.4 all-to-all-start.4
  225.8 1.9 fusion.87
  227.7 1.9 fusion.89
  229.6 1.9 convolution_add_fusion.3
  231.5 1.9 convolution_subtract_fusion.3
  238.5 17.0 %all_to_all.91 = f32[8,16,512]{2,0,1:T(8,128)S(1)} all-to-all(f32[8,16,512]{2,0,1:T(8,128)S(1)} %copy.182), channel_id=1, replica_groups=mesh['seq'=16,'chan'=16] {'seq'}, dimensions={1} | all-to-all | bytes 524288 | tf_op jit(solution)/shard_map/all_to_all | solution.py:130
  255.5 2.1 fusion.39
  259.3 5.3 collective-permute-done.1
  264.7 2.1 multiply_reduce_fusion.3
  266.7 4.6 convolution_bitcast_fusion.1
  271.4 5.7 %convolution_bitcast_fusion = f32[512,4096]{1,0:T(8,128)} fusion(bf16[3,128,512]{2,1,0:T(8,128)(2,1)S(1)} %get-tuple-element.49, bf16[3,4096,128]{2,1,0:T(8,128)(2,1)S(1)} %copy-done), kind=kOutput, calls=%fused_computation | convolution fusion | flops 1610612736 | bytes 11927552 | tf_op jit(solution)/shard_map/kct,kdc->td/dot_general | solution.py:168
  279.8 55.1 %all-reduce = (f32[3,3,128]{2,0,1:T(4,128)S(1)}, f32[2,16,128]{2,1,0:T(8,128)}, f32[128]{0:T(128)}) all-reduce(f32[3,3,128]{2,0,1:T(4,128)S(1)} %pad_maximum_fusion.4, f32[2,16,128]{2,1,0:T(8,128)S(1)} %pad_maximum_fusion.3, f32[128]{0:T(128)S(1)} %copy-done.23), channel_id=1, replica_groups=mesh['seq'=16,'chan'=16] {'seq'}, use_global_device_ids=true, to_apply=%region_6.7 | all-reduce | flops 5376 | bytes 43008 | tf_op jit(solution)/shard_map/psum | solution.py:166
  335.4 82.5 %reduce-scatter.5.cloned.1.call-done = f32[3,256,128]{1,2,0:T(8,128)} async-done(((f32[3,4096,128]{1,2,0:T(8,128)}), f32[3,256,128]{1,2,0:T(8,128)}) %reduce-scatter.5.cloned.1.call-update) | async-done | bytes 393232 | tf_op jit(solution)/shard_map/reduce_scatter | solution.py:171
  417.9 1.9 copy.219
  419.8 113.5 %reduce-scatter.3.cloned.1.call-done = f32[512,256]{1,0:T(8,128)} async-done(((f32[512,4096]{1,0:T(8,128)}), f32[512,256]{1,0:T(8,128)}) %reduce-scatter.3.cloned.1.call-update) | async-done | bytes 524304 | tf_op jit(solution)/shard_map/reduce_scatter | solution.py:169
  (118 shorter events, 62.5 us)
Async XLA Ops:
  7.2 71.8 %copy-start = (bf16[3,4096,128]{2,1,0:T(8,128)(2,1)S(1)}, bf16[3,4096,128]{2,1,0:T(8,128)(2,1)}, u32[]{:S(2)}) copy-start(bf16[3,4096,128]{2,1,0:T(8,128)(2,1)} %param.9) | copy-start | bytes 9437188
  7.2 71.8 %all-gather.2.cloned.1.call-start = ((), (), s32[]{:S(2)}) async-start(), calls=%async_computation.8 | async-start | bytes 4456448 | tf_op jit(solution)/shard_map/all_gather | solution.py:100
  83.0 6.4 %copy-start.9 = (f32[3,128,512]{2,1,0:T(8,128)}, f32[3,128,512]{2,1,0:T(8,128)S(1)}, u32[]{:S(2)}) copy-start(f32[3,128,512]{2,1,0:T(8,128)S(1)} %fusion.3) | copy-start | bytes 2359300
  83.2 6.3 %collective-permute-start = (f32[3,128,2]{2,1,0:T(8,128)S(1)}, f32[3,128,2]{2,1,0:T(8,128)S(1)}, u32[]{:S(2)}, u32[]{:S(2)}) collective-permute-start(f32[3,128,2]{2,1,0:T(8,128)S(1)} %slice.101), channel_id=1, source_target_pairs={{0,16},{16,32},{32,48},{48,64},{64,80},{80,96},{96,112},{112,128},... | collective-permute-start | bytes 9224 | tf_op jit(solution)/shard_map/ppermute | solution.py:14
  89.4 0.8 copy-start.17
  90.2 0.9 copy-start.1
  91.9 20.8 %all-to-all-start = ((f32[16,8,512]{2,1,0:T(8,128)}), f32[16,8,512]{2,1,0:T(8,128)S(1)}, u32[]{:S(2)}, u32[]{:S(2)}) async-start(f32[16,8,512]{2,1,0:T(8,128)} %multiply_bitcast_fusion.1), calls=%async_computation | async-start | bytes 524288 | tf_op jit(solution)/shard_map/all_to_all | solution.py:122
  112.7 13.8 %all-to-all-start.3 = ((f32[16,8,512]{2,1,0:T(8,128)}), f32[16,8,512]{2,1,0:T(8,128)}, u32[]{:S(2)}, u32[]{:S(2)}) async-start(f32[16,8,512]{2,1,0:T(8,128)} %bitcast.34), calls=%async_computation.3 | async-start | bytes 524288 | tf_op jit(solution)/shard_map/all_to_all | solution.py:135
  143.4 4.8 copy-start.2
  145.1 5.0 copy-start.4
  146.3 4.7 copy-start.6
  146.3 5.5 %copy-start.14 = (f32[128,128]{0,1:T(8,128)S(1)}, f32[128,128]{0,1:T(8,128)}, u32[]{:S(2)}) copy-start(f32[128,128]{0,1:T(8,128)} %fusion.105) | copy-start | bytes 196612
  148.3 4.3 copy-start.12
  155.9 13.2 %all-to-all-start.5 = ((f32[8,16,512]{2,0,1:T(8,128)}), f32[8,16,512]{2,0,1:T(8,128)S(1)}, u32[]{:S(2)}, u32[]{:S(2)}) async-start(f32[8,16,512]{2,0,1:T(8,128)} %copy.218), calls=%async_computation.7 | async-start | bytes 524288 | tf_op jit(solution)/shard_map/all_to_all | solution.py:146
  202.4 7.3 %copy-start.3 = (f32[8,128,128]{2,1,0:T(8,128)S(1)}, f32[8,128,128]{2,1,0:T(8,128)}, u32[]{:S(2)}) copy-start(f32[8,128,128]{2,1,0:T(8,128)} %copy-done.2) | copy-start | bytes 1572868
  202.4 7.3 %copy-start.5 = (f32[8,128,128]{2,1,0:T(8,128)S(1)}, f32[8,128,128]{2,1,0:T(8,128)}, u32[]{:S(2)}) copy-start(f32[8,128,128]{2,1,0:T(8,128)} %copy-done.4) | copy-start | bytes 1572868
  202.4 7.3 %copy-start.7 = (f32[8,128,128]{2,1,0:T(8,128)S(1)}, f32[8,128,128]{2,1,0:T(8,128)}, u32[]{:S(2)}) copy-start(f32[8,128,128]{2,1,0:T(8,128)} %copy-done.6) | copy-start | bytes 1572868
  202.5 7.3 %copy-start.11 = (f32[8,128,128]{2,1,0:T(8,128)S(1)}, f32[8,128,128]{2,1,0:T(8,128)}, u32[]{:S(2)}) copy-start(f32[8,128,128]{2,1,0:T(8,128)} %get-tuple-element.55) | copy-start | bytes 1572868
  212.1 3.5 copy-start.15
  212.1 4.3 copy-start.13
  221.3 17.2 %all-to-all-start.4 = ((f32[8,16,512]{2,0,1:T(8,128)}), f32[8,16,512]{2,0,1:T(8,128)}, u32[]{:S(2)}, u32[]{:S(2)}) async-start(f32[8,16,512]{2,0,1:T(8,128)} %copy.204), calls=%async_computation.4 | async-start | bytes 524288 | tf_op jit(solution)/shard_map/all_to_all | solution.py:145
  225.7 192.2 %reduce-scatter.5.cloned.1.call-start = ((), (), s32[]{:S(2)}) async-start(), calls=%async_computation.10 | async-start | bytes 6684672 | tf_op jit(solution)/shard_map/reduce_scatter | solution.py:171
  229.6 25.9 %copy-start.24 = (f32[128]{0:T(128)S(1)}, f32[128]{0:T(128)}, u32[]{:S(2)}) copy-start(f32[128]{0:T(128)} %param.14) | copy-start | bytes 1540
  238.5 26.1 %copy-start.10 = (f32[3,128,512]{2,1,0:T(8,128)S(1)}, f32[3,128,512]{2,1,0:T(8,128)}, u32[]{:S(2)}) copy-start(f32[3,128,512]{2,1,0:T(8,128)} %copy-done.9) | copy-start | bytes 2359300
  238.5 26.1 %copy-start.18 = (f32[3,128,2]{2,1,0:T(8,128)S(1)}, f32[3,128,2]{2,1,0:T(8,128)}, u32[]{:S(2)}) copy-start(f32[3,128,2]{2,1,0:T(8,128)} %copy-done.17) | copy-start | bytes 9220
  257.6 9.1 %copy-start.8 = (bf16[512,4096]{1,0:T(8,128)(2,1)S(1)}, bf16[512,4096]{1,0:T(8,128)(2,1)}, u32[]{:S(2)}) copy-start(bf16[512,4096]{1,0:T(8,128)(2,1)} %all-gather.2.cloned.1.call-done) | copy-start | bytes 12582916
  257.7 6.9 %collective-permute-start.1 = (f32[3,128,2]{2,1,0:T(8,128)S(1)}, f32[3,128,2]{2,1,0:T(8,128)S(1)}, u32[]{:S(2)}, u32[]{:S(2)}) collective-permute-start(f32[3,128,2]{2,1,0:T(8,128)S(1)} %slice.111), channel_id=1, source_target_pairs={{16,0},{32,16},{48,32},{64,48},{80,64},{96,80},{112,96},{128,112},... | collective-permute-start | bytes 9224 | tf_op jit(solution)/shard_map/ppermute | solution.py:14
  271.4 262.0 %reduce-scatter.3.cloned.1.call-start = ((), (), s32[]{:S(2)}) async-start(), calls=%async_computation.9 | async-start | bytes 8912896 | tf_op jit(solution)/shard_map/reduce_scatter | solution.py:169
  277.1 1.0 copy-start.16
  277.1 2.7 copy-start.19
  277.1 2.7 copy-start.20
  277.1 2.7 copy-start.23
  (2 other events, 1.4 us)
Sparse Core Ops, SparseCore 0:
  10.6 68.3 all-gather.1
  271.5 146.3 reduce-scatter.4
  423.1 110.2 reduce-scatter.2
where the time goes:
time: 545 us; the launch traced here: 540 us
  waiting for transfers between devices  296 us (54%)
  blocking collectives  84.4 us (15%)
  matrix products  62.6 us (11%)
  other arithmetic  32.5 us (6%)
  starting transfers between devices  27 us (5%)
  local copies, waits for them, and re-layouts  22.8 us (4%)
  between operations  14.6 us (3%)
    reduce_scatter x1, waiting for transfers between devices, on_device(): lax.psum_scatter(input_term, 'chan', scatter_dimension=1, tiled=True)  114 us
    reduce_scatter x1, waiting for transfers between devices, on_device(): lax.psum_scatter(weight_term, 'seq', scatter_dimension=1, tiled=True)  82.5 us
    all_gather x1, waiting for transfers between devices, on_device(): gathered = lax.all_gather(hidden_in, 'chan', axis=1, tiled=True)  70.2 us
    psum x1, blocking collectives, on_device(): lax.psum((local_residue, local_taps, skip_grad), 'seq')  55.1 us
    reduce_sum x1, other arithmetic, residue_sums(): jnp.sum(grad_resp[None] * decay_cos, axis=2)  19.1 us
    all_to_all x1, blocking collectives, on_device(): lax.all_to_all(conv_cols, 'seq', split_axis=1, concat_axis=0, tiled=True)  17 us
    all_to_all x1, blocking collectives, on_device(): lax.all_to_all(filter_seq, 'seq', split_axis=0, concat_axis=1, tiled=True)  12.3 us
  transfers between devices with their start and end apart: 9, of which 8 were waited for; matrix products, arithmetic and copies ran while one was open for 6% of the time, Pallas kernels for 0%

commit v1 on v0

v1 whole, which is shorter than its diff:
```python
import jax
import jax.numpy as jnp
from jax import lax
from jax.experimental import pallas as pl
from jax.experimental.pallas import tpu as pltpu
from jax.sharding import PartitionSpec as P

F32 = jnp.float32
BF16 = jnp.bfloat16
MODES = 16
SUB = 64
ROWS = 8 * SUB
EXT = ROWS + 8


def chan_pairs(dx, dy, dc):
    pairs = []
    for c in range(16):
        x, y, core = c // 4, c // 2 % 2, c % 2
        pairs.append((c, (x + dx) % 4 * 4 + (y + dy) % 2 * 2 + (core + dc) % 2))
    return pairs


def seq_pairs(dz, dy):
    return [(s, (s // 2 + dz) % 8 * 2 + (s % 2 + dy) % 2) for s in range(16)]


def to_chan(x, dx, dy, dc=0):
    return lax.ppermute(x, "chan", chan_pairs(dx, dy, dc))


def to_seq(x, dz, dy=0):
    return lax.ppermute(x, "seq", seq_pairs(dz, dy))


def pole_power(rate, angle, count):
    high = jnp.round(angle * 1024.0) * (1.0 / 1024.0)
    low = angle - high
    one, two = high * count, low * count
    mag = jnp.exp(-rate * count)
    cos1, sin1, cos2, sin2 = jnp.cos(one), jnp.sin(one), jnp.cos(two), jnp.sin(two)
    return mag * (cos1 * cos2 - sin1 * sin2), mag * (sin1 * cos2 + cos1 * sin2)


def spread(pair):
    both = jnp.concatenate(pair, axis=0)
    return jnp.broadcast_to(both[:, None, :], (2 * MODES, 8, both.shape[1]))


def times(a, b):
    return a[0] * b[0] - a[1] * b[1], a[0] * b[1] + a[1] * b[0]


def copy_all(pairs, sems):
    copies = [pltpu.make_async_copy(a, b, sems.at[i]) for i, (a, b) in enumerate(pairs)]
    for c in copies:
        c.start()
    return copies


def wait_all(copies, start=False):
    for c in copies:
        if start:
            c.start()
        c.wait()


def stream(sources, weight_far, par, held, weight, sems):
    copies = []
    for b in range(8):
        pairs = [(weight_far.at[:, b, par], weight.at[:, b])]
        pairs += [(src.at[b], dst.at[b]) for src, dst in zip(sources, held)]
        group = [pltpu.make_async_copy(f, t, sems.at[6 * b + i]) for i, (f, t) in enumerate(pairs)]
        for c in group:
            c.start()
        copies.append(group)
    return copies


def columns(weight, b):
    return jnp.concatenate([weight[k, b] for k in range(3)], axis=1)


def convolve(taps, ext, k):
    lanes = slice(128 * k, 128 * k + 128)
    total = taps[3 * k : 3 * k + 1, :] * ext[8 : 8 + ROWS, lanes]
    total = total + taps[3 * k + 1 : 3 * k + 2, :] * ext[7 : 7 + ROWS, lanes]
    return total + taps[3 * k + 2 : 3 * k + 3, :] * ext[6 : 6 + ROWS, lanes]


def half_kernel(at, mine_far, weight_far, out, mine, weight, made, sems):
    copies = stream([mine_far], weight_far, at[0], [mine], weight, sems)
    for b in range(0, 8, 4):
        for i in range(b, b + 4):
            wait_all(copies[i])
        left = jnp.concatenate([mine[i] for i in range(b, b + 4)], axis=1)
        right = jnp.concatenate([columns(weight, i) for i in range(b, b + 4)], axis=0)
        total = jnp.dot(left, right, preferred_element_type=F32)
        made[...] = total if b == 0 else made[...] + total
    wait_all([pltpu.make_async_copy(made, out, sems.at[0])], start=True)


def states_kernel(
    at, other_far, weight_far, half, taps, og, lam, pwf, pwb,
    ext, prod, gl, st, send, other, weight, ends, sems, io,
):
    seq = at[2]
    copies = stream([other_far], weight_far, 1 - at[0], [other], weight, sems)
    for b in range(0, 8, 4):
        for i in range(b, b + 4):
            wait_all(copies[i])
        left = jnp.concatenate([other[i] for i in range(b, b + 4)], axis=1)
        right = jnp.concatenate([columns(weight, i) for i in range(b, b + 4)], axis=0)
        total = jnp.dot(left, right, preferred_element_type=F32)
        if b == 0:
            io.need(0)
        ext[8:520, :] = (half[...] if b == 0 else ext[8:520, :]) + total
    ext[0:8, :] = jnp.zeros((8, 384), F32)
    ext[520:528, :] = jnp.zeros((8, 384), F32)
    io.done(0)
    io.need(1, 2)
    q, k, v = (convolve(taps, ext, i) for i in range(3))
    fresh = lax.broadcasted_iota(jnp.int32, (ROWS, 128), 0) >= 2
    prod[...] = jnp.where(fresh, k * v, 0.0)
    gl[...] = jnp.where(fresh, og[0:ROWS, :] * q, 0.0)
    io.done(1, 2)
    edge = [k[0:2], v[0:2], q[0:2], og[0:2, :]]
    edge += [ext[518:520, 128 * i : 128 * i + 128] for i in range(3)]
    edge = jnp.concatenate(edge + [jnp.zeros((2, 128), F32)], axis=0)
    io.need(3, 4, 5)
    half = MODES // 2
    for src, powers, back, base in ((prod, pwf, False, 0), (gl, pwb, True, 32)):
        for n0 in range(0, MODES, half):

            def body(step, carry, n0=n0, back=back, src=src):
                i = SUB - 1 - step if back else step
                v = src[pl.ds(i, 8, stride=SUB), :]
                out = []
                for k in range(half):
                    re, im = carry[2 * k], carry[2 * k + 1]
                    lr, li = lam[n0 + k], lam[MODES + n0 + k]
                    out += [re * lr - im * li + v, re * li + im * lr]
                return tuple(out)

            zero = tuple(jnp.zeros((8, 128), F32) for _ in range(2 * half))
            carry = lax.fori_loop(0, SUB, body, zero, unroll=4)
            for k in range(half):
                n = n0 + k
                re, im = carry[2 * k], carry[2 * k + 1]
                st[base + n] = re
                st[base + MODES + n] = im
                er, ei = times((re, im), (powers[n], powers[MODES + n]))
                ends[base + n : base + n + 1, :] = jnp.sum(er, axis=0, keepdims=True)
                ends[base + MODES + n : base + MODES + n + 1, :] = jnp.sum(ei, axis=0, keepdims=True)
    io.done(3)
    for j in range(16):
        send[j, 0:32, :] = jnp.where(j >= seq, ends[0:32, :], ends[32:64, :])
        send[j, 32:48, :] = edge


def scan_kernel(prod, gl, st, lam, rho, lam64, y, gp, sums):
    half = MODES // 2
    place = lax.broadcasted_iota(jnp.int32, (8, 128), 0)
    for base, back in ((0, False), (32, True)):
        for n in range(MODES):

            def shift(v, by, back=back):
                moved = pltpu.roll(v, 8 - by if back else by, 0)
                return jnp.where(place < 8 - by if back else place >= by, moved, 0.0)

            re, im = shift(st[base + n], 1), shift(st[base + MODES + n], 1)
            for level, by in enumerate((1, 2, 4)):
                ar, ai = times(
                    (shift(re, by), shift(im, by)), (lam64[32 * level + n], lam64[32 * level + MODES + n])
                )
                re, im = re + ar, im + ai
            sums[32 + base + n] = re
            sums[32 + base + MODES + n] = im
    for n0 in range(0, MODES, half):

        def forward(step, carry, n0=n0):
            p = prod[pl.ds(step, 8, stride=SUB), :]
            g = gl[pl.ds(step, 8, stride=SUB), :]
            out = []
            total = None
            for k in range(half):
                re, im, sr, si = carry[4 * k : 4 * k + 4]
                lr, li = lam[n0 + k], lam[MODES + n0 + k]
                re, im = re * lr - im * li + p, re * li + im * lr
                term = re * rho[n0 + k] - im * rho[MODES + n0 + k]
                total = term if total is None else total + term
                out += [re, im, sr + g * re, si + g * im]
            y[step] = total if n0 == 0 else y[step] + total
            return tuple(out)

        zero = tuple(jnp.zeros((8, 128), F32) for _ in range(4 * half))
        carry = lax.fori_loop(0, SUB, forward, zero, unroll=4)
        for k in range(half):
            sums[n0 + k] = carry[4 * k + 2]
            sums[MODES + n0 + k] = carry[4 * k + 3]

        def backward(step, carry, n0=n0):
            i = SUB - 1 - step
            g = gl[pl.ds(i, 8, stride=SUB), :]
            out = []
            total = None
            for k in range(half):
                re, im = carry[2 * k : 2 * k + 2]
                lr, li = lam[n0 + k], lam[MODES + n0 + k]
                re, im = re * lr - im * li + g, re * li + im * lr
                term = re * rho[n0 + k] - im * rho[MODES + n0 + k]
                total = term if total is None else total + term
                out += [re, im]
            gp[i] = total if n0 == 0 else gp[i] + total
            return tuple(out)

        zero = tuple(jnp.zeros((8, 128), F32) for _ in range(2 * half))
        lax.fori_loop(0, SUB, backward, zero, unroll=4)


def grads_kernel(
    at, arrived, wt, consts, lam, rho, pwf, pwb, y, gp, sums, st, ext, taps, og,
    mixed, low, yt, gt, gb, br, prod, gl, small, io,
):
    seq = at[2]

    def pair(ref, start):
        return ref[start : start + MODES, :], ref[start + MODES : start + 2 * MODES, :]

    io.need(0, 1, 2, 12)
    lam16, inv16, rho16, lam512 = pair(consts, 0), pair(consts, 32), pair(consts, 64), pair(consts, 96)
    lam511, lam510 = pair(consts, 128), pair(consts, 160)
    zero16 = jnp.zeros((MODES, 128), F32)
    s_in, u_in = (zero16, zero16), (zero16, zero16)
    zero2 = jnp.zeros((2, 128), F32)
    own = nxt = [zero2] * 6
    rim = [zero2] * 3
    first = lax.broadcasted_iota(jnp.int32, (2, 128), 0) == 0

    def choose(flag, new, old):
        return [jnp.where(flag, a, b) for a, b in zip(new, old)]

    before = [zero2] * 3
    for j in range(16):
        tilde = arrived[j, 32:40, :]
        kvq = []
        for k, rows in ((1, tilde[0:2]), (2, tilde[2:4]), (0, tilde[4:6])):
            t1, t2 = taps[3 * k + 1 : 3 * k + 2, :], taps[3 * k + 2 : 3 * k + 3, :]
            p2, p1 = before[k][0:1], before[k][1:2]
            kvq.append(rows + jnp.where(first, t1 * p1 + t2 * p2, t2 * p1))
        out_grad = tilde[6:8]
        product = kvq[0] * kvq[1]
        cotangent = out_grad * kvq[2]
        mine = kvq + [out_grad, product, cotangent]
        tail = arrived[j, 40:48, :]
        before = [tail[0:2], tail[2:4], tail[4:6]]
        own = choose(j == seq, mine, own)
        nxt = choose(j == seq + 1, mine, nxt)
        rim = choose(j == seq - 1, before, rim)
        got = pair(arrived.at[j], 0)
        p0, p1 = product[0:1], product[1:2]
        g0, g1 = cotangent[0:1], cotangent[1:2]
        ahead = j < seq
        fixed = [
            got[i] + jnp.where(ahead, lam511[i] * p0 + lam510[i] * p1, lam16[i] * g1 + (g0 if i == 0 else 0.0))
            for i in range(2)
        ]
        re, im = times(fixed, (wt[j, 0:MODES, :], wt[j, MODES : 2 * MODES, :]))
        behind = j > seq
        s_in = (s_in[0] + jnp.where(ahead, re, 0.0), s_in[1] + jnp.where(ahead, im, 0.0))
        u_in = (u_in[0] + jnp.where(behind, re, 0.0), u_in[1] + jnp.where(behind, im, 0.0))

    def read_out(state):
        return jnp.sum(rho16[0] * state[0] - rho16[1] * state[1], axis=0, keepdims=True)

    p0, p1, g0, g1 = own[4][0:1], own[4][1:2], own[5][0:1], own[5][1:2]
    x0 = times(lam16, s_in)
    x0 = (x0[0] + p0, x0[1])
    x1 = times(lam16, x0)
    x1 = (x1[0] + p1, x1[1])
    small[0:16, :] = g0 * x0[0] + g1 * x1[0]
    small[16:32, :] = -(g0 * x0[1] + g1 * x1[1])
    inv2 = times(inv16, inv16)
    s_in = tuple(s_in[i] + inv16[i] * p0 + inv2[i] * p1 for i in range(2))
    carried = times(lam512, s_in)
    last = pair(arrived.at[seq], 0)
    last = (last[0] + carried[0], last[1] + carried[1])
    for extra in range(2):
        moved = times(lam16, last)
        last = (moved[0] + nxt[4][extra : extra + 1], moved[1])
        yt[ROWS + extra : ROWS + extra + 1, :] = read_out(last)
    gt[ROWS : ROWS + 1, :] = read_out(u_in)
    later = times(inv16, (u_in[0] - nxt[5][0:1], u_in[1]))
    gt[ROWS + 1 : ROWS + 2, :] = read_out(later)
    yt[ROWS + 2 : EXT, :] = jnp.zeros((EXT - ROWS - 2, 128), F32)
    gt[ROWS + 2 : EXT, :] = jnp.zeros((EXT - ROWS - 2, 128), F32)
    io.need(3, 4, 5, 6, 7, 8, 9, 10)

    half = MODES // 2
    for n0 in range(0, MODES, half):
        start_f, start_b = [], []
        for k in range(half):
            n = n0 + k
            l8 = (lam[n], lam[MODES + n])
            r8 = (rho[n], rho[MODES + n])

            def full(state, powers, base, n=n):
                wide = tuple(jnp.broadcast_to(s[n : n + 1, :], (8, 128)) for s in state)
                add = times(wide, (powers[n], powers[MODES + n]))
                return times((sums[base + n] + add[0], sums[base + MODES + n] + add[1]), l8)

            q = full(s_in, pwb, 32)
            rr, ri = times(q, (st[32 + n], st[48 + n]))
            small[n : n + 1, :] += jnp.sum(sums[n] + rr, axis=0, keepdims=True)
            small[MODES + n : MODES + n + 1, :] -= jnp.sum(sums[MODES + n] + ri, axis=0, keepdims=True)
            start_f += list(times(q, r8))
            start_b += list(times(full(u_in, pwf, 64), r8))

        def follow(src, dst, back, start, n0=n0):
            def body(step, carry):
                i = SUB - 1 - step if back else step
                at = pl.ds(i, 8, stride=SUB)
                total = src[i] if n0 == 0 else dst[at, :]
                out = []
                for k in range(half):
                    re, im = carry[2 * k], carry[2 * k + 1]
                    total = total + re
                    lr, li = lam[n0 + k], lam[MODES + n0 + k]
                    out += [re * lr - im * li, re * li + im * lr]
                dst[at, :] = total
                return tuple(out)

            lax.fori_loop(0, SUB, body, tuple(start), unroll=4)

        follow(y, yt, False, start_f)
        follow(gp, gt, True, start_b)

    none, one = (jnp.ones_like(zero16), zero16), lam16
    yt[0:1, :] -= read_out(inv16) * p1
    gt[0:1, :] += read_out(none) * g0 + read_out(one) * g1
    gt[1:2, :] += read_out(none) * g1

    io.need(11, 13)
    for k in range(3):
        ext[6:8, 128 * k : 128 * k + 128] = rim[k]
    og[ROWS : ROWS + 2, :] = nxt[3]
    for k, at_k in ((0, 2), (1, 0), (2, 1)):
        lanes = slice(128 * k, 128 * k + 128)
        br[0:ROWS, lanes] = convolve(taps, ext, k)
        br[ROWS : ROWS + 2, lanes] = nxt[at_k]
    br[ROWS + 2 : EXT, :] = jnp.zeros((EXT - ROWS - 2, 384), F32)
    prod[...] = br[:, 128:256] * br[:, 256:384]
    gl[...] = og[...] * br[:, 0:128]
    gain = consts[192:193, :]
    long_out = yt[...] + gain * prod[...]
    gb[:, 0:128] = og[...] * long_out
    grad_prod = gt[...] + gain * gl[...]
    gb[:, 128:256] = grad_prod * br[:, 256:384]
    gb[:, 256:384] = grad_prod * br[:, 128:256]
    for k in range(3):
        lanes = slice(128 * k, 128 * k + 128)
        total = None
        for j in range(3):
            term = taps[3 * k + j : 3 * k + j + 1, :] * gb[j : j + ROWS, lanes]
            total = term if total is None else total + term
            row = 32 + 3 * k + j
            small[row : row + 1, :] = jnp.sum(
                gb[0:ROWS, lanes] * ext[8 - j : 8 - j + ROWS, lanes], axis=0, keepdims=True
            )
        low[0:ROWS, lanes] = total.astype(BF16)
    small[41:42, :] = jnp.sum(gl[0:ROWS, :] * prod[0:ROWS, :], axis=0, keepdims=True)
    small[42:48, :] = jnp.zeros((6, 128), F32)
    wide = jnp.concatenate([small[16 * i : 16 * i + 16, :] for i in range(3)], axis=1)
    high = wide.astype(BF16)
    low[ROWS : ROWS + 16, :] = high
    low[ROWS + 16 :, :] = (wide - high.astype(F32)).astype(BF16)
    io.done(1)
    mixed[...] = (br[0:ROWS, 0:128] * long_out[0:ROWS, :]).T


def turn_kernel(at, a, b, *rest):
    out, held, turned, sems = rest[-4:]

    def run(src):
        copies = copy_all([(src.at[i], held.at[i]) for i in range(8)], sems)
        sent = []
        for i in range(8):
            copies[i].wait()
            turned[i] = held[i].T
            sent += [pltpu.make_async_copy(turned.at[i], out.at[i], sems.at[8 + i])]
            sent[i].start()
        wait_all(sent)

    @pl.when(at[3] == 1)
    def _():
        run(a)

    @pl.when(at[3] == 0)
    def _():
        run(b)


def input_kernel(at, low, low_core, weight, partner, *rest):
    outs, (left, lturn, right, parts, sems) = rest[:8], rest[8:]
    core, x, y = at[0], at[4], at[5]
    copies = copy_all([(low.at[0:ROWS], left.at[0]), (low_core.at[0:ROWS], left.at[1])], sems)
    places = []
    for r in range(8):
        dx, dy = r // 2, r % 2
        places.append((x + dx) % 4 * 2 + (y + dy) % 2)
    order = [1, 2, 3, 4, 5, 6, 7, 0]
    far = []
    for n, r in enumerate(order):
        for s, src in enumerate((weight, partner)):
            c = pltpu.make_async_copy(
                src.at[:, places[r], core], right.at[r, s], sems.at[2 + 2 * n + s]
            )
            c.start()
            far.append(c)
    wait_all(copies)
    lturn[...] = jnp.concatenate([left[0].T, left[1].T], axis=0)
    sent = []
    for n, r in enumerate(order):
        wait_all(far[2 * n : 2 * n + 2])
        cols = jnp.concatenate([right[r, s, k] for s in range(2) for k in range(3)], axis=1)
        parts[r] = jnp.dot(cols, lturn[...], preferred_element_type=F32).astype(BF16)
        c = pltpu.make_async_copy(parts.at[r], outs[r], sems.at[18 + r])
        c.start()
        sent.append(c)
    wait_all(sent)


def weight_kernel(at, kept, given, passed, low, low_y, *rest):
    out, kv, pv, cols, parts, sems = rest[-6:]
    copies = copy_all([(low, cols.at[0]), (low_y, cols.at[1])], sems)
    far = []
    for i in range(8):
        c = pltpu.make_async_copy(kept.at[i], kv.at[i], sems.at[2 + 2 * i])
        c.start()
        far.append(c)
        for flag, src in ((1, given), (0, passed)):
            c = pltpu.make_async_copy(src.at[i], pv.at[i], sems.at[3 + 2 * i])

            @pl.when(at[3] == flag)
            def _(c=c):
                c.start()

        far.append(c)
    wait_all(copies)
    total = jnp.zeros((16, 384), F32)
    for i in range(2):
        for r in (ROWS, ROWS + 16):
            total = total + cols[i, r : r + 16, :].astype(F32)
    high = total.astype(BF16)
    rest_low = (total - high.astype(F32)).astype(BF16)
    sent = []
    for i in range(8):
        wait_all(far[2 * i : 2 * i + 2])
        total = jnp.dot(kv[i], cols[0, 0:ROWS, :], preferred_element_type=F32)
        total = total + lax.dot_general(
            pv[i], cols[1, 0:ROWS, :], (((0,), (0,)), ((), ())), preferred_element_type=F32
        )
        parts[i, 0:256, :] = total.astype(BF16)
        parts[i, 256:272, :] = high
        parts[i, 272:288, :] = rest_low
        c = pltpu.make_async_copy(parts.at[i], out.at[i], sems.at[18 + i])
        c.start()
        sent.append(c)
    wait_all(sent)


def fold_input_kernel(own, *rest):
    parts, out = rest[:-1], rest[-1]
    total = own[...].astype(F32)
    for p in parts:
        total = total + p[...].astype(F32)
    out[...] = total.T


def fold_kernel(parts, out, small):
    for k in range(3):
        lanes = slice(128 * k, 128 * k + 128)
        total = parts[0, :, lanes].astype(F32)
        for j in range(1, 8):
            total = total + parts[j, :, lanes].astype(F32)
        out[k] = total[0:256]
        small[16 * k : 16 * k + 16, :] = total[256:272] + total[272:288]


FAR = pl.BlockSpec(memory_space=pltpu.HBM)
SCALARS = pl.BlockSpec(memory_space=pltpu.SMEM)


def raw_call(kernel, us, outs, scratch, sems, args, in_specs, out_specs):
    return pl.pallas_call(
        kernel,
        in_specs=in_specs,
        out_specs=out_specs,
        out_shape=[jax.ShapeDtypeStruct(s, t) for s, t in outs],
        scratch_shapes=[pltpu.VMEM(s, t) for s, t in scratch] + [pltpu.SemaphoreType.DMA((sems,))],
        compiler_params=pltpu.CompilerParams(vmem_limit_bytes=62 * 1024 * 1024),
        cost_estimate=pl.CostEstimate(flops=int(us * 1.1e9), bytes_accessed=0, transcendentals=0),
    )(*args)


def far_call(kernel, us, at, outs, scratch, sems, *args):
    scalars = () if at is None else (at,)
    specs = [SCALARS] * len(scalars) + [FAR] * len(args)
    return raw_call(kernel, us, outs, scratch, sems, scalars + args, specs, [FAR] * len(outs))


class Staged:
    def __init__(self, ins, outs):
        self.ins, self.outs, self.here, self.gone = ins, outs, set(), set()

    def need(self, *which):
        for i in which:
            if i not in self.here:
                self.here.add(i)
                self.ins[i].wait()

    def done(self, *which):
        for i in which:
            if i not in self.gone:
                self.gone.add(i)
                self.outs[i].start()


def call(kernel, us, at, outs, scratch, *args, far=(), sems=0, late=(), staged=False):
    scalars = () if at is None else (at,)
    n_s, n_f, n_i, n_l, n_o = len(scalars), len(far), len(args), len(late), len(outs)

    def body(*refs):
        refs = list(refs)

        def take(count):
            head = refs[:count]
            del refs[:count]
            return head

        top, far_refs, ins, _, results = take(n_s), take(n_f), take(n_i), take(n_l), take(n_o)
        held, made, own, sem = take(n_i), take(n_o), refs[:-1], refs[-1]

        def copies(pairs, base):
            return [pltpu.make_async_copy(a, b, sem.at[base + i]) for i, (a, b) in enumerate(pairs)]

        coming = copies(zip(ins, held), sems)
        for c in coming:
            c.start()
        io = Staged(coming, copies(zip(made, results), sems + n_i))
        if not staged:
            io.need(*range(n_i))
        extra = ((sem,) if far else ()) + ((io,) if staged else ())
        kernel(*top, *far_refs, *held, *made, *own, *extra)
        io.need(*range(n_i))
        io.done(*range(n_o))
        wait_all(io.outs)

    buffers = [(a.shape, a.dtype) for a in args] + list(outs) + list(scratch)
    specs = [SCALARS] * n_s + [FAR] * (n_f + n_i + n_l)
    total = sems + n_i + n_o
    return raw_call(
        body, us, outs, buffers, total, scalars + tuple(far) + args + tuple(late), specs, [FAR] * n_o
    )


def after(x, *deps):
    return pl.pallas_call(
        lambda *_: None,
        in_specs=[FAR] * (1 + len(deps)),
        out_specs=FAR,
        out_shape=jax.ShapeDtypeStruct(x.shape, x.dtype),
        input_output_aliases={0: 0},
    )(x, *deps)


CHIPS = [[x * 4 + y * 2 + c for x in range(4) for y in range(2)] for c in range(2)]
COLUMNS = [[z * 2 + y for z in range(8)] for y in range(2)]


def exchange(x, axis, groups=None):
    return lax.all_to_all(
        x, axis, split_axis=0, concat_axis=0, tiled=True, axis_index_groups=groups
    )


def joint_pairs(kind):
    pairs = []
    for s in range(16):
        for c in range(16):
            wanted = s % 2 == c % 2
            if kind == "give" and not wanted:
                pairs.append((s * 16 + c, (s ^ 1) * 16 + c))
            if kind == "pass" and wanted:
                pairs.append((s * 16 + c, s * 16 + (c ^ 1)))
    return pairs


def on_device(
    hidden_in, in_weight, conv_taps, decay_rate, mode_angle, residue, skip_gain, out_grad
):
    chan, seq = lax.axis_index("chan"), lax.axis_index("seq")
    core, yl = chan % 2, seq % 2
    same = (yl == core).astype(jnp.int32)
    at = jnp.stack([core, chan, seq, same, chan // 4, chan // 2 % 2]).astype(jnp.int32)

    mine = exchange(jnp.broadcast_to(hidden_in[None], (8, ROWS, 256)), "chan", CHIPS)
    partner = to_chan(in_weight, 0, 0, 1)

    def power(count):
        return pole_power(decay_rate, mode_angle, count)

    lam = power(1.0)
    lam8 = spread(lam)
    rho8 = spread((residue[0], residue[1]))
    eighth = jnp.arange(8, dtype=F32)[None, :, None] * float(SUB)
    sub_rate, sub_angle = decay_rate[:, None, :], mode_angle[:, None, :]
    pwb = jnp.concatenate(pole_power(sub_rate, sub_angle, eighth), axis=0)
    pwf = jnp.concatenate(pole_power(sub_rate, sub_angle, float(7 * SUB) - eighth), axis=0)
    lam64 = jnp.concatenate([spread(power(float(SUB * d))) for d in (1, 2, 4)], axis=0)
    source = jnp.arange(16, dtype=jnp.int32)
    away = jnp.abs(source - seq).astype(F32)[:, None, None] - 1.0
    away = jnp.maximum(away, 0.0) * float(ROWS)
    wt = jnp.concatenate(pole_power(decay_rate[None], mode_angle[None], away), axis=1)
    consts = jnp.concatenate(
        lam + power(-1.0) + (residue[0], residue[1]) + power(float(ROWS))
        + power(float(ROWS - 1)) + power(float(ROWS - 2))
        + (jnp.broadcast_to(skip_gain[None, :], (8, 128)),),
        axis=0,
    )
    taps = jnp.concatenate([conv_taps.reshape(9, 128), jnp.zeros((7, 128), F32)], axis=0)
    og = jnp.concatenate([out_grad, jnp.zeros((128, 8), F32)], axis=1).T

    mine = after(mine, lam8, rho8, pwb, pwf, lam64, wt, consts, taps, og, at)
    other = to_chan(mine, 0, 0, 1)
    weight = in_weight.reshape(3, 8, 2, 256, 128)
    block, wblock = ((8, ROWS, 256), BF16), ((3, 8, 256, 128), BF16)
    half = far_call(
        half_kernel, 4.0, at, [((ROWS, 384), F32)], [block, wblock, ((ROWS, 384), F32)], 48, mine, weight
    )[0]
    given = lax.ppermute(mine, ("seq", "chan"), joint_pairs("give"))
    ext, prod, gl, st, send = call(
        states_kernel,
        8.0,
        at,
        [((528, 384), F32), ((ROWS, 128), F32), ((ROWS, 128), F32), ((64, 8, 128), F32), ((16, 48, 128), F32)],
        [block, wblock, ((64, 128), F32)],
        half, taps, og, lam8, pwf, pwb,
        far=(other, weight),
        sems=48,
        staged=True,
    )
    arrived = exchange(send, "seq")
    y, gp, sums = call(
        scan_kernel,
        7.0,
        None,
        [((SUB, 8, 128), F32)] * 2 + [((96, 8, 128), F32)],
        [],
        prod, gl, st, lam8, rho8, lam64,
    )
    shapes = [((8, ROWS, 256), BF16), ((8, 256, ROWS), BF16)]
    kept = far_call(turn_kernel, 3.5, at, shapes[1:], shapes, 16, mine, other, st)[0]
    given = after(given, arrived)
    passed = lax.ppermute(given, ("seq", "chan"), joint_pairs("pass"))
    mixed_out, low = call(
        grads_kernel,
        8.0,
        at,
        [((128, ROWS), F32), ((ROWS + 32, 384), BF16)],
        [((EXT, 128), F32), ((EXT, 128), F32), ((EXT, 384), F32), ((EXT, 384), F32)]
        + [((EXT, 128), F32), ((EXT, 128), F32), ((48, 128), F32)],
        arrived, wt, consts, lam8, rho8, pwf, pwb, y, gp, sums, st, ext, taps, og,
        late=(kept,),
        staged=True,
    )

    low_y = to_seq(low, 0, 1)
    low_core = to_chan(low, 0, 0, 1)
    terms = far_call(
        input_kernel,
        6.0,
        at,
        [((256, ROWS), BF16)] * 8,
        [((2, ROWS, 384), BF16), ((768, ROWS), BF16), ((8, 2, 3, 256, 128), BF16), ((8, 256, ROWS), BF16)],
        26,
        low, low_core, weight, partner.reshape(weight.shape),
    )
    grads = far_call(
        weight_kernel,
        5.0,
        at,
        [((8, 288, 384), BF16)],
        [((8, 256, ROWS), BF16), block, ((2, ROWS + 32, 384), BF16), ((8, 288, 384), BF16)],
        26,
        kept, given, passed, low, low_y, terms[0],
    )[0]
    terms = [terms[0]] + [to_chan(terms[r], r // 2, r % 2) for r in (2, 6, 4, 1, 3, 7, 5)]
    grads = exchange(grads, "seq", COLUMNS)
    input_grad = call(fold_input_kernel, 2.5, None, [((ROWS, 256), F32)], [], *terms)[0]
    weight_grad, small = call(
        fold_kernel, 2.5, None, [((3, 256, 128), F32), ((48, 128), F32)], [], grads
    )
    residue_grad = small[:32].reshape(2, MODES, 128)
    taps_grad = small[32:41].reshape(3, 3, 128)
    return (mixed_out, input_grad, weight_grad, taps_grad, residue_grad, small[41])


def solution(mesh):
    in_specs = (
        P("seq", "chan"),
        P(None, None, "chan"),
        P(None, None, "chan"),
        P(None, "chan"),
        P(None, "chan"),
        P(None, None, "chan"),
        P("chan"),
        P("chan", "seq"),
    )
    out_specs = (
        P("chan", "seq"),
        P("seq", "chan"),
        P(None, "seq", "chan"),
        P(None, None, "chan"),
        P(None, None, "chan"),
        P("chan"),
    )
    return jax.shard_map(
        on_device, mesh=mesh, in_specs=in_specs, out_specs=out_specs, check_vma=False
    )
```

time: 545 us -> 177 us (0.32)
  waiting for transfers between devices: 296 us -> 67.1 us
  blocking collectives: 84.4 us -> 0 us
  matrix products: 62.6 us -> 0 us
  Pallas kernels: 0 us -> 49.5 us
  other arithmetic: 32.5 us -> 5.32 us
  between operations: 14.6 us -> 1.16 us
  starting transfers between devices: 27 us -> 38.2 us
  local copies, waits for them, and re-layouts: 22.8 us -> 14.9 us
    reduce_scatter x2 -> x0, waiting for transfers between devices: 196 us -> none  [the longest x1 114 us: on_device(): lax.psum_scatter(input_term, 'chan', scatter_dimension=1, tiled=True)]
    all_gather x1 -> x0, waiting for transfers between devices: 70.2 us -> none  [on_device(): gathered = lax.all_gather(hidden_in, 'chan', axis=1, tiled=True)]
    dot_general x39 -> x0, matrix products: 62.6 us -> none  [the longest x1 5.66 us: on_device(): jnp.einsum('kct,kdc->td', grad_low, in_weight, preferred_element_type=jnp...]
    psum x1 -> x0, blocking collectives: 55.1 us -> none  [on_device(): lax.psum((local_residue, local_taps, skip_grad), 'seq')]
    pallas_call x0 -> x11, Pallas kernels: none -> 49.5 us  [the longest x9 49.5 us: raw_call(): pl.pallas_call(kernel, in_specs=in_specs, out_specs=out_specs, out_shape=...]
    all_to_all x2 -> x0, blocking collectives: 29.3 us -> none  [the longest x1 17 us: on_device(): lax.all_to_all(conv_cols, 'seq', split_axis=1, concat_axis=0, tiled=True)]
    reduce_sum x3 -> x0, other arithmetic: 23.6 us -> none  [the longest x1 19.1 us: residue_sums(): jnp.sum(grad_resp[None] * decay_cos, axis=2)]
    all_to_all x4 -> x3, waiting for transfers between devices: 20.1 us -> 43.6 us  [exchange(): lax.all_to_all(x, axis, split_axis=0, concat_axis=0, tiled=True, axis_ind...]
  transfers between devices with their start and end apart: 9 -> 16, of which waited for: 8 -> 8; matrix products, arithmetic and copies ran while one was open for 6% -> 4% of each run, Pallas kernels for 0% -> 23%
where the time goes in v1:
time: 177 us; the launch traced here: 176 us
  waiting for transfers between devices  67.1 us (38%)
  Pallas kernels  49.5 us (28%)
  starting transfers between devices  38.2 us (22%)
  local copies, waits for them, and re-layouts  14.9 us (8%)
  other arithmetic  5.32 us (3%)
    pallas_call x9, Pallas kernels, raw_call(): pl.pallas_call(kernel, in_specs=in_specs, out_specs=out_specs, out_shape=...  49.5 us
    all_to_all x3, waiting for transfers between devices, exchange(): lax.all_to_all(x, axis, split_axis=0, concat_axis=0, tiled=True, axis_ind...  43.6 us
    all_to_all x3, starting transfers between devices, exchange(): lax.all_to_all(x, axis, split_axis=0, concat_axis=0, tiled=True, axis_ind...  20.7 us
    ppermute x10, waiting for transfers between devices, to_chan(): return lax.ppermute(x, 'chan', chan_pairs(dx, dy, dc))  20.4 us
    ppermute x10, starting transfers between devices, to_chan(): return lax.ppermute(x, 'chan', chan_pairs(dx, dy, dc))  11.5 us
    unnamed x53, local copies, waits for them, and re-layouts  5.19 us
    ppermute x1, starting transfers between devices, on_device(): given = lax.ppermute(mine, ('seq', 'chan'), joint_pairs('give'))  3.59 us
  transfers between devices with their start and end apart: 16, of which 8 were waited for; matrix products, arithmetic and copies ran while one was open for 4% of the time, Pallas kernels for 23%

profile of v1, /device:TPU:1, one launch (start us, length us, event | category | flops | bytes accessed | tf_op | source)
XLA Modules:
  0.0 176.1 jit_solution(10214959050605370778)
XLA Ops:
  0.6 2.4 %broadcast_in_dim.14 = bf16[8,512,256]{2,1,0:T(8,128)(2,1)} broadcast(bf16[512,256]{1,0:T(8,128)(2,1)} %param.8), dimensions={1,2} | broadcast | bytes 2359296 | tf_op jit(solution)/shard_map/broadcast_in_dim | solution.py:607
  3.1 7.6 %all-to-all-start = ((bf16[8,512,256]{2,1,0:T(8,128)(2,1)}), bf16[8,512,256]{2,1,0:T(8,128)(2,1)S(1)}, u32[]{:S(2)}, u32[]{:S(2)}) async-start(bf16[8,512,256]{2,1,0:T(8,128)(2,1)} %broadcast_in_dim.14), calls=%async_computation | async-start | bytes 4194304 | tf_op jit(solution)/shard_map/all_to_all | solution.py:582
  15.1 1.0 fusion.17
  18.4 22.8 %all-to-all-done.__0_ = bf16[8,512,256]{2,1,0:T(8,128)(2,1)S(1)} async-done(((bf16[8,512,256]{2,1,0:T(8,128)(2,1)}), bf16[8,512,256]{2,1,0:T(8,128)(2,1)S(1)}, u32[]{:S(2)}, u32[]{:S(2)}) %all-to-all-start) | async-done | bytes 2097184 | tf_op jit(solution)/shard_map/all_to_all | solution.py:582
  42.7 1.6 collective-permute-start
  44.3 3.6 %collective-permute-start.10 = (bf16[8,512,256]{2,1,0:T(8,128)(2,1)}, bf16[8,512,256]{2,1,0:T(8,128)(2,1)}, u32[]{:S(2)}, u32[]{:S(2)}) collective-permute-start(bf16[8,512,256]{2,1,0:T(8,128)(2,1)} %shard_map.127.mine_far.a), channel_id=1, source_target_pairs={{1,17},{3,19},{5,21},{7,23},{9,25},{11,27},{13,29},{15,31},{16,0},... | collective-permute-start | bytes 6291464 | tf_op jit(solution)/shard_map/ppermute | solution.py:641
  47.9 4.8 %shard_map.128.refs_3_ = f32[512,384]{1,0:T(8,128)} custom-call(s32[6]{0:T(128)} %stack.31.__10_.at.refs_0_, bf16[8,512,256]{2,1,0:T(8,128)(2,1)} %shard_map.127.mine_far.a, bf16[3,8,2,256,128]{4,3,2,1,0:T(8,128)(2,1)} %bitcast.22), custom_call_target="tpu_custom_call" | custom-call | flops 4400000000 | tf_op jit(solution)/shard_map/pallas_call | solution.py:495
  52.7 8.1 %shard_map.129 = (f32[528,384]{1,0:T(8,128)}, f32[512,128]{1,0:T(8,128)}, f32[512,128]{1,0:T(8,128)}, f32[64,8,128]{2,1,0:T(8,128)}, f32[16,48,128]{2,1,0:T(8,128)}) custom-call(s32[6]{0:T(128)} %stack.31.__10_.at.refs_0_, bf16[8,512,256]{2,1,0:T(8,128)(2,1)} %collective-permute-done.refs_1_.b, bf16[3,8,2,256,128]{4,3,2,1,0:T(8,128)(2,1)} %bitcast.23, ...), custom_call_target="tpu_custom_call" | custom-call | flops 8800000000 | tf_op jit(solution)/shard_map/pallas_call | solution.py:495
  60.8 9.4 %all-to-all-start.1 = ((f32[16,48,128]{2,1,0:T(8,128)}), f32[16,48,128]{2,1,0:T(8,128)S(1)}, u32[]{:S(2)}, u32[]{:S(2)}) async-start(f32[16,48,128]{2,1,0:T(8,128)} %get-tuple-element.26), calls=%async_computation.1 | async-start | bytes 786432 | tf_op jit(solution)/shard_map/all_to_all | solution.py:582
  70.2 7.3 %shard_map.130 = (f32[64,8,128]{2,1,0:T(8,128)}, f32[64,8,128]{2,1,0:T(8,128)}, f32[96,8,128]{2,1,0:T(8,128)}) custom-call(f32[512,128]{1,0:T(8,128)} %get-tuple-element.27.refs_0_, f32[512,128]{1,0:T(8,128)} %get-tuple-element.28.refs_1_, f32[64,8,128]{2,1,0:T(8,128)} %get-tuple-element.29.refs_2_.rest_0_.refs_11_, ...), custom_call_target="tpu_custom_call" | custom-call | flops 7699999744 | tf_op jit(solution)/shard_map/pallas_call | solution.py:495
  77.5 6.6 %all-to-all-done.1.refs_1_.__1_ = f32[16,48,128]{2,1,0:T(8,128)S(1)} async-done(((f32[16,48,128]{2,1,0:T(8,128)}), f32[16,48,128]{2,1,0:T(8,128)S(1)}, u32[]{:S(2)}, u32[]{:S(2)}) %all-to-all-start.1) | async-done | bytes 393248 | tf_op jit(solution)/shard_map/all_to_all | solution.py:582
  84.8 1.3 collective-permute-start.11
  86.1 3.4 %shard_map.131.refs_15_.kept = bf16[8,256,512]{2,1,0:T(8,128)(2,1)} custom-call(s32[6]{0:T(128)} %stack.31.__10_.at.refs_0_, bf16[8,512,256]{2,1,0:T(8,128)(2,1)} %shard_map.127.mine_far.a, bf16[8,512,256]{2,1,0:T(8,128)(2,1)} %collective-permute-done.refs_1_.b, f32[64,8,128]{2,1,0:T(8,128)} %get-tuple-element.29.refs_2_.rest_0_.refs_11_), custom_call_target="tpu_custom_call" | custom-call | flops 3849999872 | tf_op jit(solution)/shard_map/pallas_call | solution.py:495
  89.6 8.2 %shard_map.132 = (f32[128,512]{1,0:T(8,128)}, bf16[544,384]{1,0:T(8,128)(2,1)}) custom-call(s32[6]{0:T(128)} %stack.31.__10_.at.refs_0_, f32[16,48,128]{2,1,0:T(8,128)} %copy-done.2, f32[16,32,128]{2,1,0:T(8,128)} %pad_maximum_fusion.1.__6_.refs_2_, f32[200,128]{1,0:T(8,128)} %copy-done.6, f32[32,8,128]{2,1,0:T(8,128)} %broadcast_in_dim.15.__1_.refs_6_.refs_3_.refs_4_, ...), custom_call_target="tpu_custom_call" | custom-call | flops 8800000000 | tf_op jit(solution)/shard_map/pallas_call | solution.py:495
  97.8 3.7 %collective-permute-start.1 = (bf16[544,384]{1,0:T(8,128)(2,1)}, bf16[544,384]{1,0:T(8,128)(2,1)S(1)}, u32[]{:S(2)}, u32[]{:S(2)}) collective-permute-start(bf16[544,384]{1,0:T(8,128)(2,1)} %get-tuple-element.35.low), channel_id=1, source_target_pairs={{0,1},{1,0},{2,3},{3,2},{4,5},{5,4},{6,7},{7,6},{8,9},{9,8},{10,11... | collective-permute-start | bytes 1253384 | tf_op jit(solution)/shard_map/ppermute | solution.py:29
  101.5 1.0 collective-permute-start.12
  103.9 5.9 %shard_map.133 = (bf16[256,512]{1,0:T(8,128)(2,1)}, bf16[256,512]{1,0:T(8,128)(2,1)}, bf16[256,512]{1,0:T(8,128)(2,1)}, bf16[256,512]{1,0:T(8,128)(2,1)}, bf16[2...) custom-call(s32[6]{0:T(128)} %stack.31.__10_.at.refs_0_, ...), custom_call_target="tpu_custom_call" | custom-call | flops 6600000000 | tf_op jit(solution)/shard_map/pallas_call | solution.py:495
  109.8 3.1 %collective-permute-done.12.low_y = bf16[544,384]{1,0:T(8,128)(2,1)S(1)} collective-permute-done((bf16[544,384]{1,0:T(8,128)(2,1)}, bf16[544,384]{1,0:T(8,128)(2,1)S(1)}, u32[]{:S(2)}, u32[]{:S(2)}) %collective-permute-start.12) | collective-permute-done | bytes 417824 | tf_op jit(solution)/shard_map/ppermute | solution.py:33
  113.6 6.6 %shard_map.136 = bf16[8,288,384]{2,1,0:T(8,128)(2,1)} custom-call(s32[6]{0:T(128)} %stack.31.__10_.at.refs_0_, bf16[8,256,512]{2,1,0:T(8,128)(2,1)} %shard_map.131.refs_15_.kept, bf16[8,512,256]{2,1,0:T(8,128)(2,1)} %shard_map.135.given, bf16[8,512,256]{2,1,0:T(8,128)(2,1)} %collective-permute-done.11.passed, bf16[544,384]{1,0:T(8,128)(2,1)} %get-tuple-element.35.low, ...), custom_call_target="tpu_custom_call" | custom-call | flops 5500000256 | tf_op jit(solution)/shard_map/pallas_call | solution.py:495
  120.3 3.7 %all-to-all-start.2 = ((bf16[8,288,384]{2,1,0:T(8,128)(2,1)}), bf16[8,288,384]{2,1,0:T(8,128)(2,1)S(1)}, u32[]{:S(2)}, u32[]{:S(2)}) async-start(bf16[8,288,384]{2,1,0:T(8,128)(2,1)} %shard_map.136), calls=%async_computation.2 | async-start | bytes 3538944 | tf_op jit(solution)/shard_map/all_to_all | solution.py:582
  124.1 2.7 %collective-permute-start.4 = (bf16[256,512]{1,0:T(8,128)(2,1)S(1)}, bf16[256,512]{1,0:T(8,128)(2,1)S(1)}, u32[]{:S(2)}, u32[]{:S(2)}) collective-permute-start(bf16[256,512]{1,0:T(8,128)(2,1)S(1)} %copy-done.17), channel_id=1, source_target_pairs={{0,12},{1,13},{2,14},{3,15},{4,0},{5,1},{6,2},{7,3},{8,4},{9,5},{1... | collective-permute-start | bytes 786440 | tf_op jit(solution)/shard_map/ppermute | solution.py:29
  126.8 1.4 collective-permute-start.6
  128.2 2.0 %collective-permute-start.7 = (bf16[256,512]{1,0:T(8,128)(2,1)S(1)}, bf16[256,512]{1,0:T(8,128)(2,1)S(1)}, u32[]{:S(2)}, u32[]{:S(2)}) collective-permute-start(bf16[256,512]{1,0:T(8,128)(2,1)S(1)} %copy-done.14), channel_id=1, source_target_pairs={{0,6},{1,7},{2,4},{3,5},{4,10},{5,11},{6,8},{7,9},{8,14},{9,15},{1... | collective-permute-start | bytes 786440 | tf_op jit(solution)/shard_map/ppermute | solution.py:29
  130.2 7.4 %collective-permute-done.3.refs_1_ = bf16[256,512]{1,0:T(8,128)(2,1)S(1)} collective-permute-done((bf16[256,512]{1,0:T(8,128)(2,1)}, bf16[256,512]{1,0:T(8,128)(2,1)S(1)}, u32[]{:S(2)}, u32[]{:S(2)}) %collective-permute-start.3) | collective-permute-done | bytes 262176 | tf_op jit(solution)/shard_map/ppermute | solution.py:29
  137.8 8.5 %collective-permute-done.7.refs_5_ = bf16[256,512]{1,0:T(8,128)(2,1)S(1)} collective-permute-done((bf16[256,512]{1,0:T(8,128)(2,1)S(1)}, bf16[256,512]{1,0:T(8,128)(2,1)S(1)}, u32[]{:S(2)}, u32[]{:S(2)}) %collective-permute-start.7) | collective-permute-done | bytes 262176 | tf_op jit(solution)/shard_map/ppermute | solution.py:29
  146.3 3.9 %collective-permute-done.8.refs_6_ = bf16[256,512]{1,0:T(8,128)(2,1)S(1)} collective-permute-done((bf16[256,512]{1,0:T(8,128)(2,1)S(1)}, bf16[256,512]{1,0:T(8,128)(2,1)S(1)}, u32[]{:S(2)}, u32[]{:S(2)}) %collective-permute-start.8) | collective-permute-done | bytes 262176 | tf_op jit(solution)/shard_map/ppermute | solution.py:29
  151.7 2.7 %shard_map.134 = f32[512,256]{1,0:T(8,128)} custom-call(bf16[256,512]{1,0:T(8,128)(2,1)} %get-tuple-element.36.refs_0_.rest_0_, bf16[256,512]{1,0:T(8,128)(2,1)} %copy-done.18, bf16[256,512]{1,0:T(8,128)(2,1)} %copy-done.19, bf16[256,512]{1,0:T(8,128)(2,1)} %copy-done.20, bf16[256,512]{1,0:T(8,128)(2,1)} %copy-done.21, bf16[256,512]{1,0:T(8,128)(2,1)} %copy-done.22, ...), custom_call_target="tpu_custom_call" | custom-call | flops 2750000128 | tf_op jit(solution)/shard_map/pallas_call | solution.py:495
  154.4 14.2 %all-to-all-done.2.refs_0_ = bf16[8,288,384]{2,1,0:T(8,128)(2,1)S(1)} async-done(((bf16[8,288,384]{2,1,0:T(8,128)(2,1)}), bf16[8,288,384]{2,1,0:T(8,128)(2,1)S(1)}, u32[]{:S(2)}, u32[]{:S(2)}) %all-to-all-start.2) | async-done | bytes 1769504 | tf_op jit(solution)/shard_map/all_to_all | solution.py:582
  168.6 1.2 copy-done.1
  169.8 2.4 %shard_map.137 = (f32[3,256,128]{2,1,0:T(8,128)}, f32[48,128]{1,0:T(8,128)}) custom-call(bf16[8,288,384]{2,1,0:T(8,128)(2,1)} %copy-done.1), custom_call_target="tpu_custom_call" | custom-call | flops 2750000128 | tf_op jit(solution)/shard_map/pallas_call | solution.py:495
  173.0 1.3 slice.20
  174.3 1.2 slice_bitcast_fusion.2
  (102 shorter events, 13.8 us)
Async XLA Ops:
  3.1 7.7 %copy-start.3 = (f32[16,128]{1,0:T(8,128)S(1)}, f32[16,128]{1,0:T(8,128)}, u32[]{:S(2)}) copy-start(f32[16,128]{1,0:T(8,128)} %param.12) | copy-start | bytes 24580
  3.1 7.7 %copy-start.4 = (f32[16,128]{1,0:T(8,128)S(1)}, f32[16,128]{1,0:T(8,128)}, u32[]{:S(2)}) copy-start(f32[16,128]{1,0:T(8,128)} %param.11) | copy-start | bytes 24580
  3.1 7.9 %copy-start.7 = (f32[2,16,128]{2,1,0:T(8,128)S(1)}, f32[2,16,128]{2,1,0:T(8,128)}, u32[]{:S(2)}) copy-start(f32[2,16,128]{2,1,0:T(8,128)} %param.13) | copy-start | bytes 49156
  3.1 8.4 %copy-start.8 = (f32[3,3,128]{2,1,0:T(4,128)S(1)}, f32[3,3,128]{2,1,0:T(4,128)}, u32[]{:S(2)}) copy-start(f32[3,3,128]{2,1,0:T(4,128)} %param.10) | copy-start | bytes 13828
  3.1 8.5 %copy-start.5 = (f32[128,512]{1,0:T(8,128)S(1)}, f32[128,512]{1,0:T(8,128)}, u32[]{:S(2)}) copy-start(f32[128,512]{1,0:T(8,128)} %param.15) | copy-start | bytes 786436
  3.1 38.1 %all-to-all-start = ((bf16[8,512,256]{2,1,0:T(8,128)(2,1)}), bf16[8,512,256]{2,1,0:T(8,128)(2,1)S(1)}, u32[]{:S(2)}, u32[]{:S(2)}) async-start(bf16[8,512,256]{2,1,0:T(8,128)(2,1)} %broadcast_in_dim.14), calls=%async_computation | async-start | bytes 4194304 | tf_op jit(solution)/shard_map/all_to_all | solution.py:582
  11.5 6.9 %copy-start.9 = (f32[128]{0:T(128)S(1)}, f32[128]{0:T(128)}, u32[]{:S(2)}) copy-start(f32[128]{0:T(128)} %param.14) | copy-start | bytes 1540
  18.4 24.2 %copy-start.6 = (f32[200,128]{1,0:T(8,128)}, f32[200,128]{1,0:T(8,128)S(1)}, u32[]{:S(2)}) copy-start(f32[200,128]{1,0:T(8,128)S(1)} %constant_dynamic-update-slice_fusion.__7_.refs_3_) | copy-start | bytes 307204
  42.7 10.0 %collective-permute-start = (bf16[8,512,256]{2,1,0:T(8,128)(2,1)}, bf16[8,512,256]{2,1,0:T(8,128)(2,1)}, u32[]{:S(2)}, u32[]{:S(2)}) collective-permute-start(bf16[8,512,256]{2,1,0:T(8,128)(2,1)} %shard_map.127.mine_far.a), channel_id=1, source_target_pairs={{0,1},{1,0},{2,3},{3,2},{4,5},{5,4},{6,7},{7,6},{8,9},{9,8},{10,11... | collective-permute-start | bytes 6291464 | tf_op jit(solution)/shard_map/ppermute | solution.py:29
  44.3 33.2 %collective-permute-start.10 = (bf16[8,512,256]{2,1,0:T(8,128)(2,1)}, bf16[8,512,256]{2,1,0:T(8,128)(2,1)}, u32[]{:S(2)}, u32[]{:S(2)}) collective-permute-start(bf16[8,512,256]{2,1,0:T(8,128)(2,1)} %shard_map.127.mine_far.a), channel_id=1, source_target_pairs={{1,17},{3,19},{5,21},{7,23},{9,25},{11,27},{13,29},{15,31},{16,0},... | collective-permute-start | bytes 6291464 | tf_op jit(solution)/shard_map/ppermute | solution.py:641
  47.9 54.6 %collective-permute-start.2 = (bf16[3,4096,128]{2,1,0:T(8,128)(2,1)}, bf16[3,4096,128]{2,1,0:T(8,128)(2,1)}, u32[]{:S(2)}, u32[]{:S(2)}) collective-permute-start(bf16[3,4096,128]{2,1,0:T(8,128)(2,1)} %param.9), channel_id=1, source_target_pairs={{0,1},{1,0},{2,3},{3,2},{4,5},{5,4},{6,7},{7,6},{8,9},{9,8},{10,11... | collective-permute-start | bytes 9437192 | tf_op jit(solution)/shard_map/ppermute | solution.py:29
  60.8 23.3 %all-to-all-start.1 = ((f32[16,48,128]{2,1,0:T(8,128)}), f32[16,48,128]{2,1,0:T(8,128)S(1)}, u32[]{:S(2)}, u32[]{:S(2)}) async-start(f32[16,48,128]{2,1,0:T(8,128)} %get-tuple-element.26), calls=%async_computation.1 | async-start | bytes 786432 | tf_op jit(solution)/shard_map/all_to_all | solution.py:582
  84.8 28.0 %collective-permute-start.11 = (bf16[8,512,256]{2,1,0:T(8,128)(2,1)}, bf16[8,512,256]{2,1,0:T(8,128)(2,1)}, u32[]{:S(2)}, u32[]{:S(2)}) collective-permute-start(bf16[8,512,256]{2,1,0:T(8,128)(2,1)} %shard_map.135.given), channel_id=1, source_target_pairs={{0,1},{2,3},{4,5},{6,7},{8,9},{10,11},{12,13},{14,15},{17,16},{19,... | collective-permute-start | bytes 6291464 | tf_op jit(solution)/shard_map/ppermute | solution.py:665
  97.8 5.3 %collective-permute-start.1 = (bf16[544,384]{1,0:T(8,128)(2,1)}, bf16[544,384]{1,0:T(8,128)(2,1)S(1)}, u32[]{:S(2)}, u32[]{:S(2)}) collective-permute-start(bf16[544,384]{1,0:T(8,128)(2,1)} %get-tuple-element.35.low), channel_id=1, source_target_pairs={{0,1},{1,0},{2,3},{3,2},{4,5},{5,4},{6,7},{7,6},{8,9},{9,8},{10,11... | collective-permute-start | bytes 1253384 | tf_op jit(solution)/shard_map/ppermute | solution.py:29
  101.5 11.4 %collective-permute-start.12 = (bf16[544,384]{1,0:T(8,128)(2,1)}, bf16[544,384]{1,0:T(8,128)(2,1)S(1)}, u32[]{:S(2)}, u32[]{:S(2)}) collective-permute-start(bf16[544,384]{1,0:T(8,128)(2,1)} %get-tuple-element.35.low), channel_id=1, source_target_pairs={{0,16},{16,0},{32,48},{48,32},{64,80},{80,64},{96,112},{112,96},{1... | collective-permute-start | bytes 1253384 | tf_op jit(solution)/shard_map/ppermute | solution.py:33
  120.2 6.5 %copy-start.16 = (bf16[256,512]{1,0:T(8,128)(2,1)S(1)}, bf16[256,512]{1,0:T(8,128)(2,1)}, u32[]{:S(2)}) copy-start(bf16[256,512]{1,0:T(8,128)(2,1)} %get-tuple-element.39) | copy-start | bytes 786436
  120.3 6.5 %copy-start.15 = (bf16[256,512]{1,0:T(8,128)(2,1)S(1)}, bf16[256,512]{1,0:T(8,128)(2,1)}, u32[]{:S(2)}) copy-start(bf16[256,512]{1,0:T(8,128)(2,1)} %get-tuple-element.40) | copy-start | bytes 786436
  120.3 7.9 %copy-start.14 = (bf16[256,512]{1,0:T(8,128)(2,1)S(1)}, bf16[256,512]{1,0:T(8,128)(2,1)}, u32[]{:S(2)}) copy-start(bf16[256,512]{1,0:T(8,128)(2,1)} %get-tuple-element.41) | copy-start | bytes 786436
  120.3 17.3 %copy-start.13 = (bf16[256,512]{1,0:T(8,128)(2,1)S(1)}, bf16[256,512]{1,0:T(8,128)(2,1)}, u32[]{:S(2)}) copy-start(bf16[256,512]{1,0:T(8,128)(2,1)} %get-tuple-element.42) | copy-start | bytes 786436
  120.3 17.3 %copy-start.12 = (bf16[256,512]{1,0:T(8,128)(2,1)S(1)}, bf16[256,512]{1,0:T(8,128)(2,1)}, u32[]{:S(2)}) copy-start(bf16[256,512]{1,0:T(8,128)(2,1)} %get-tuple-element.43) | copy-start | bytes 786436
  120.3 48.3 %all-to-all-start.2 = ((bf16[8,288,384]{2,1,0:T(8,128)(2,1)}), bf16[8,288,384]{2,1,0:T(8,128)(2,1)S(1)}, u32[]{:S(2)}, u32[]{:S(2)}) async-start(bf16[8,288,384]{2,1,0:T(8,128)(2,1)} %shard_map.136), calls=%async_computation.2 | async-start | bytes 3538944 | tf_op jit(solution)/shard_map/all_to_all | solution.py:582
  124.0 13.5 %collective-permute-start.3 = (bf16[256,512]{1,0:T(8,128)(2,1)}, bf16[256,512]{1,0:T(8,128)(2,1)S(1)}, u32[]{:S(2)}, u32[]{:S(2)}) collective-permute-start(bf16[256,512]{1,0:T(8,128)(2,1)} %get-tuple-element.37), channel_id=1, source_target_pairs={{0,4},{1,5},{2,6},{3,7},{4,8},{5,9},{6,10},{7,11},{8,12},{9,13},{1... | collective-permute-start | bytes 786440 | tf_op jit(solution)/shard_map/ppermute | solution.py:29
  124.1 13.4 %collective-permute-start.4 = (bf16[256,512]{1,0:T(8,128)(2,1)S(1)}, bf16[256,512]{1,0:T(8,128)(2,1)S(1)}, u32[]{:S(2)}, u32[]{:S(2)}) collective-permute-start(bf16[256,512]{1,0:T(8,128)(2,1)S(1)} %copy-done.17), channel_id=1, source_target_pairs={{0,12},{1,13},{2,14},{3,15},{4,0},{5,1},{6,2},{7,3},{8,4},{9,5},{1... | collective-permute-start | bytes 786440 | tf_op jit(solution)/shard_map/ppermute | solution.py:29
  126.8 10.9 %collective-permute-start.5 = (bf16[256,512]{1,0:T(8,128)(2,1)S(1)}, bf16[256,512]{1,0:T(8,128)(2,1)S(1)}, u32[]{:S(2)}, u32[]{:S(2)}) collective-permute-start(bf16[256,512]{1,0:T(8,128)(2,1)S(1)} %copy-done.16), channel_id=1, source_target_pairs={{0,8},{1,9},{2,10},{3,11},{4,12},{5,13},{6,14},{7,15},{8,0},{9,1},... | collective-permute-start | bytes 786440 | tf_op jit(solution)/shard_map/ppermute | solution.py:29
  126.8 10.9 %collective-permute-start.6 = (bf16[256,512]{1,0:T(8,128)(2,1)S(1)}, bf16[256,512]{1,0:T(8,128)(2,1)S(1)}, u32[]{:S(2)}, u32[]{:S(2)}) collective-permute-start(bf16[256,512]{1,0:T(8,128)(2,1)S(1)} %copy-done.15), channel_id=1, source_target_pairs={{0,2},{1,3},{2,0},{3,1},{4,6},{5,7},{6,4},{7,5},{8,10},{9,11},{10,... | collective-permute-start | bytes 786440 | tf_op jit(solution)/shard_map/ppermute | solution.py:29
  128.2 18.1 %collective-permute-start.7 = (bf16[256,512]{1,0:T(8,128)(2,1)S(1)}, bf16[256,512]{1,0:T(8,128)(2,1)S(1)}, u32[]{:S(2)}, u32[]{:S(2)}) collective-permute-start(bf16[256,512]{1,0:T(8,128)(2,1)S(1)} %copy-done.14), channel_id=1, source_target_pairs={{0,6},{1,7},{2,4},{3,5},{4,10},{5,11},{6,8},{7,9},{8,14},{9,15},{1... | collective-permute-start | bytes 786440 | tf_op jit(solution)/shard_map/ppermute | solution.py:29
  137.6 12.6 %copy-start.18 = (bf16[256,512]{1,0:T(8,128)(2,1)}, bf16[256,512]{1,0:T(8,128)(2,1)S(1)}, u32[]{:S(2)}) copy-start(bf16[256,512]{1,0:T(8,128)(2,1)S(1)} %collective-permute-done.3.refs_1_) | copy-start | bytes 786436
  137.6 12.6 %collective-permute-start.8 = (bf16[256,512]{1,0:T(8,128)(2,1)S(1)}, bf16[256,512]{1,0:T(8,128)(2,1)S(1)}, u32[]{:S(2)}, u32[]{:S(2)}) collective-permute-start(bf16[256,512]{1,0:T(8,128)(2,1)S(1)} %copy-done.13), channel_id=1, source_target_pairs={{0,14},{1,15},{2,12},{3,13},{4,2},{5,3},{6,0},{7,1},{8,6},{9,7},{1... | collective-permute-start | bytes 786440 | tf_op jit(solution)/shard_map/ppermute | solution.py:29
  137.6 12.6 %copy-start.19 = (bf16[256,512]{1,0:T(8,128)(2,1)}, bf16[256,512]{1,0:T(8,128)(2,1)S(1)}, u32[]{:S(2)}) copy-start(bf16[256,512]{1,0:T(8,128)(2,1)S(1)} %collective-permute-done.4.refs_2_) | copy-start | bytes 786436
  137.6 13.3 %collective-permute-start.9 = (bf16[256,512]{1,0:T(8,128)(2,1)S(1)}, bf16[256,512]{1,0:T(8,128)(2,1)S(1)}, u32[]{:S(2)}, u32[]{:S(2)}) collective-permute-start(bf16[256,512]{1,0:T(8,128)(2,1)S(1)} %copy-done.12), channel_id=1, source_target_pairs={{0,10},{1,11},{2,8},{3,9},{4,14},{5,15},{6,12},{7,13},{8,2},{9,3},... | collective-permute-start | bytes 786440 | tf_op jit(solution)/shard_map/ppermute | solution.py:29
  137.7 12.5 %copy-start.20 = (bf16[256,512]{1,0:T(8,128)(2,1)}, bf16[256,512]{1,0:T(8,128)(2,1)S(1)}, u32[]{:S(2)}) copy-start(bf16[256,512]{1,0:T(8,128)(2,1)S(1)} %collective-permute-done.5.refs_3_) | copy-start | bytes 786436
  137.7 12.5 %copy-start.21 = (bf16[256,512]{1,0:T(8,128)(2,1)}, bf16[256,512]{1,0:T(8,128)(2,1)S(1)}, u32[]{:S(2)}) copy-start(bf16[256,512]{1,0:T(8,128)(2,1)S(1)} %collective-permute-done.6.refs_4_) | copy-start | bytes 786436
  (9 other events, 14.3 us)

commit v2 on v1

--- a/solution.py
+++ b/solution.py
@@ -42,9 +42,33 @@
     return mag * (cos1 * cos2 - sin1 * sin2), mag * (sin1 * cos2 + cos1 * sin2)
 
 
-def spread(pair):
-    both = jnp.concatenate(pair, axis=0)
-    return jnp.broadcast_to(both[:, None, :], (2 * MODES, 8, both.shape[1]))
+COUNTS = (1.0, -1.0, float(ROWS), float(ROWS - 1), float(ROWS - 2), float(SUB), float(2 * SUB), float(4 * SUB))
+
+
+def halves(ref, row=None):
+    if row is None:
+        return ref[0:MODES, :], ref[MODES : 2 * MODES, :]
+    return ref[row, 0:MODES, :], ref[row, MODES : 2 * MODES, :]
+
+
+def fill(pw, rows, dst):
+    for n in range(2 * MODES):
+        line = rows[n : n + 1, :] if pw is None else pw[rows, n : n + 1, :]
+        dst[n] = jnp.broadcast_to(line, (8, 128))
+
+
+def sub_powers(pw, dst, back):
+    place = lax.broadcasted_iota(jnp.int32, (8, 128), 0)
+    place = 7 - place if back else place
+    for n in range(MODES):
+        re, im = jnp.ones((8, 128), F32), jnp.zeros((8, 128), F32)
+        for level in range(3):
+            here = (place >> level) & 1 == 1
+            step = pw[5 + level, n : n + 1, :], pw[5 + level, MODES + n : MODES + n + 1, :]
+            step = tuple(jnp.where(here, s, t) for s, t in zip(step, (1.0, 0.0)))
+            re, im = times((re, im), step)
+        dst[n] = re
+        dst[MODES + n] = im
 
 
 def times(a, b):
@@ -83,34 +107,38 @@
 
 def convolve(taps, ext, k):
     lanes = slice(128 * k, 128 * k + 128)
-    total = taps[3 * k : 3 * k + 1, :] * ext[8 : 8 + ROWS, lanes]
-    total = total + taps[3 * k + 1 : 3 * k + 2, :] * ext[7 : 7 + ROWS, lanes]
-    return total + taps[3 * k + 2 : 3 * k + 3, :] * ext[6 : 6 + ROWS, lanes]
+    total = taps[k, 0:1, :] * ext[8 : 8 + ROWS, lanes]
+    total = total + taps[k, 1:2, :] * ext[7 : 7 + ROWS, lanes]
+    return total + taps[k, 2:3, :] * ext[6 : 6 + ROWS, lanes]
 
 
 def half_kernel(at, mine_far, weight_far, out, mine, weight, made, sems):
     copies = stream([mine_far], weight_far, at[0], [mine], weight, sems)
-    for b in range(0, 8, 4):
-        for i in range(b, b + 4):
+    for b in range(0, 8, 2):
+        for i in range(b, b + 2):
             wait_all(copies[i])
-        left = jnp.concatenate([mine[i] for i in range(b, b + 4)], axis=1)
-        right = jnp.concatenate([columns(weight, i) for i in range(b, b + 4)], axis=0)
+        left = jnp.concatenate([mine[i] for i in range(b, b + 2)], axis=1)
+        right = jnp.concatenate([columns(weight, i) for i in range(b, b + 2)], axis=0)
         total = jnp.dot(left, right, preferred_element_type=F32)
         made[...] = total if b == 0 else made[...] + total
     wait_all([pltpu.make_async_copy(made, out, sems.at[0])], start=True)
 
 
 def states_kernel(
-    at, other_far, weight_far, half, taps, og, lam, pwf, pwb,
-    ext, prod, gl, st, send, other, weight, ends, sems, io,
+    at, other_far, weight_far, half, taps, og, pw,
+    ext, prod, gl, st, send, other, weight, ends, lam, pwf, pwb, sems, io,
 ):
     seq = at[2]
     copies = stream([other_far], weight_far, 1 - at[0], [other], weight, sems)
-    for b in range(0, 8, 4):
-        for i in range(b, b + 4):
+    io.need(3)
+    fill(pw, 0, lam)
+    sub_powers(pw, pwf, True)
+    sub_powers(pw, pwb, False)
+    for b in range(0, 8, 2):
+        for i in range(b, b + 2):
             wait_all(copies[i])
-        left = jnp.concatenate([other[i] for i in range(b, b + 4)], axis=1)
-        right = jnp.concatenate([columns(weight, i) for i in range(b, b + 4)], axis=0)
+        left = jnp.concatenate([other[i] for i in range(b, b + 2)], axis=1)
+        right = jnp.concatenate([columns(weight, i) for i in range(b, b + 2)], axis=0)
         total = jnp.dot(left, right, preferred_element_type=F32)
         if b == 0:
             io.need(0)
@@ -122,12 +150,12 @@
     q, k, v = (convolve(taps, ext, i) for i in range(3))
     fresh = lax.broadcasted_iota(jnp.int32, (ROWS, 128), 0) >= 2
     prod[...] = jnp.where(fresh, k * v, 0.0)
-    gl[...] = jnp.where(fresh, og[0:ROWS, :] * q, 0.0)
+    cot = og[...].T
+    gl[...] = jnp.where(fresh, cot * q, 0.0)
     io.done(1, 2)
-    edge = [k[0:2], v[0:2], q[0:2], og[0:2, :]]
+    edge = [k[0:2], v[0:2], q[0:2], cot[0:2]]
     edge += [ext[518:520, 128 * i : 128 * i + 128] for i in range(3)]
     edge = jnp.concatenate(edge + [jnp.zeros((2, 128), F32)], axis=0)
-    io.need(3, 4, 5)
     half = MODES // 2
     for src, powers, back, base in ((prod, pwf, False, 0), (gl, pwb, True, 32)):
         for n0 in range(0, MODES, half):
@@ -158,7 +186,9 @@
         send[j, 32:48, :] = edge
 
 
-def scan_kernel(prod, gl, st, lam, rho, lam64, y, gp, sums):
+def scan_kernel(prod, gl, st, pw, res, y, gp, sums, lam, rho):
+    fill(pw, 0, lam)
+    fill(None, res, rho)
     half = MODES // 2
     place = lax.broadcasted_iota(jnp.int32, (8, 128), 0)
     for base, back in ((0, False), (32, True)):
@@ -171,7 +201,8 @@
             re, im = shift(st[base + n], 1), shift(st[base + MODES + n], 1)
             for level, by in enumerate((1, 2, 4)):
                 ar, ai = times(
-                    (shift(re, by), shift(im, by)), (lam64[32 * level + n], lam64[32 * level + MODES + n])
+                    (shift(re, by), shift(im, by)),
+                    (pw[5 + level, n : n + 1, :], pw[5 + level, MODES + n : MODES + n + 1, :]),
                 )
                 re, im = re + ar, im + ai
             sums[32 + base + n] = re
@@ -219,17 +250,19 @@
 
 
 def grads_kernel(
-    at, arrived, wt, consts, lam, rho, pwf, pwb, y, gp, sums, st, ext, taps, og,
-    mixed, low, yt, gt, gb, br, prod, gl, small, io,
+    at, arrived, pw, res, skip, y, gp, sums, st, ext, taps, og_far,
+    mixed, low, yt, gt, gb, br, prod, gl, small, og, lam, rho, pwf, pwb, io,
 ):
     seq = at[2]
 
-    def pair(ref, start):
-        return ref[start : start + MODES, :], ref[start + MODES : start + 2 * MODES, :]
-
-    io.need(0, 1, 2, 12)
-    lam16, inv16, rho16, lam512 = pair(consts, 0), pair(consts, 32), pair(consts, 64), pair(consts, 96)
-    lam511, lam510 = pair(consts, 128), pair(consts, 160)
+    io.need(1, 2, 9)
+    fill(pw, 0, lam)
+    fill(None, res, rho)
+    sub_powers(pw, pwf, True)
+    sub_powers(pw, pwb, False)
+    lam16, inv16, lam512, lam511, lam510 = (halves(pw, i) for i in range(5))
+    rho16 = halves(res)
+    io.need(0, 3)
     zero16 = jnp.zeros((MODES, 128), F32)
     s_in, u_in = (zero16, zero16), (zero16, zero16)
     zero2 = jnp.zeros((2, 128), F32)
@@ -245,7 +278,7 @@
         tilde = arrived[j, 32:40, :]
         kvq = []
         for k, rows in ((1, tilde[0:2]), (2, tilde[2:4]), (0, tilde[4:6])):
-            t1, t2 = taps[3 * k + 1 : 3 * k + 2, :], taps[3 * k + 2 : 3 * k + 3, :]
+            t1, t2 = taps[k, 1:2, :], taps[k, 2:3, :]
             p2, p1 = before[k][0:1], before[k][1:2]
             kvq.append(rows + jnp.where(first, t1 * p1 + t2 * p2, t2 * p1))
         out_grad = tilde[6:8]
@@ -257,7 +290,7 @@
         own = choose(j == seq, mine, own)
         nxt = choose(j == seq + 1, mine, nxt)
         rim = choose(j == seq - 1, before, rim)
-        got = pair(arrived.at[j], 0)
+        got = halves(arrived, j)
         p0, p1 = product[0:1], product[1:2]
         g0, g1 = cotangent[0:1], cotangent[1:2]
         ahead = j < seq
@@ -265,7 +298,7 @@
             got[i] + jnp.where(ahead, lam511[i] * p0 + lam510[i] * p1, lam16[i] * g1 + (g0 if i == 0 else 0.0))
             for i in range(2)
         ]
-        re, im = times(fixed, (wt[j, 0:MODES, :], wt[j, MODES : 2 * MODES, :]))
+        re, im = times(fixed, halves(pw, 8 + j))
         behind = j > seq
         s_in = (s_in[0] + jnp.where(ahead, re, 0.0), s_in[1] + jnp.where(ahead, im, 0.0))
         u_in = (u_in[0] + jnp.where(behind, re, 0.0), u_in[1] + jnp.where(behind, im, 0.0))
@@ -283,7 +316,7 @@
     inv2 = times(inv16, inv16)
     s_in = tuple(s_in[i] + inv16[i] * p0 + inv2[i] * p1 for i in range(2))
     carried = times(lam512, s_in)
-    last = pair(arrived.at[seq], 0)
+    last = halves(arrived, seq)
     last = (last[0] + carried[0], last[1] + carried[1])
     for extra in range(2):
         moved = times(lam16, last)
@@ -294,7 +327,7 @@
     gt[ROWS + 1 : ROWS + 2, :] = read_out(later)
     yt[ROWS + 2 : EXT, :] = jnp.zeros((EXT - ROWS - 2, 128), F32)
     gt[ROWS + 2 : EXT, :] = jnp.zeros((EXT - ROWS - 2, 128), F32)
-    io.need(3, 4, 5, 6, 7, 8, 9, 10)
+    io.need(4, 5, 6, 7)
 
     half = MODES // 2
     for n0 in range(0, MODES, half):
@@ -340,7 +373,9 @@
     gt[0:1, :] += read_out(none) * g0 + read_out(one) * g1
     gt[1:2, :] += read_out(none) * g1
 
-    io.need(11, 13)
+    io.need(8, 10)
+    og[0:ROWS, :] = og_far[...].T
+    og[ROWS + 2 : EXT, :] = jnp.zeros((EXT - ROWS - 2, 128), F32)
     for k in range(3):
         ext[6:8, 128 * k : 128 * k + 128] = rim[k]
     og[ROWS : ROWS + 2, :] = nxt[3]
@@ -351,7 +386,7 @@
     br[ROWS + 2 : EXT, :] = jnp.zeros((EXT - ROWS - 2, 384), F32)
     prod[...] = br[:, 128:256] * br[:, 256:384]
     gl[...] = og[...] * br[:, 0:128]
-    gain = consts[192:193, :]
+    gain = skip[...]
     long_out = yt[...] + gain * prod[...]
     gb[:, 0:128] = og[...] * long_out
     grad_prod = gt[...] + gain * gl[...]
@@ -361,7 +396,7 @@
         lanes = slice(128 * k, 128 * k + 128)
         total = None
         for j in range(3):
-            term = taps[3 * k + j : 3 * k + j + 1, :] * gb[j : j + ROWS, lanes]
+            term = taps[k, j : j + 1, :] * gb[j : j + ROWS, lanes]
             total = term if total is None else total + term
             row = 32 + 3 * k + j
             small[row : row + 1, :] = jnp.sum(
@@ -371,122 +406,160 @@
     small[41:42, :] = jnp.sum(gl[0:ROWS, :] * prod[0:ROWS, :], axis=0, keepdims=True)
     small[42:48, :] = jnp.zeros((6, 128), F32)
     wide = jnp.concatenate([small[16 * i : 16 * i + 16, :] for i in range(3)], axis=1)
-    high = wide.astype(BF16)
-    low[ROWS : ROWS + 16, :] = high
-    low[ROWS + 16 :, :] = (wide - high.astype(F32)).astype(BF16)
+    split_rows(wide, low, ROWS)
     io.done(1)
     mixed[...] = (br[0:ROWS, 0:128] * long_out[0:ROWS, :]).T
 
 
-def turn_kernel(at, a, b, *rest):
-    out, held, turned, sems = rest[-4:]
-
-    def run(src):
-        copies = copy_all([(src.at[i], held.at[i]) for i in range(8)], sems)
-        sent = []
-        for i in range(8):
-            copies[i].wait()
-            turned[i] = held[i].T
-            sent += [pltpu.make_async_copy(turned.at[i], out.at[i], sems.at[8 + i])]
-            sent[i].start()
-        wait_all(sent)
-
-    @pl.when(at[3] == 1)
-    def _():
-        run(a)
-
-    @pl.when(at[3] == 0)
-    def _():
-        run(b)
-
-
-def input_kernel(at, low, low_core, weight, partner, *rest):
-    outs, (left, lturn, right, parts, sems) = rest[:8], rest[8:]
-    core, x, y = at[0], at[4], at[5]
+def split_rows(wide, dst, row):
+    high = wide.astype(BF16)
+    dst[row : row + 16, :] = high
+    dst[row + 16 : row + 32, :] = (wide - high.astype(F32)).astype(BF16)
+
+
+def join_rows(src, row):
+    return src[row : row + 16, :].astype(F32) + src[row + 16 : row + 32, :].astype(F32)
+
+
+def input_kernel(at, low, low_core, weight, partner, out, left, lturn, right, parts, sems):
+    core = at[0]
     copies = copy_all([(low.at[0:ROWS], left.at[0]), (low_core.at[0:ROWS], left.at[1])], sems)
-    places = []
-    for r in range(8):
-        dx, dy = r // 2, r % 2
-        places.append((x + dx) % 4 * 2 + (y + dy) % 2)
-    order = [1, 2, 3, 4, 5, 6, 7, 0]
     far = []
-    for n, r in enumerate(order):
+    for n in range(8):
         for s, src in enumerate((weight, partner)):
-            c = pltpu.make_async_copy(
-                src.at[:, places[r], core], right.at[r, s], sems.at[2 + 2 * n + s]
-            )
+            c = pltpu.make_async_copy(src.at[:, n, core], right.at[n, s], sems.at[2 + 2 * n + s])
             c.start()
             far.append(c)
     wait_all(copies)
     lturn[...] = jnp.concatenate([left[0].T, left[1].T], axis=0)
     sent = []
-    for n, r in enumerate(order):
-        wait_all(far[2 * n : 2 * n + 2])
-        cols = jnp.concatenate([right[r, s, k] for s in range(2) for k in range(3)], axis=1)
-        parts[r] = jnp.dot(cols, lturn[...], preferred_element_type=F32).astype(BF16)
-        c = pltpu.make_async_copy(parts.at[r], outs[r], sems.at[18 + r])
+    for n in range(0, 8, 2):
+        wait_all(far[2 * n : 2 * n + 4])
+        cols = [
+            jnp.concatenate([right[i, s, k] for s in range(2) for k in range(3)], axis=1)
+            for i in (n, n + 1)
+        ]
+        cols = jnp.concatenate(cols, axis=0)
+        total = jnp.dot(cols, lturn[...], preferred_element_type=F32).astype(BF16)
+        for i in range(2):
+            parts[n + i] = total[256 * i : 256 * i + 256]
+            c = pltpu.make_async_copy(parts.at[n + i], out.at[n + i], sems.at[18 + n + i])
+            c.start()
+            sent.append(c)
+    wait_all(sent)
+
+
+FAR_ORDER = (4, 3, -3, 1, -1, 2, -2, 0)
+HALF = 128
+
+
+def weight_kernel(at, mine, other, given, passed, low, low_y, _, *rest):
+    outs, (held, cols, made, far_made, near_made, sems) = rest[:7], rest[7:]
+    z = at[6]
+    one, one_back, four, four_back, near, middle, own_small = outs
+    far = []
+    for n, d in enumerate(FAR_ORDER):
+        p = lax.rem(z + (d + 8), 8)
+        for s, pair in enumerate(((other, mine), (passed, given))):
+            dst = held.at[n, ROWS * s : ROWS * s + ROWS]
+            for flag, src in enumerate(pair):
+                c = pltpu.make_async_copy(src.at[p], dst, sems.at[2 + 2 * n + s])
+
+                @pl.when(at[3] == flag)
+                def _(c=c):
+                    c.start()
+
+            far.append(c)
+        if n == 0:
+            copies = copy_all([(low, cols.at[0]), (low_y, cols.at[1])], sems)
+    wait_all(copies)
+    right = jnp.concatenate([cols[0, 0:ROWS, :], cols[1, 0:ROWS, :]], axis=0)
+    wide = join_rows(cols.at[0], ROWS) + join_rows(cols.at[1], ROWS)
+    for i in range(2):
+        split_rows(wide, made.at[i], 512)
+        split_rows(wide, far_made.at[i], HALF)
+    sent = []
+
+    def send(src, dst):
+        c = pltpu.make_async_copy(src, dst, sems.at[18 + len(sent)])
         c.start()
         sent.append(c)
+
+    send(made.at[0, 512:544], own_small)
+    for n, d in enumerate(FAR_ORDER):
+        if n % 2 == 0:
+            wait_all(far[2 * n : 2 * n + 4])
+            both = jnp.concatenate([held[n], held[n + 1]], axis=1)
+            both = lax.dot_general(both, right, (((0,), (0,)), ((), ())), preferred_element_type=F32)
+        total = both[256 * (n % 2) : 256 * (n % 2) + 256]
+        if n == 0:
+            total = total.astype(BF16)
+            far_made[0, 0:HALF, :] = total[HALF:]
+            far_made[1, 0:HALF, :] = total[0:HALF]
+            send(far_made.at[0], four)
+            send(far_made.at[1], four_back)
+        elif n < 5:
+            row = 0 if n < 3 else 256
+            made[(n - 1) % 2, row : row + 256, :] = total.astype(BF16)
+            if n >= 3:
+                send(made.at[n - 3], (one, one_back)[n - 3])
+        else:
+            near_made[n - 5] = total
+            send(near_made.at[n - 5], middle if n == 7 else near.at[n - 5])
     wait_all(sent)
 
 
-def weight_kernel(at, kept, given, passed, low, low_y, *rest):
-    out, kv, pv, cols, parts, sems = rest[-6:]
-    copies = copy_all([(low, cols.at[0]), (low_y, cols.at[1])], sems)
-    far = []
-    for i in range(8):
-        c = pltpu.make_async_copy(kept.at[i], kv.at[i], sems.at[2 + 2 * i])
-        c.start()
-        far.append(c)
-        for flag, src in ((1, given), (0, passed)):
-            c = pltpu.make_async_copy(src.at[i], pv.at[i], sems.at[3 + 2 * i])
-
-            @pl.when(at[3] == flag)
-            def _(c=c):
-                c.start()
-
-        far.append(c)
-    wait_all(copies)
-    total = jnp.zeros((16, 384), F32)
-    for i in range(2):
-        for r in (ROWS, ROWS + 16):
-            total = total + cols[i, r : r + 16, :].astype(F32)
-    high = total.astype(BF16)
-    rest_low = (total - high.astype(F32)).astype(BF16)
-    sent = []
-    for i in range(8):
-        wait_all(far[2 * i : 2 * i + 2])
-        total = jnp.dot(kv[i], cols[0, 0:ROWS, :], preferred_element_type=F32)
-        total = total + lax.dot_general(
-            pv[i], cols[1, 0:ROWS, :], (((0,), (0,)), ((), ())), preferred_element_type=F32
-        )
-        parts[i, 0:256, :] = total.astype(BF16)
-        parts[i, 256:272, :] = high
-        parts[i, 272:288, :] = rest_low
-        c = pltpu.make_async_copy(parts.at[i], out.at[i], sems.at[18 + i])
-        c.start()
-        sent.append(c)
-    wait_all(sent)
-
-
-def fold_input_kernel(own, *rest):
-    parts, out = rest[:-1], rest[-1]
-    total = own[...].astype(F32)
-    for p in parts:
-        total = total + p[...].astype(F32)
+def relay_kernel(near, one, four, one_back, four_back, back, ahead, io):
+    io.need(0, 3, 4)
+    total = near[1] + one_back[0:256, :].astype(F32)
+    back[0:HALF, :] = (total[0:HALF] + four_back[0:HALF, :].astype(F32)).astype(BF16)
+    back[HALF:256, :] = total[HALF:].astype(BF16)
+    back[256:288, :] = one_back[512:544, :]
+    back[288:320, :] = four_back[HALF : HALF + 32, :]
+    io.done(0)
+    io.need(1, 2)
+    total = near[0] + one[0:256, :].astype(F32)
+    ahead[0:HALF, :] = total[0:HALF].astype(BF16)
+    ahead[HALF:256, :] = (total[HALF:] + four[0:HALF, :].astype(F32)).astype(BF16)
+    ahead[256:288, :] = one[512:544, :]
+
+
+def fold_input_kernel(parts, out):
+    total = parts[0].astype(F32)
+    for j in range(1, 8):
+        total = total + parts[j].astype(F32)
     out[...] = total.T
 
 
-def fold_kernel(parts, out, small):
+def early_kernel(middle, one, one_back, out):
+    out[...] = middle[...] + one[256:512, :].astype(F32) + one_back[256:512, :].astype(F32)
+
+
+def fold_kernel(
+    at, early, back, ahead, own_small, one, one_back, four, four_back, out, res, taps, skip, table, io
+):
+    z = at[6]
+    io.need(0, 1, 2)
+    total = early[...] + back[0:256, :].astype(F32) + ahead[0:256, :].astype(F32)
     for k in range(3):
-        lanes = slice(128 * k, 128 * k + 128)
-        total = parts[0, :, lanes].astype(F32)
-        for j in range(1, 8):
-            total = total + parts[j, :, lanes].astype(F32)
-        out[k] = total[0:256]
-        small[16 * k : 16 * k + 16, :] = total[256:272] + total[272:288]
-
-
+        out[k] = total[:, 128 * k : 128 * k + 128]
+    io.done(0)
+    io.need(3, 4, 5, 6, 7)
+    came = ((own_small, 0, 0), (one, 0, -1), (four, 0, -2), (ahead, 256, -3))
+    came += ((one_back, 0, 1), (four_back, 0, 2), (back, 256, 3), (back, 288, 4))
+    for src, row, d in came:
+        table[lax.rem(z + (d + 8), 8)] = join_rows(src, row)
+    wide = table[0]
+    for j in range(1, 8):
+        wide = wide + table[j]
+    res[0] = wide[:, 0:128]
+    res[1] = wide[:, 128:256]
+    for k in range(3):
+        taps[k] = wide[3 * k : 3 * k + 3, 256:384]
+    skip[...] = wide[9:10, 256:384]
+
+
+VMEM_BYTES = 64 * 1024 * 1024 - 128 * 1024
 FAR = pl.BlockSpec(memory_space=pltpu.HBM)
 SCALARS = pl.BlockSpec(memory_space=pltpu.SMEM)
 
@@ -498,7 +571,7 @@
         out_specs=out_specs,
         out_shape=[jax.ShapeDtypeStruct(s, t) for s, t in outs],
         scratch_shapes=[pltpu.VMEM(s, t) for s, t in scratch] + [pltpu.SemaphoreType.DMA((sems,))],
-        compiler_params=pltpu.CompilerParams(vmem_limit_bytes=62 * 1024 * 1024),
+        compiler_params=pltpu.CompilerParams(vmem_limit_bytes=VMEM_BYTES),
         cost_estimate=pl.CostEstimate(flops=int(us * 1.1e9), bytes_accessed=0, transcendentals=0),
     )(*args)
 
@@ -526,7 +599,7 @@
                 self.outs[i].start()
 
 
-def call(kernel, us, at, outs, scratch, *args, far=(), sems=0, late=(), staged=False):
+def call(kernel, us, at, outs, scratch, *args, far=(), sems=0, late=(), staged=False, windows=()):
     scalars = () if at is None else (at,)
     n_s, n_f, n_i, n_l, n_o = len(scalars), len(far), len(args), len(late), len(outs)
 
@@ -544,6 +617,8 @@
         def copies(pairs, base):
             return [pltpu.make_async_copy(a, b, sem.at[base + i]) for i, (a, b) in enumerate(pairs)]
 
+        for i, row in windows:
+            ins[i] = ins[i].at[row : row + 32]
         coming = copies(zip(ins, held), sems)
         for c in coming:
             c.start()
@@ -556,7 +631,10 @@
         io.done(*range(n_o))
         wait_all(io.outs)
 
-    buffers = [(a.shape, a.dtype) for a in args] + list(outs) + list(scratch)
+    shapes = [(a.shape, a.dtype) for a in args]
+    for i, _ in windows:
+        shapes[i] = ((32, args[i].shape[1]), args[i].dtype)
+    buffers = shapes + list(outs) + list(scratch)
     specs = [SCALARS] * n_s + [FAR] * (n_f + n_i + n_l)
     total = sems + n_i + n_o
     return raw_call(
@@ -567,8 +645,8 @@
 def after(x, *deps):
     return pl.pallas_call(
         lambda *_: None,
-        in_specs=[FAR] * (1 + len(deps)),
-        out_specs=FAR,
+        in_specs=[pl.BlockSpec(memory_space=pl.ANY)] * (1 + len(deps)),
+        out_specs=pl.BlockSpec(memory_space=pl.ANY),
         out_shape=jax.ShapeDtypeStruct(x.shape, x.dtype),
         input_output_aliases={0: 0},
     )(x, *deps)
@@ -602,36 +680,18 @@
     chan, seq = lax.axis_index("chan"), lax.axis_index("seq")
     core, yl = chan % 2, seq % 2
     same = (yl == core).astype(jnp.int32)
-    at = jnp.stack([core, chan, seq, same, chan // 4, chan // 2 % 2]).astype(jnp.int32)
+    at = jnp.stack([core, chan, seq, same, chan // 4, chan // 2 % 2, seq // 2]).astype(jnp.int32)
 
     mine = exchange(jnp.broadcast_to(hidden_in[None], (8, ROWS, 256)), "chan", CHIPS)
     partner = to_chan(in_weight, 0, 0, 1)
 
-    def power(count):
-        return pole_power(decay_rate, mode_angle, count)
-
-    lam = power(1.0)
-    lam8 = spread(lam)
-    rho8 = spread((residue[0], residue[1]))
-    eighth = jnp.arange(8, dtype=F32)[None, :, None] * float(SUB)
-    sub_rate, sub_angle = decay_rate[:, None, :], mode_angle[:, None, :]
-    pwb = jnp.concatenate(pole_power(sub_rate, sub_angle, eighth), axis=0)
-    pwf = jnp.concatenate(pole_power(sub_rate, sub_angle, float(7 * SUB) - eighth), axis=0)
-    lam64 = jnp.concatenate([spread(power(float(SUB * d))) for d in (1, 2, 4)], axis=0)
-    source = jnp.arange(16, dtype=jnp.int32)
-    away = jnp.abs(source - seq).astype(F32)[:, None, None] - 1.0
-    away = jnp.maximum(away, 0.0) * float(ROWS)
-    wt = jnp.concatenate(pole_power(decay_rate[None], mode_angle[None], away), axis=1)
-    consts = jnp.concatenate(
-        lam + power(-1.0) + (residue[0], residue[1]) + power(float(ROWS))
-        + power(float(ROWS - 1)) + power(float(ROWS - 2))
-        + (jnp.broadcast_to(skip_gain[None, :], (8, 128)),),
-        axis=0,
-    )
-    taps = jnp.concatenate([conv_taps.reshape(9, 128), jnp.zeros((7, 128), F32)], axis=0)
-    og = jnp.concatenate([out_grad, jnp.zeros((128, 8), F32)], axis=1).T
-
-    mine = after(mine, lam8, rho8, pwb, pwf, lam64, wt, consts, taps, og, at)
+    away = jnp.abs(jnp.arange(16, dtype=jnp.int32) - seq).astype(F32) - 1.0
+    counts = jnp.concatenate([jnp.array(COUNTS, F32), jnp.maximum(away, 0.0) * float(ROWS)])
+    pw = pole_power(decay_rate[None], mode_angle[None], counts[:, None, None])
+    pw = jnp.concatenate(pw, axis=1)
+    res = residue.reshape(2 * MODES, 128)
+
+    mine = after(mine, pw, at)
     other = to_chan(mine, 0, 0, 1)
     weight = in_weight.reshape(3, 8, 2, 256, 128)
     block, wblock = ((8, ROWS, 256), BF16), ((3, 8, 256, 128), BF16)
@@ -644,8 +704,8 @@
         8.0,
         at,
         [((528, 384), F32), ((ROWS, 128), F32), ((ROWS, 128), F32), ((64, 8, 128), F32), ((16, 48, 128), F32)],
-        [block, wblock, ((64, 128), F32)],
-        half, taps, og, lam8, pwf, pwb,
+        [block, wblock, ((64, 128), F32)] + [((32, 8, 128), F32)] * 3,
+        half, conv_taps, out_grad, pw,
         far=(other, weight),
         sems=48,
         staged=True,
@@ -656,12 +716,10 @@
         7.0,
         None,
         [((SUB, 8, 128), F32)] * 2 + [((96, 8, 128), F32)],
-        [],
-        prod, gl, st, lam8, rho8, lam64,
-    )
-    shapes = [((8, ROWS, 256), BF16), ((8, 256, ROWS), BF16)]
-    kept = far_call(turn_kernel, 3.5, at, shapes[1:], shapes, 16, mine, other, st)[0]
-    given = after(given, arrived)
+        [((32, 8, 128), F32)] * 2,
+        prod, gl, st, pw, res,
+    )
+    given = after(given, arrived, y)
     passed = lax.ppermute(given, ("seq", "chan"), joint_pairs("pass"))
     mixed_out, low = call(
         grads_kernel,
@@ -669,9 +727,9 @@
         at,
         [((128, ROWS), F32), ((ROWS + 32, 384), BF16)],
         [((EXT, 128), F32), ((EXT, 128), F32), ((EXT, 384), F32), ((EXT, 384), F32)]
-        + [((EXT, 128), F32), ((EXT, 128), F32), ((48, 128), F32)],
-        arrived, wt, consts, lam8, rho8, pwf, pwb, y, gp, sums, st, ext, taps, og,
-        late=(kept,),
+        + [((EXT, 128), F32), ((EXT, 128), F32), ((48, 128), F32), ((EXT, 128), F32)]
+        + [((32, 8, 128), F32)] * 4,
+        arrived, pw, res, skip_gain[None, :], y, gp, sums, st, ext, conv_taps, out_grad,
         staged=True,
     )
 
@@ -681,29 +739,50 @@
         input_kernel,
         6.0,
         at,
-        [((256, ROWS), BF16)] * 8,
+        [((8, 256, ROWS), BF16)],
         [((2, ROWS, 384), BF16), ((768, ROWS), BF16), ((8, 2, 3, 256, 128), BF16), ((8, 256, ROWS), BF16)],
         26,
         low, low_core, weight, partner.reshape(weight.shape),
-    )
-    grads = far_call(
+    )[0]
+    pair_rows, half_rows = ((544, 384), BF16), ((HALF + 32, 384), BF16)
+    one, one_back, four, four_back, near, middle, own_small = far_call(
         weight_kernel,
-        5.0,
+        40.0,
         at,
-        [((8, 288, 384), BF16)],
-        [((8, 256, ROWS), BF16), block, ((2, ROWS + 32, 384), BF16), ((8, 288, 384), BF16)],
-        26,
-        kept, given, passed, low, low_y, terms[0],
-    )[0]
-    terms = [terms[0]] + [to_chan(terms[r], r // 2, r % 2) for r in (2, 6, 4, 1, 3, 7, 5)]
-    grads = exchange(grads, "seq", COLUMNS)
-    input_grad = call(fold_input_kernel, 2.5, None, [((ROWS, 256), F32)], [], *terms)[0]
-    weight_grad, small = call(
-        fold_kernel, 2.5, None, [((3, 256, 128), F32), ((48, 128), F32)], [], grads
-    )
-    residue_grad = small[:32].reshape(2, MODES, 128)
-    taps_grad = small[32:41].reshape(3, 3, 128)
-    return (mixed_out, input_grad, weight_grad, taps_grad, residue_grad, small[41])
+        [pair_rows] * 2 + [half_rows] * 2
+        + [((2, 256, 384), F32), ((256, 384), F32), ((32, 384), BF16)],
+        [((8, 2 * ROWS, 256), BF16), ((2, ROWS + 32, 384), BF16), ((2, 544, 384), BF16)]
+        + [((2, HALF + 32, 384), BF16), ((3, 256, 384), F32)],
+        28,
+        mine, other, given, passed, low, low_y, terms,
+    )
+    terms = exchange(terms, "chan", CHIPS)
+    four, four_back = to_seq(four, 2), to_seq(four_back, -2)
+    one, one_back = to_seq(one, 1), to_seq(one_back, -1)
+    back, ahead = call(
+        relay_kernel,
+        2.0,
+        None,
+        [((320, 384), BF16), ((288, 384), BF16)],
+        [],
+        near, one, four, one_back, four_back,
+        staged=True,
+    )
+    back, ahead = to_seq(back, -2), to_seq(ahead, 2)
+    input_grad = call(fold_input_kernel, 2.5, None, [((ROWS, 256), F32)], [], terms)[0]
+    early = call(early_kernel, 2.0, None, [((256, 384), F32)], [], middle, one, one_back)[0]
+    weight_grad, residue_grad, taps_grad, skip_grad = call(
+        fold_kernel,
+        2.5,
+        at,
+        [((3, 256, 128), F32), ((2, MODES, 128), F32), ((3, 3, 128), F32), ((1, 128), F32)],
+        [((8, 16, 384), F32)],
+        early, back, ahead, own_small, one, one_back, four, four_back,
+        windows=((4, 512), (5, 512), (6, HALF), (7, HALF)),
+        late=(input_grad,),
+        staged=True,
+    )
+    return (mixed_out, input_grad, weight_grad, taps_grad, residue_grad, skip_grad.reshape(128))
 
 
 def solution(mesh):

time: 177 us -> 153 us (0.86)
  waiting for transfers between devices: 67.1 us -> 50.3 us
  local copies, waits for them, and re-layouts: 14.9 us -> 4.43 us
  starting transfers between devices: 38.2 us -> 43.6 us
  other arithmetic: 5.32 us -> 2.39 us
    ppermute x10 -> x3, waiting for transfers between devices: 20.4 us -> 0.69 us  [to_chan(): return lax.ppermute(x, 'chan', chan_pairs(dx, dy, dc))]
    ppermute x1 -> x7, starting transfers between devices: 1.03 us -> 11.9 us  [to_seq(): return lax.ppermute(x, 'seq', seq_pairs(dz, dy))]
    ppermute x1 -> x7, waiting for transfers between devices: 3.06 us -> 13.5 us  [to_seq(): return lax.ppermute(x, 'seq', seq_pairs(dz, dy))]
    all_to_all x3, waiting for transfers between devices: 43.6 us -> 36.1 us  [exchange(): lax.all_to_all(x, axis, split_axis=0, concat_axis=0, tiled=True, axis_ind...]
    ppermute x10 -> x3, starting transfers between devices: 11.5 us -> 5.23 us  [to_chan(): return lax.ppermute(x, 'chan', chan_pairs(dx, dy, dc))]
    unnamed x53 -> x8, local copies, waits for them, and re-layouts: 5.19 us -> 1.36 us
    slice x2 -> x0, local copies, waits for them, and re-layouts: 2.02 us -> none  [the longest x1 1.32 us: on_device(): residue_grad = small[:32].reshape(2, MODES, 128)]
    pallas_call x9 -> x10, Pallas kernels: 49.5 us -> 49.3 us  [raw_call(): pl.pallas_call(kernel, in_specs=in_specs, out_specs=out_specs, out_shape=...]
  transfers between devices with their start and end apart: 16 -> 15, of which waited for: 8 -> 7; matrix products, arithmetic and copies ran while one was open for 4% -> 2% of each run, Pallas kernels for 23% -> 31%
where the time goes in v2:
time: 153 us; the launch traced here: 151 us
  waiting for transfers between devices  50.3 us (33%)
  Pallas kernels  49.3 us (32%)
  starting transfers between devices  43.6 us (28%)
  local copies, waits for them, and re-layouts  4.43 us (3%)
  other arithmetic  2.39 us (2%)
    pallas_call x10, Pallas kernels, raw_call(): pl.pallas_call(kernel, in_specs=in_specs, out_specs=out_specs, out_shape=...  49.3 us
    all_to_all x3, waiting for transfers between devices, exchange(): lax.all_to_all(x, axis, split_axis=0, concat_axis=0, tiled=True, axis_ind...  36.1 us
    all_to_all x3, starting transfers between devices, exchange(): lax.all_to_all(x, axis, split_axis=0, concat_axis=0, tiled=True, axis_ind...  21.6 us
    ppermute x7, waiting for transfers between devices, to_seq(): return lax.ppermute(x, 'seq', seq_pairs(dz, dy))  13.5 us
    ppermute x7, starting transfers between devices, to_seq(): return lax.ppermute(x, 'seq', seq_pairs(dz, dy))  11.9 us
    ppermute x3, starting transfers between devices, to_chan(): return lax.ppermute(x, 'chan', chan_pairs(dx, dy, dc))  5.23 us
    ppermute x1, starting transfers between devices, on_device(): given = lax.ppermute(mine, ('seq', 'chan'), joint_pairs('give'))  3.66 us
  transfers between devices with their start and end apart: 15, of which 7 were waited for; matrix products, arithmetic and copies ran while one was open for 2% of the time, Pallas kernels for 31%

profile of v2, /device:TPU:1, one launch (start us, length us, event | category | flops | bytes accessed | tf_op | source)
XLA Modules:
  0.0 151.1 jit_solution(11357375943868276292)
XLA Ops:
  0.6 2.4 %broadcast_in_dim.4 = bf16[8,512,256]{2,1,0:T(8,128)(2,1)} broadcast(bf16[512,256]{1,0:T(8,128)(2,1)} %param.9), dimensions={1,2} | broadcast | bytes 2359296 | tf_op jit(solution)/shard_map/broadcast_in_dim | solution.py:685
  3.1 7.6 %all-to-all-start = ((bf16[8,512,256]{2,1,0:T(8,128)(2,1)}), bf16[8,512,256]{2,1,0:T(8,128)(2,1)S(1)}, u32[]{:S(2)}, u32[]{:S(2)}) async-start(bf16[8,512,256]{2,1,0:T(8,128)(2,1)} %broadcast_in_dim.4), calls=%async_computation | async-start | bytes 4194304 | tf_op jit(solution)/shard_map/all_to_all | solution.py:660
  11.4 1.5 fusion.5
  13.0 0.8 pad_maximum_fusion.__1_.refs_6_.refs_3_.refs_2_
  13.8 27.4 %all-to-all-done.__0_ = bf16[8,512,256]{2,1,0:T(8,128)(2,1)S(1)} async-done(((bf16[8,512,256]{2,1,0:T(8,128)(2,1)}), bf16[8,512,256]{2,1,0:T(8,128)(2,1)S(1)}, u32[]{:S(2)}, u32[]{:S(2)}) %all-to-all-start) | async-done | bytes 2097184 | tf_op jit(solution)/shard_map/all_to_all | solution.py:660
  41.2 1.4 copy-done
  42.5 1.6 %collective-permute-start = (bf16[8,512,256]{2,1,0:T(8,128)(2,1)}, bf16[8,512,256]{2,1,0:T(8,128)(2,1)}, u32[]{:S(2)}, u32[]{:S(2)}) collective-permute-start(bf16[8,512,256]{2,1,0:T(8,128)(2,1)} %shard_map.136.mine_far.mine), channel_id=1, source_target_pairs={{0,1},{1,0},{2,3},{3,2},{4,5},{5,4},{6,7},{7,6},{8,9},{9,8},{10,11... | collective-permute-start | bytes 6291464 | tf_op jit(solution)/shard_map/ppermute | solution.py:29
  44.2 3.7 %collective-permute-start.3 = (bf16[8,512,256]{2,1,0:T(8,128)(2,1)}, bf16[8,512,256]{2,1,0:T(8,128)(2,1)}, u32[]{:S(2)}, u32[]{:S(2)}) collective-permute-start(bf16[8,512,256]{2,1,0:T(8,128)(2,1)} %shard_map.136.mine_far.mine), channel_id=1, source_target_pairs={{1,17},{3,19},{5,21},{7,23},{9,25},{11,27},{13,29},{15,31},{16,0},... | collective-permute-start | bytes 6291464 | tf_op jit(solution)/shard_map/ppermute | solution.py:701
  47.8 4.7 %shard_map.137.refs_3_ = f32[512,384]{1,0:T(8,128)} custom-call(s32[7]{0:T(128)} %stack.35.__2_.at.refs_0_, bf16[8,512,256]{2,1,0:T(8,128)(2,1)} %shard_map.136.mine_far.mine, bf16[3,8,2,256,128]{4,3,2,1,0:T(8,128)(2,1)} %bitcast.12), custom_call_target="tpu_custom_call" | custom-call | flops 4400000000 | tf_op jit(solution)/shard_map/pallas_call | solution.py:568
  52.5 8.0 %shard_map.138 = (f32[528,384]{1,0:T(8,128)}, f32[512,128]{1,0:T(8,128)}, f32[512,128]{1,0:T(8,128)}, f32[64,8,128]{2,1,0:T(8,128)}, f32[16,48,128]{2,1,0:T(8,128)}) custom-call(s32[7]{0:T(128)} %stack.35.__2_.at.refs_0_, bf16[8,512,256]{2,1,0:T(8,128)(2,1)} %collective-permute-done.refs_1_.other, bf16[3,8,2,256,128]{4,3,2,1,0:T(8,128)(2,1)} %bitcast.13, ...), custom_call_target="tpu_custom_call" | custom-call | flops 8800000000 | tf_op jit(solution)/shard_map/pallas_call | solution.py:568
  60.6 9.4 %all-to-all-start.1 = ((f32[16,48,128]{2,1,0:T(8,128)}), f32[16,48,128]{2,1,0:T(8,128)}, u32[]{:S(2)}, u32[]{:S(2)}) async-start(f32[16,48,128]{2,1,0:T(8,128)} %get-tuple-element.29), calls=%async_computation.1 | async-start | bytes 786432 | tf_op jit(solution)/shard_map/all_to_all | solution.py:660
  70.0 7.3 %shard_map.139 = (f32[64,8,128]{2,1,0:T(8,128)}, f32[64,8,128]{2,1,0:T(8,128)}, f32[96,8,128]{2,1,0:T(8,128)}) custom-call(f32[512,128]{1,0:T(8,128)} %get-tuple-element.30.refs_0_, f32[512,128]{1,0:T(8,128)} %get-tuple-element.31.refs_1_, f32[64,8,128]{2,1,0:T(8,128)} %get-tuple-element.32.refs_2_.refs_8_, ...), custom_call_target="tpu_custom_call" | custom-call | flops 7699999744 | tf_op jit(solution)/shard_map/pallas_call | solution.py:568
  77.3 6.7 %all-to-all-done.1.refs_1_.__1_ = f32[16,48,128]{2,1,0:T(8,128)} async-done(((f32[16,48,128]{2,1,0:T(8,128)}), f32[16,48,128]{2,1,0:T(8,128)}, u32[]{:S(2)}, u32[]{:S(2)}) %all-to-all-start.1) | async-done | bytes 393248 | tf_op jit(solution)/shard_map/all_to_all | solution.py:660
  83.9 1.3 collective-permute-start.4
  85.2 8.0 %shard_map.140 = (f32[128,512]{1,0:T(8,128)}, bf16[544,384]{1,0:T(8,128)(2,1)}) custom-call(s32[7]{0:T(128)} %stack.35.__2_.at.refs_0_, f32[16,48,128]{2,1,0:T(8,128)} %all-to-all-done.1.refs_1_.__1_, f32[24,32,128]{2,1,0:T(8,128)} %pad_maximum_fusion.__1_.refs_6_.refs_3_.refs_2_, f32[32,128]{1,0:T(8,128)} %bitcast.16, f32[1,128]{1,0:T(1,128)} %bitcast.17, ...), custom_call_target="tpu_custom_call" | custom-call | flops 8800000000 | tf_op jit(solution)/shard_map/pallas_call | solution.py:568
  93.2 3.6 %collective-permute-start.1 = (bf16[544,384]{1,0:T(8,128)(2,1)}, bf16[544,384]{1,0:T(8,128)(2,1)}, u32[]{:S(2)}, u32[]{:S(2)}) collective-permute-start(bf16[544,384]{1,0:T(8,128)(2,1)} %get-tuple-element.38.low), channel_id=1, source_target_pairs={{0,1},{1,0},{2,3},{3,2},{4,5},{5,4},{6,7},{7,6},{8,9},{9,8},{10,11... | collective-permute-start | bytes 1253384 | tf_op jit(solution)/shard_map/ppermute | solution.py:29
  96.8 1.0 collective-permute-start.5
  97.9 0.7 collective-permute-done.1.low_core
  98.6 5.4 %shard_map.141._ = bf16[8,256,512]{2,1,0:T(8,128)(2,1)} custom-call(s32[7]{0:T(128)} %stack.35.__2_.at.refs_0_, bf16[544,384]{1,0:T(8,128)(2,1)} %get-tuple-element.38.low, bf16[544,384]{1,0:T(8,128)(2,1)} %collective-permute-done.1.low_core, bf16[3,8,2,256,128]{4,3,2,1,0:T(8,128)(2,1)} %bitcast.14, bf16[3,8,2,256,128]{4,3,2,1,0:T(8,128)(2,1)} %bitcast.10.partner), custom_call_target="tpu_custom_call" | custom-call | flops 6600000000 | tf_op jit(solution)/shard_map/pallas_call | solution.py:568
  103.9 4.6 %all-to-all-start.2 = ((bf16[8,256,512]{2,1,0:T(8,128)(2,1)}), bf16[8,256,512]{2,1,0:T(8,128)(2,1)}, u32[]{:S(2)}, u32[]{:S(2)}) async-start(bf16[8,256,512]{2,1,0:T(8,128)(2,1)} %shard_map.141._), calls=%async_computation.2 | async-start | bytes 4194304 | tf_op jit(solution)/shard_map/all_to_all | solution.py:660
  108.5 6.1 %shard_map.144 = (bf16[544,384]{1,0:T(8,128)(2,1)}, bf16[544,384]{1,0:T(8,128)(2,1)}, bf16[160,384]{1,0:T(8,128)(2,1)}, bf16[160,384]{1,0:T(8,128)(2,1)}, f32[2,...) custom-call(s32[7]{0:T(128)} %stack.35.__2_.at.refs_0_, ...), custom_call_target="tpu_custom_call" | custom-call | flops 44000002048 | tf_op jit(solution)/shard_map/pallas_call | solution.py:568
  114.7 2.7 %collective-permute-start.7 = (bf16[544,384]{1,0:T(8,128)(2,1)}, bf16[544,384]{1,0:T(8,128)(2,1)}, u32[]{:S(2)}, u32[]{:S(2)}) collective-permute-start(bf16[544,384]{1,0:T(8,128)(2,1)} %get-tuple-element.41), channel_id=1, source_target_pairs={{0,224},{16,240},{32,0},{48,16},{64,32},{80,48},{96,64},{112,80},{... | collective-permute-start | bytes 1253384 | tf_op jit(solution)/shard_map/ppermute | solution.py:33
  117.4 3.6 %collective-permute-start.9 = (bf16[160,384]{1,0:T(8,128)(2,1)}, bf16[160,384]{1,0:T(8,128)(2,1)}, u32[]{:S(2)}, u32[]{:S(2)}) collective-permute-start(bf16[160,384]{1,0:T(8,128)(2,1)} %get-tuple-element.44), channel_id=1, source_target_pairs={{0,192},{16,208},{32,224},{48,240},{64,0},{80,16},{96,32},{112,48}... | collective-permute-start | bytes 368648 | tf_op jit(solution)/shard_map/ppermute | solution.py:33
  121.0 7.1 %collective-permute-done.8.refs_2_.refs_7_ = bf16[160,384]{1,0:T(8,128)(2,1)} collective-permute-done((bf16[160,384]{1,0:T(8,128)(2,1)}, bf16[160,384]{1,0:T(8,128)(2,1)}, u32[]{:S(2)}, u32[]{:S(2)}) %collective-permute-start.8) | collective-permute-done | bytes 122912 | tf_op jit(solution)/shard_map/ppermute | solution.py:33
  128.1 2.7 %collective-permute-done.9.refs_4_.refs_8_ = bf16[160,384]{1,0:T(8,128)(2,1)} collective-permute-done((bf16[160,384]{1,0:T(8,128)(2,1)}, bf16[160,384]{1,0:T(8,128)(2,1)}, u32[]{:S(2)}, u32[]{:S(2)}) %collective-permute-start.9) | collective-permute-done | bytes 122912 | tf_op jit(solution)/shard_map/ppermute | solution.py:33
  130.8 2.3 %shard_map.146 = (bf16[320,384]{1,0:T(8,128)(2,1)}, bf16[288,384]{1,0:T(8,128)(2,1)}) custom-call(f32[2,256,384]{2,1,0:T(8,128)} %get-tuple-element.42.refs_0_, bf16[544,384]{1,0:T(8,128)(2,1)} %collective-permute-done.6.refs_1_.refs_5_, bf16[160,384]{1,0:T(8,128)(2,1)} %collective-permute-done.8.refs_2_.refs_7_, ...), custom_call_target="tpu_custom_call" | custom-call | flops 2200000000 | tf_op jit(solution)/shard_map/pallas_call | solution.py:568
  133.1 4.5 %collective-permute-start.10 = (bf16[320,384]{1,0:T(8,128)(2,1)}, bf16[320,384]{1,0:T(8,128)(2,1)}, u32[]{:S(2)}, u32[]{:S(2)}) collective-permute-start(bf16[320,384]{1,0:T(8,128)(2,1)} %get-tuple-element.45), channel_id=1, source_target_pairs={{0,192},{16,208},{32,224},{48,240},{64,0},{80,16},{96,32},{112,48}... | collective-permute-start | bytes 737288 | tf_op jit(solution)/shard_map/ppermute | solution.py:33
  137.6 2.1 %all-to-all-done.2.refs_0_ = bf16[8,256,512]{2,1,0:T(8,128)(2,1)} async-done(((bf16[8,256,512]{2,1,0:T(8,128)(2,1)}), bf16[8,256,512]{2,1,0:T(8,128)(2,1)}, u32[]{:S(2)}, u32[]{:S(2)}) %all-to-all-start.2) | async-done | bytes 2097184 | tf_op jit(solution)/shard_map/all_to_all | solution.py:660
  139.7 2.7 %shard_map.142.refs_9_ = f32[512,256]{1,0:T(8,128)} custom-call(bf16[8,256,512]{2,1,0:T(8,128)(2,1)} %all-to-all-done.2.refs_0_), custom_call_target="tpu_custom_call" | custom-call | flops 2750000128 | tf_op jit(solution)/shard_map/pallas_call | solution.py:568
  142.4 2.1 %shard_map.145.refs_1_ = f32[256,384]{1,0:T(8,128)} custom-call(f32[256,384]{1,0:T(8,128)} %get-tuple-element.39.refs_0_, bf16[544,384]{1,0:T(8,128)(2,1)} %collective-permute-done.6.refs_1_.refs_5_, bf16[544,384]{1,0:T(8,128)(2,1)} %collective-permute-done.7.refs_2_.refs_3_.refs_6_), custom_call_target="tpu_custom_call" | custom-call | flops 2200000000 | tf_op jit(solution)/shard_map/pallas_call | solution.py:568
  144.5 3.6 %collective-permute-done.11.refs_3_ = bf16[288,384]{1,0:T(8,128)(2,1)} collective-permute-done((bf16[288,384]{1,0:T(8,128)(2,1)}, bf16[288,384]{1,0:T(8,128)(2,1)}, u32[]{:S(2)}, u32[]{:S(2)}) %collective-permute-start.11) | collective-permute-done | bytes 221216 | tf_op jit(solution)/shard_map/ppermute | solution.py:33
  148.2 2.7 %shard_map.147 = (f32[3,256,128]{2,1,0:T(8,128)}, f32[2,16,128]{2,1,0:T(8,128)}, f32[3,3,128]{2,1,0:T(4,128)}, f32[1,128]{1,0:T(1,128)}) custom-call(s32[7]{0:T(128)} %stack.35.__2_.at.refs_0_, f32[256,384]{1,0:T(8,128)} %shard_map.145.refs_1_, bf16[320,384]{1,0:T(8,128)(2,1)} %collective-permute-done.10.refs_2_, ...), custom_call_target="tpu_custom_call" | custom-call | flops 2750000128 | tf_op jit(solution)/shard_map/pallas_call | solution.py:568
  (26 shorter events, 0.8 us)
Async XLA Ops:
  3.1 7.6 %copy-start.2 = (f32[16,128]{1,0:T(8,128)S(1)}, f32[16,128]{1,0:T(8,128)}, u32[]{:S(2)}) copy-start(f32[16,128]{1,0:T(8,128)} %param.12) | copy-start | bytes 24580
  3.1 8.3 %copy-start.3 = (f32[8]{0:T(128)S(1)}, f32[8]{0:T(128)}, u32[]{:S(2)}) copy-start(f32[8]{0:T(128)} %constant.69.clone) | copy-start | bytes 100
  3.1 8.4 %copy-start.1 = (f32[16,128]{1,0:T(8,128)S(1)}, f32[16,128]{1,0:T(8,128)}, u32[]{:S(2)}) copy-start(f32[16,128]{1,0:T(8,128)} %param.13) | copy-start | bytes 24580
  3.1 38.1 %all-to-all-start = ((bf16[8,512,256]{2,1,0:T(8,128)(2,1)}), bf16[8,512,256]{2,1,0:T(8,128)(2,1)S(1)}, u32[]{:S(2)}, u32[]{:S(2)}) async-start(bf16[8,512,256]{2,1,0:T(8,128)(2,1)} %broadcast_in_dim.4), calls=%async_computation | async-start | bytes 4194304 | tf_op jit(solution)/shard_map/all_to_all | solution.py:660
  41.2 1.4 copy-start
  42.5 10.0 %collective-permute-start = (bf16[8,512,256]{2,1,0:T(8,128)(2,1)}, bf16[8,512,256]{2,1,0:T(8,128)(2,1)}, u32[]{:S(2)}, u32[]{:S(2)}) collective-permute-start(bf16[8,512,256]{2,1,0:T(8,128)(2,1)} %shard_map.136.mine_far.mine), channel_id=1, source_target_pairs={{0,1},{1,0},{2,3},{3,2},{4,5},{5,4},{6,7},{7,6},{8,9},{9,8},{10,11... | collective-permute-start | bytes 6291464 | tf_op jit(solution)/shard_map/ppermute | solution.py:29
  44.2 33.1 %collective-permute-start.3 = (bf16[8,512,256]{2,1,0:T(8,128)(2,1)}, bf16[8,512,256]{2,1,0:T(8,128)(2,1)}, u32[]{:S(2)}, u32[]{:S(2)}) collective-permute-start(bf16[8,512,256]{2,1,0:T(8,128)(2,1)} %shard_map.136.mine_far.mine), channel_id=1, source_target_pairs={{1,17},{3,19},{5,21},{7,23},{9,25},{11,27},{13,29},{15,31},{16,0},... | collective-permute-start | bytes 6291464 | tf_op jit(solution)/shard_map/ppermute | solution.py:701
  47.8 50.1 %collective-permute-start.2 = (bf16[3,4096,128]{2,1,0:T(8,128)(2,1)}, bf16[3,4096,128]{2,1,0:T(8,128)(2,1)}, u32[]{:S(2)}, u32[]{:S(2)}) collective-permute-start(bf16[3,4096,128]{2,1,0:T(8,128)(2,1)} %param.10), channel_id=1, source_target_pairs={{0,1},{1,0},{2,3},{3,2},{4,5},{5,4},{6,7},{7,6},{8,9},{9,8},{10,11... | collective-permute-start | bytes 9437192 | tf_op jit(solution)/shard_map/ppermute | solution.py:29
  60.6 23.4 %all-to-all-start.1 = ((f32[16,48,128]{2,1,0:T(8,128)}), f32[16,48,128]{2,1,0:T(8,128)}, u32[]{:S(2)}, u32[]{:S(2)}) async-start(f32[16,48,128]{2,1,0:T(8,128)} %get-tuple-element.29), calls=%async_computation.1 | async-start | bytes 786432 | tf_op jit(solution)/shard_map/all_to_all | solution.py:660
  83.9 24.6 %collective-permute-start.4 = (bf16[8,512,256]{2,1,0:T(8,128)(2,1)}, bf16[8,512,256]{2,1,0:T(8,128)(2,1)}, u32[]{:S(2)}, u32[]{:S(2)}) collective-permute-start(bf16[8,512,256]{2,1,0:T(8,128)(2,1)} %shard_map.143.given), channel_id=1, source_target_pairs={{0,1},{2,3},{4,5},{6,7},{8,9},{10,11},{12,13},{14,15},{17,16},{19,... | collective-permute-start | bytes 6291464 | tf_op jit(solution)/shard_map/ppermute | solution.py:723
  93.2 5.3 %collective-permute-start.1 = (bf16[544,384]{1,0:T(8,128)(2,1)}, bf16[544,384]{1,0:T(8,128)(2,1)}, u32[]{:S(2)}, u32[]{:S(2)}) collective-permute-start(bf16[544,384]{1,0:T(8,128)(2,1)} %get-tuple-element.38.low), channel_id=1, source_target_pairs={{0,1},{1,0},{2,3},{3,2},{4,5},{5,4},{6,7},{7,6},{8,9},{9,8},{10,11... | collective-permute-start | bytes 1253384 | tf_op jit(solution)/shard_map/ppermute | solution.py:29
  96.8 11.7 %collective-permute-start.5 = (bf16[544,384]{1,0:T(8,128)(2,1)}, bf16[544,384]{1,0:T(8,128)(2,1)}, u32[]{:S(2)}, u32[]{:S(2)}) collective-permute-start(bf16[544,384]{1,0:T(8,128)(2,1)} %get-tuple-element.38.low), channel_id=1, source_target_pairs={{0,16},{16,0},{32,48},{48,32},{64,80},{80,64},{96,112},{112,96},{1... | collective-permute-start | bytes 1253384 | tf_op jit(solution)/shard_map/ppermute | solution.py:33
  103.9 35.8 %all-to-all-start.2 = ((bf16[8,256,512]{2,1,0:T(8,128)(2,1)}), bf16[8,256,512]{2,1,0:T(8,128)(2,1)}, u32[]{:S(2)}, u32[]{:S(2)}) async-start(bf16[8,256,512]{2,1,0:T(8,128)(2,1)} %shard_map.141._), calls=%async_computation.2 | async-start | bytes 4194304 | tf_op jit(solution)/shard_map/all_to_all | solution.py:660
  114.6 16.1 %collective-permute-start.6 = (bf16[544,384]{1,0:T(8,128)(2,1)}, bf16[544,384]{1,0:T(8,128)(2,1)}, u32[]{:S(2)}, u32[]{:S(2)}) collective-permute-start(bf16[544,384]{1,0:T(8,128)(2,1)} %get-tuple-element.40), channel_id=1, source_target_pairs={{0,32},{16,48},{32,64},{48,80},{64,96},{80,112},{96,128},{112,144}... | collective-permute-start | bytes 1253384 | tf_op jit(solution)/shard_map/ppermute | solution.py:33
  114.7 16.1 %collective-permute-start.7 = (bf16[544,384]{1,0:T(8,128)(2,1)}, bf16[544,384]{1,0:T(8,128)(2,1)}, u32[]{:S(2)}, u32[]{:S(2)}) collective-permute-start(bf16[544,384]{1,0:T(8,128)(2,1)} %get-tuple-element.41), channel_id=1, source_target_pairs={{0,224},{16,240},{32,0},{48,16},{64,32},{80,48},{96,64},{112,80},{... | collective-permute-start | bytes 1253384 | tf_op jit(solution)/shard_map/ppermute | solution.py:33
  117.4 10.7 %collective-permute-start.8 = (bf16[160,384]{1,0:T(8,128)(2,1)}, bf16[160,384]{1,0:T(8,128)(2,1)}, u32[]{:S(2)}, u32[]{:S(2)}) collective-permute-start(bf16[160,384]{1,0:T(8,128)(2,1)} %get-tuple-element.43), channel_id=1, source_target_pairs={{0,64},{16,80},{32,96},{48,112},{64,128},{80,144},{96,160},{112,17... | collective-permute-start | bytes 368648 | tf_op jit(solution)/shard_map/ppermute | solution.py:33
  117.4 13.4 %collective-permute-start.9 = (bf16[160,384]{1,0:T(8,128)(2,1)}, bf16[160,384]{1,0:T(8,128)(2,1)}, u32[]{:S(2)}, u32[]{:S(2)}) collective-permute-start(bf16[160,384]{1,0:T(8,128)(2,1)} %get-tuple-element.44), channel_id=1, source_target_pairs={{0,192},{16,208},{32,224},{48,240},{64,0},{80,16},{96,32},{112,48}... | collective-permute-start | bytes 368648 | tf_op jit(solution)/shard_map/ppermute | solution.py:33
  133.1 15.1 %collective-permute-start.10 = (bf16[320,384]{1,0:T(8,128)(2,1)}, bf16[320,384]{1,0:T(8,128)(2,1)}, u32[]{:S(2)}, u32[]{:S(2)}) collective-permute-start(bf16[320,384]{1,0:T(8,128)(2,1)} %get-tuple-element.45), channel_id=1, source_target_pairs={{0,192},{16,208},{32,224},{48,240},{64,0},{80,16},{96,32},{112,48}... | collective-permute-start | bytes 737288 | tf_op jit(solution)/shard_map/ppermute | solution.py:33
  137.6 10.6 %collective-permute-start.11 = (bf16[288,384]{1,0:T(8,128)(2,1)}, bf16[288,384]{1,0:T(8,128)(2,1)}, u32[]{:S(2)}, u32[]{:S(2)}) collective-permute-start(bf16[288,384]{1,0:T(8,128)(2,1)} %get-tuple-element.46), channel_id=1, source_target_pairs={{0,64},{16,80},{32,96},{48,112},{64,128},{80,144},{96,160},{112,17... | collective-permute-start | bytes 663560 | tf_op jit(solution)/shard_map/ppermute | solution.py:33

commit v3 on v2

--- a/solution.py
+++ b/solution.py
@@ -11,6 +11,7 @@
 SUB = 64
 ROWS = 8 * SUB
 EXT = ROWS + 8
+SPAN = ROWS + SUB
 
 
 def chan_pairs(dx, dy, dc):
@@ -149,9 +150,9 @@
     io.need(1, 2)
     q, k, v = (convolve(taps, ext, i) for i in range(3))
     fresh = lax.broadcasted_iota(jnp.int32, (ROWS, 128), 0) >= 2
-    prod[...] = jnp.where(fresh, k * v, 0.0)
+    prod[0:ROWS, :] = jnp.where(fresh, k * v, 0.0)
     cot = og[...].T
-    gl[...] = jnp.where(fresh, cot * q, 0.0)
+    gl[0:ROWS, :] = jnp.where(fresh, cot * q, 0.0)
     io.done(1, 2)
     edge = [k[0:2], v[0:2], q[0:2], cot[0:2]]
     edge += [ext[518:520, 128 * i : 128 * i + 128] for i in range(3)]
@@ -387,9 +388,9 @@
     prod[...] = br[:, 128:256] * br[:, 256:384]
     gl[...] = og[...] * br[:, 0:128]
     gain = skip[...]
-    long_out = yt[...] + gain * prod[...]
+    long_out = yt[0:EXT, :] + gain * prod[...]
     gb[:, 0:128] = og[...] * long_out
-    grad_prod = gt[...] + gain * gl[...]
+    grad_prod = gt[0:EXT, :] + gain * gl[...]
     gb[:, 128:256] = grad_prod * br[:, 256:384]
     gb[:, 256:384] = grad_prod * br[:, 128:256]
     for k in range(3):
@@ -703,7 +704,7 @@
         states_kernel,
         8.0,
         at,
-        [((528, 384), F32), ((ROWS, 128), F32), ((ROWS, 128), F32), ((64, 8, 128), F32), ((16, 48, 128), F32)],
+        [((528, 384), F32), ((SPAN, 128), F32), ((SPAN, 128), F32), ((64, 8, 128), F32), ((16, 48, 128), F32)],
         [block, wblock, ((64, 128), F32)] + [((32, 8, 128), F32)] * 3,
         half, conv_taps, out_grad, pw,
         far=(other, weight),
@@ -726,7 +727,7 @@
         8.0,
         at,
         [((128, ROWS), F32), ((ROWS + 32, 384), BF16)],
-        [((EXT, 128), F32), ((EXT, 128), F32), ((EXT, 384), F32), ((EXT, 384), F32)]
+        [((SPAN, 128), F32), ((SPAN, 128), F32), ((EXT, 384), F32), ((EXT, 384), F32)]
         + [((EXT, 128), F32), ((EXT, 128), F32), ((48, 128), F32), ((EXT, 128), F32)]
         + [((32, 8, 128), F32)] * 4,
         arrived, pw, res, skip_gain[None, :], y, gp, sums, st, ext, conv_taps, out_grad,

time: 153 us -> 153 us (level)
  no operation moved by 1% of the time
where the time goes in v3:
time: 153 us; the launch traced here: 151 us
  waiting for transfers between devices  50.3 us (33%)
  Pallas kernels  49.4 us (32%)
  starting transfers between devices  43.6 us (28%)
  local copies, waits for them, and re-layouts  4.43 us (3%)
  other arithmetic  2.39 us (2%)
    pallas_call x10, Pallas kernels, raw_call(): pl.pallas_call(kernel, in_specs=in_specs, out_specs=out_specs, out_shape=...  49.4 us
    all_to_all x3, waiting for transfers between devices, exchange(): lax.all_to_all(x, axis, split_axis=0, concat_axis=0, tiled=True, axis_ind...  36.1 us
    all_to_all x3, starting transfers between devices, exchange(): lax.all_to_all(x, axis, split_axis=0, concat_axis=0, tiled=True, axis_ind...  21.6 us
    ppermute x7, waiting for transfers between devices, to_seq(): return lax.ppermute(x, 'seq', seq_pairs(dz, dy))  13.5 us
    ppermute x7, starting transfers between devices, to_seq(): return lax.ppermute(x, 'seq', seq_pairs(dz, dy))  11.9 us
    ppermute x3, starting transfers between devices, to_chan(): return lax.ppermute(x, 'chan', chan_pairs(dx, dy, dc))  5.23 us
    ppermute x1, starting transfers between devices, on_device(): given = lax.ppermute(mine, ('seq', 'chan'), joint_pairs('give'))  3.66 us
  transfers between devices with their start and end apart: 15, of which 7 were waited for; matrix products, arithmetic and copies ran while one was open for 2% of the time, Pallas kernels for 31%

profile of v3, /device:TPU:1, one launch (start us, length us, event | category | flops | bytes accessed | tf_op | source)
XLA Modules:
  0.0 151.1 jit_solution(11569905112829340141)
XLA Ops:
  0.6 2.4 %broadcast_in_dim.4 = bf16[8,512,256]{2,1,0:T(8,128)(2,1)} broadcast(bf16[512,256]{1,0:T(8,128)(2,1)} %param.9), dimensions={1,2} | broadcast | bytes 2359296 | tf_op jit(solution)/shard_map/broadcast_in_dim | solution.py:686
  3.1 7.6 %all-to-all-start = ((bf16[8,512,256]{2,1,0:T(8,128)(2,1)}), bf16[8,512,256]{2,1,0:T(8,128)(2,1)S(1)}, u32[]{:S(2)}, u32[]{:S(2)}) async-start(bf16[8,512,256]{2,1,0:T(8,128)(2,1)} %broadcast_in_dim.4), calls=%async_computation | async-start | bytes 4194304 | tf_op jit(solution)/shard_map/all_to_all | solution.py:661
  11.4 1.5 fusion.5
  13.0 0.8 pad_maximum_fusion.__1_.refs_6_.refs_3_.refs_2_
  13.8 27.4 %all-to-all-done.__0_ = bf16[8,512,256]{2,1,0:T(8,128)(2,1)S(1)} async-done(((bf16[8,512,256]{2,1,0:T(8,128)(2,1)}), bf16[8,512,256]{2,1,0:T(8,128)(2,1)S(1)}, u32[]{:S(2)}, u32[]{:S(2)}) %all-to-all-start) | async-done | bytes 2097184 | tf_op jit(solution)/shard_map/all_to_all | solution.py:661
  41.2 1.4 copy-done
  42.5 1.6 %collective-permute-start = (bf16[8,512,256]{2,1,0:T(8,128)(2,1)}, bf16[8,512,256]{2,1,0:T(8,128)(2,1)}, u32[]{:S(2)}, u32[]{:S(2)}) collective-permute-start(bf16[8,512,256]{2,1,0:T(8,128)(2,1)} %shard_map.136.mine_far.mine), channel_id=1, source_target_pairs={{0,1},{1,0},{2,3},{3,2},{4,5},{5,4},{6,7},{7,6},{8,9},{9,8},{10,11... | collective-permute-start | bytes 6291464 | tf_op jit(solution)/shard_map/ppermute | solution.py:30
  44.2 3.7 %collective-permute-start.3 = (bf16[8,512,256]{2,1,0:T(8,128)(2,1)}, bf16[8,512,256]{2,1,0:T(8,128)(2,1)}, u32[]{:S(2)}, u32[]{:S(2)}) collective-permute-start(bf16[8,512,256]{2,1,0:T(8,128)(2,1)} %shard_map.136.mine_far.mine), channel_id=1, source_target_pairs={{1,17},{3,19},{5,21},{7,23},{9,25},{11,27},{13,29},{15,31},{16,0},... | collective-permute-start | bytes 6291464 | tf_op jit(solution)/shard_map/ppermute | solution.py:702
  47.8 4.7 %shard_map.137.refs_3_ = f32[512,384]{1,0:T(8,128)} custom-call(s32[7]{0:T(128)} %stack.35.__2_.at.refs_0_, bf16[8,512,256]{2,1,0:T(8,128)(2,1)} %shard_map.136.mine_far.mine, bf16[3,8,2,256,128]{4,3,2,1,0:T(8,128)(2,1)} %bitcast.12), custom_call_target="tpu_custom_call" | custom-call | flops 4400000000 | tf_op jit(solution)/shard_map/pallas_call | solution.py:569
  52.5 8.0 %shard_map.138 = (f32[528,384]{1,0:T(8,128)}, f32[576,128]{1,0:T(8,128)}, f32[576,128]{1,0:T(8,128)}, f32[64,8,128]{2,1,0:T(8,128)}, f32[16,48,128]{2,1,0:T(8,128)}) custom-call(s32[7]{0:T(128)} %stack.35.__2_.at.refs_0_, bf16[8,512,256]{2,1,0:T(8,128)(2,1)} %collective-permute-done.refs_1_.other, bf16[3,8,2,256,128]{4,3,2,1,0:T(8,128)(2,1)} %bitcast.13, ...), custom_call_target="tpu_custom_call" | custom-call | flops 8800000000 | tf_op jit(solution)/shard_map/pallas_call | solution.py:569
  60.6 9.4 %all-to-all-start.1 = ((f32[16,48,128]{2,1,0:T(8,128)}), f32[16,48,128]{2,1,0:T(8,128)}, u32[]{:S(2)}, u32[]{:S(2)}) async-start(f32[16,48,128]{2,1,0:T(8,128)} %get-tuple-element.29), calls=%async_computation.1 | async-start | bytes 786432 | tf_op jit(solution)/shard_map/all_to_all | solution.py:661
  70.0 7.3 %shard_map.139 = (f32[64,8,128]{2,1,0:T(8,128)}, f32[64,8,128]{2,1,0:T(8,128)}, f32[96,8,128]{2,1,0:T(8,128)}) custom-call(f32[576,128]{1,0:T(8,128)} %get-tuple-element.30.refs_0_, f32[576,128]{1,0:T(8,128)} %get-tuple-element.31.refs_1_, f32[64,8,128]{2,1,0:T(8,128)} %get-tuple-element.32.refs_2_.refs_8_, ...), custom_call_target="tpu_custom_call" | custom-call | flops 7699999744 | tf_op jit(solution)/shard_map/pallas_call | solution.py:569
  77.3 6.6 %all-to-all-done.1.refs_1_.__1_ = f32[16,48,128]{2,1,0:T(8,128)} async-done(((f32[16,48,128]{2,1,0:T(8,128)}), f32[16,48,128]{2,1,0:T(8,128)}, u32[]{:S(2)}, u32[]{:S(2)}) %all-to-all-start.1) | async-done | bytes 393248 | tf_op jit(solution)/shard_map/all_to_all | solution.py:661
  83.9 1.3 collective-permute-start.4
  85.2 8.0 %shard_map.140 = (f32[128,512]{1,0:T(8,128)}, bf16[544,384]{1,0:T(8,128)(2,1)}) custom-call(s32[7]{0:T(128)} %stack.35.__2_.at.refs_0_, f32[16,48,128]{2,1,0:T(8,128)} %all-to-all-done.1.refs_1_.__1_, f32[24,32,128]{2,1,0:T(8,128)} %pad_maximum_fusion.__1_.refs_6_.refs_3_.refs_2_, f32[32,128]{1,0:T(8,128)} %bitcast.16, f32[1,128]{1,0:T(1,128)} %bitcast.17, ...), custom_call_target="tpu_custom_call" | custom-call | flops 8800000000 | tf_op jit(solution)/shard_map/pallas_call | solution.py:569
  93.2 3.6 %collective-permute-start.1 = (bf16[544,384]{1,0:T(8,128)(2,1)}, bf16[544,384]{1,0:T(8,128)(2,1)}, u32[]{:S(2)}, u32[]{:S(2)}) collective-permute-start(bf16[544,384]{1,0:T(8,128)(2,1)} %get-tuple-element.38.low), channel_id=1, source_target_pairs={{0,1},{1,0},{2,3},{3,2},{4,5},{5,4},{6,7},{7,6},{8,9},{9,8},{10,11... | collective-permute-start | bytes 1253384 | tf_op jit(solution)/shard_map/ppermute | solution.py:30
  96.9 1.0 collective-permute-start.5
  97.9 0.7 collective-permute-done.1.low_core
  98.6 5.4 %shard_map.141._ = bf16[8,256,512]{2,1,0:T(8,128)(2,1)} custom-call(s32[7]{0:T(128)} %stack.35.__2_.at.refs_0_, bf16[544,384]{1,0:T(8,128)(2,1)} %get-tuple-element.38.low, bf16[544,384]{1,0:T(8,128)(2,1)} %collective-permute-done.1.low_core, bf16[3,8,2,256,128]{4,3,2,1,0:T(8,128)(2,1)} %bitcast.14, bf16[3,8,2,256,128]{4,3,2,1,0:T(8,128)(2,1)} %bitcast.10.partner), custom_call_target="tpu_custom_call" | custom-call | flops 6600000000 | tf_op jit(solution)/shard_map/pallas_call | solution.py:569
  103.9 4.6 %all-to-all-start.2 = ((bf16[8,256,512]{2,1,0:T(8,128)(2,1)}), bf16[8,256,512]{2,1,0:T(8,128)(2,1)}, u32[]{:S(2)}, u32[]{:S(2)}) async-start(bf16[8,256,512]{2,1,0:T(8,128)(2,1)} %shard_map.141._), calls=%async_computation.2 | async-start | bytes 4194304 | tf_op jit(solution)/shard_map/all_to_all | solution.py:661
  108.5 6.1 %shard_map.144 = (bf16[544,384]{1,0:T(8,128)(2,1)}, bf16[544,384]{1,0:T(8,128)(2,1)}, bf16[160,384]{1,0:T(8,128)(2,1)}, bf16[160,384]{1,0:T(8,128)(2,1)}, f32[2,...) custom-call(s32[7]{0:T(128)} %stack.35.__2_.at.refs_0_, ...), custom_call_target="tpu_custom_call" | custom-call | flops 44000002048 | tf_op jit(solution)/shard_map/pallas_call | solution.py:569
  114.8 2.7 %collective-permute-start.7 = (bf16[544,384]{1,0:T(8,128)(2,1)}, bf16[544,384]{1,0:T(8,128)(2,1)}, u32[]{:S(2)}, u32[]{:S(2)}) collective-permute-start(bf16[544,384]{1,0:T(8,128)(2,1)} %get-tuple-element.41), channel_id=1, source_target_pairs={{0,224},{16,240},{32,0},{48,16},{64,32},{80,48},{96,64},{112,80},{... | collective-permute-start | bytes 1253384 | tf_op jit(solution)/shard_map/ppermute | solution.py:34
  117.4 3.6 %collective-permute-start.9 = (bf16[160,384]{1,0:T(8,128)(2,1)}, bf16[160,384]{1,0:T(8,128)(2,1)}, u32[]{:S(2)}, u32[]{:S(2)}) collective-permute-start(bf16[160,384]{1,0:T(8,128)(2,1)} %get-tuple-element.44), channel_id=1, source_target_pairs={{0,192},{16,208},{32,224},{48,240},{64,0},{80,16},{96,32},{112,48}... | collective-permute-start | bytes 368648 | tf_op jit(solution)/shard_map/ppermute | solution.py:34
  121.0 7.1 %collective-permute-done.8.refs_2_.refs_7_ = bf16[160,384]{1,0:T(8,128)(2,1)} collective-permute-done((bf16[160,384]{1,0:T(8,128)(2,1)}, bf16[160,384]{1,0:T(8,128)(2,1)}, u32[]{:S(2)}, u32[]{:S(2)}) %collective-permute-start.8) | collective-permute-done | bytes 122912 | tf_op jit(solution)/shard_map/ppermute | solution.py:34
  128.1 2.7 %collective-permute-done.9.refs_4_.refs_8_ = bf16[160,384]{1,0:T(8,128)(2,1)} collective-permute-done((bf16[160,384]{1,0:T(8,128)(2,1)}, bf16[160,384]{1,0:T(8,128)(2,1)}, u32[]{:S(2)}, u32[]{:S(2)}) %collective-permute-start.9) | collective-permute-done | bytes 122912 | tf_op jit(solution)/shard_map/ppermute | solution.py:34
  130.8 2.3 %shard_map.146 = (bf16[320,384]{1,0:T(8,128)(2,1)}, bf16[288,384]{1,0:T(8,128)(2,1)}) custom-call(f32[2,256,384]{2,1,0:T(8,128)} %get-tuple-element.42.refs_0_, bf16[544,384]{1,0:T(8,128)(2,1)} %collective-permute-done.6.refs_1_.refs_5_, bf16[160,384]{1,0:T(8,128)(2,1)} %collective-permute-done.8.refs_2_.refs_7_, ...), custom_call_target="tpu_custom_call" | custom-call | flops 2200000000 | tf_op jit(solution)/shard_map/pallas_call | solution.py:569
  133.1 4.5 %collective-permute-start.10 = (bf16[320,384]{1,0:T(8,128)(2,1)}, bf16[320,384]{1,0:T(8,128)(2,1)}, u32[]{:S(2)}, u32[]{:S(2)}) collective-permute-start(bf16[320,384]{1,0:T(8,128)(2,1)} %get-tuple-element.45), channel_id=1, source_target_pairs={{0,192},{16,208},{32,224},{48,240},{64,0},{80,16},{96,32},{112,48}... | collective-permute-start | bytes 737288 | tf_op jit(solution)/shard_map/ppermute | solution.py:34
  137.7 2.0 %all-to-all-done.2.refs_0_ = bf16[8,256,512]{2,1,0:T(8,128)(2,1)} async-done(((bf16[8,256,512]{2,1,0:T(8,128)(2,1)}), bf16[8,256,512]{2,1,0:T(8,128)(2,1)}, u32[]{:S(2)}, u32[]{:S(2)}) %all-to-all-start.2) | async-done | bytes 2097184 | tf_op jit(solution)/shard_map/all_to_all | solution.py:661
  139.7 2.7 %shard_map.142.refs_9_ = f32[512,256]{1,0:T(8,128)} custom-call(bf16[8,256,512]{2,1,0:T(8,128)(2,1)} %all-to-all-done.2.refs_0_), custom_call_target="tpu_custom_call" | custom-call | flops 2750000128 | tf_op jit(solution)/shard_map/pallas_call | solution.py:569
  142.4 2.1 %shard_map.145.refs_1_ = f32[256,384]{1,0:T(8,128)} custom-call(f32[256,384]{1,0:T(8,128)} %get-tuple-element.39.refs_0_, bf16[544,384]{1,0:T(8,128)(2,1)} %collective-permute-done.6.refs_1_.refs_5_, bf16[544,384]{1,0:T(8,128)(2,1)} %collective-permute-done.7.refs_2_.refs_3_.refs_6_), custom_call_target="tpu_custom_call" | custom-call | flops 2200000000 | tf_op jit(solution)/shard_map/pallas_call | solution.py:569
  144.5 3.6 %collective-permute-done.11.refs_3_ = bf16[288,384]{1,0:T(8,128)(2,1)} collective-permute-done((bf16[288,384]{1,0:T(8,128)(2,1)}, bf16[288,384]{1,0:T(8,128)(2,1)}, u32[]{:S(2)}, u32[]{:S(2)}) %collective-permute-start.11) | collective-permute-done | bytes 221216 | tf_op jit(solution)/shard_map/ppermute | solution.py:34
  148.2 2.7 %shard_map.147 = (f32[3,256,128]{2,1,0:T(8,128)}, f32[2,16,128]{2,1,0:T(8,128)}, f32[3,3,128]{2,1,0:T(4,128)}, f32[1,128]{1,0:T(1,128)}) custom-call(s32[7]{0:T(128)} %stack.35.__2_.at.refs_0_, f32[256,384]{1,0:T(8,128)} %shard_map.145.refs_1_, bf16[320,384]{1,0:T(8,128)(2,1)} %collective-permute-done.10.refs_2_, ...), custom_call_target="tpu_custom_call" | custom-call | flops 2750000128 | tf_op jit(solution)/shard_map/pallas_call | solution.py:569
  (26 shorter events, 0.9 us)
Async XLA Ops:
  3.1 7.6 %copy-start.2 = (f32[16,128]{1,0:T(8,128)S(1)}, f32[16,128]{1,0:T(8,128)}, u32[]{:S(2)}) copy-start(f32[16,128]{1,0:T(8,128)} %param.12) | copy-start | bytes 24580
  3.1 8.3 %copy-start.3 = (f32[8]{0:T(128)S(1)}, f32[8]{0:T(128)}, u32[]{:S(2)}) copy-start(f32[8]{0:T(128)} %constant.69.clone) | copy-start | bytes 100
  3.1 8.4 %copy-start.1 = (f32[16,128]{1,0:T(8,128)S(1)}, f32[16,128]{1,0:T(8,128)}, u32[]{:S(2)}) copy-start(f32[16,128]{1,0:T(8,128)} %param.13) | copy-start | bytes 24580
  3.1 38.1 %all-to-all-start = ((bf16[8,512,256]{2,1,0:T(8,128)(2,1)}), bf16[8,512,256]{2,1,0:T(8,128)(2,1)S(1)}, u32[]{:S(2)}, u32[]{:S(2)}) async-start(bf16[8,512,256]{2,1,0:T(8,128)(2,1)} %broadcast_in_dim.4), calls=%async_computation | async-start | bytes 4194304 | tf_op jit(solution)/shard_map/all_to_all | solution.py:661
  41.2 1.4 copy-start
  42.5 10.0 %collective-permute-start = (bf16[8,512,256]{2,1,0:T(8,128)(2,1)}, bf16[8,512,256]{2,1,0:T(8,128)(2,1)}, u32[]{:S(2)}, u32[]{:S(2)}) collective-permute-start(bf16[8,512,256]{2,1,0:T(8,128)(2,1)} %shard_map.136.mine_far.mine), channel_id=1, source_target_pairs={{0,1},{1,0},{2,3},{3,2},{4,5},{5,4},{6,7},{7,6},{8,9},{9,8},{10,11... | collective-permute-start | bytes 6291464 | tf_op jit(solution)/shard_map/ppermute | solution.py:30
  44.2 33.1 %collective-permute-start.3 = (bf16[8,512,256]{2,1,0:T(8,128)(2,1)}, bf16[8,512,256]{2,1,0:T(8,128)(2,1)}, u32[]{:S(2)}, u32[]{:S(2)}) collective-permute-start(bf16[8,512,256]{2,1,0:T(8,128)(2,1)} %shard_map.136.mine_far.mine), channel_id=1, source_target_pairs={{1,17},{3,19},{5,21},{7,23},{9,25},{11,27},{13,29},{15,31},{16,0},... | collective-permute-start | bytes 6291464 | tf_op jit(solution)/shard_map/ppermute | solution.py:702
  47.8 50.1 %collective-permute-start.2 = (bf16[3,4096,128]{2,1,0:T(8,128)(2,1)}, bf16[3,4096,128]{2,1,0:T(8,128)(2,1)}, u32[]{:S(2)}, u32[]{:S(2)}) collective-permute-start(bf16[3,4096,128]{2,1,0:T(8,128)(2,1)} %param.10), channel_id=1, source_target_pairs={{0,1},{1,0},{2,3},{3,2},{4,5},{5,4},{6,7},{7,6},{8,9},{9,8},{10,11... | collective-permute-start | bytes 9437192 | tf_op jit(solution)/shard_map/ppermute | solution.py:30
  60.6 23.4 %all-to-all-start.1 = ((f32[16,48,128]{2,1,0:T(8,128)}), f32[16,48,128]{2,1,0:T(8,128)}, u32[]{:S(2)}, u32[]{:S(2)}) async-start(f32[16,48,128]{2,1,0:T(8,128)} %get-tuple-element.29), calls=%async_computation.1 | async-start | bytes 786432 | tf_op jit(solution)/shard_map/all_to_all | solution.py:661
  83.9 24.6 %collective-permute-start.4 = (bf16[8,512,256]{2,1,0:T(8,128)(2,1)}, bf16[8,512,256]{2,1,0:T(8,128)(2,1)}, u32[]{:S(2)}, u32[]{:S(2)}) collective-permute-start(bf16[8,512,256]{2,1,0:T(8,128)(2,1)} %shard_map.143.given), channel_id=1, source_target_pairs={{0,1},{2,3},{4,5},{6,7},{8,9},{10,11},{12,13},{14,15},{17,16},{19,... | collective-permute-start | bytes 6291464 | tf_op jit(solution)/shard_map/ppermute | solution.py:724
  93.2 5.3 %collective-permute-start.1 = (bf16[544,384]{1,0:T(8,128)(2,1)}, bf16[544,384]{1,0:T(8,128)(2,1)}, u32[]{:S(2)}, u32[]{:S(2)}) collective-permute-start(bf16[544,384]{1,0:T(8,128)(2,1)} %get-tuple-element.38.low), channel_id=1, source_target_pairs={{0,1},{1,0},{2,3},{3,2},{4,5},{5,4},{6,7},{7,6},{8,9},{9,8},{10,11... | collective-permute-start | bytes 1253384 | tf_op jit(solution)/shard_map/ppermute | solution.py:30
  96.9 11.7 %collective-permute-start.5 = (bf16[544,384]{1,0:T(8,128)(2,1)}, bf16[544,384]{1,0:T(8,128)(2,1)}, u32[]{:S(2)}, u32[]{:S(2)}) collective-permute-start(bf16[544,384]{1,0:T(8,128)(2,1)} %get-tuple-element.38.low), channel_id=1, source_target_pairs={{0,16},{16,0},{32,48},{48,32},{64,80},{80,64},{96,112},{112,96},{1... | collective-permute-start | bytes 1253384 | tf_op jit(solution)/shard_map/ppermute | solution.py:34
  103.9 35.8 %all-to-all-start.2 = ((bf16[8,256,512]{2,1,0:T(8,128)(2,1)}), bf16[8,256,512]{2,1,0:T(8,128)(2,1)}, u32[]{:S(2)}, u32[]{:S(2)}) async-start(bf16[8,256,512]{2,1,0:T(8,128)(2,1)} %shard_map.141._), calls=%async_computation.2 | async-start | bytes 4194304 | tf_op jit(solution)/shard_map/all_to_all | solution.py:661
  114.7 16.2 %collective-permute-start.6 = (bf16[544,384]{1,0:T(8,128)(2,1)}, bf16[544,384]{1,0:T(8,128)(2,1)}, u32[]{:S(2)}, u32[]{:S(2)}) collective-permute-start(bf16[544,384]{1,0:T(8,128)(2,1)} %get-tuple-element.40), channel_id=1, source_target_pairs={{0,32},{16,48},{32,64},{48,80},{64,96},{80,112},{96,128},{112,144}... | collective-permute-start | bytes 1253384 | tf_op jit(solution)/shard_map/ppermute | solution.py:34
  114.8 16.1 %collective-permute-start.7 = (bf16[544,384]{1,0:T(8,128)(2,1)}, bf16[544,384]{1,0:T(8,128)(2,1)}, u32[]{:S(2)}, u32[]{:S(2)}) collective-permute-start(bf16[544,384]{1,0:T(8,128)(2,1)} %get-tuple-element.41), channel_id=1, source_target_pairs={{0,224},{16,240},{32,0},{48,16},{64,32},{80,48},{96,64},{112,80},{... | collective-permute-start | bytes 1253384 | tf_op jit(solution)/shard_map/ppermute | solution.py:34
  117.4 10.7 %collective-permute-start.8 = (bf16[160,384]{1,0:T(8,128)(2,1)}, bf16[160,384]{1,0:T(8,128)(2,1)}, u32[]{:S(2)}, u32[]{:S(2)}) collective-permute-start(bf16[160,384]{1,0:T(8,128)(2,1)} %get-tuple-element.43), channel_id=1, source_target_pairs={{0,64},{16,80},{32,96},{48,112},{64,128},{80,144},{96,160},{112,17... | collective-permute-start | bytes 368648 | tf_op jit(solution)/shard_map/ppermute | solution.py:34
  117.4 13.4 %collective-permute-start.9 = (bf16[160,384]{1,0:T(8,128)(2,1)}, bf16[160,384]{1,0:T(8,128)(2,1)}, u32[]{:S(2)}, u32[]{:S(2)}) collective-permute-start(bf16[160,384]{1,0:T(8,128)(2,1)} %get-tuple-element.44), channel_id=1, source_target_pairs={{0,192},{16,208},{32,224},{48,240},{64,0},{80,16},{96,32},{112,48}... | collective-permute-start | bytes 368648 | tf_op jit(solution)/shard_map/ppermute | solution.py:34
  133.1 15.1 %collective-permute-start.10 = (bf16[320,384]{1,0:T(8,128)(2,1)}, bf16[320,384]{1,0:T(8,128)(2,1)}, u32[]{:S(2)}, u32[]{:S(2)}) collective-permute-start(bf16[320,384]{1,0:T(8,128)(2,1)} %get-tuple-element.45), channel_id=1, source_target_pairs={{0,192},{16,208},{32,224},{48,240},{64,0},{80,16},{96,32},{112,48}... | collective-permute-start | bytes 737288 | tf_op jit(solution)/shard_map/ppermute | solution.py:34
  137.7 10.5 %collective-permute-start.11 = (bf16[288,384]{1,0:T(8,128)(2,1)}, bf16[288,384]{1,0:T(8,128)(2,1)}, u32[]{:S(2)}, u32[]{:S(2)}) collective-permute-start(bf16[288,384]{1,0:T(8,128)(2,1)} %get-tuple-element.46), channel_id=1, source_target_pairs={{0,64},{16,80},{32,96},{48,112},{64,128},{80,144},{96,160},{112,17... | collective-permute-start | bytes 663560 | tf_op jit(solution)/shard_map/ppermute | solution.py:34

commit v4 on v3

--- a/solution.py
+++ b/solution.py
@@ -113,7 +113,7 @@
     return total + taps[k, 2:3, :] * ext[6 : 6 + ROWS, lanes]
 
 
-def half_kernel(at, mine_far, weight_far, out, mine, weight, made, sems):
+def half_kernel(at, mine_far, weight_far, _, out, mine, weight, made, sems):
     copies = stream([mine_far], weight_far, at[0], [mine], weight, sems)
     for b in range(0, 8, 2):
         for i in range(b, b + 2):
@@ -692,12 +692,11 @@
     pw = jnp.concatenate(pw, axis=1)
     res = residue.reshape(2 * MODES, 128)
 
-    mine = after(mine, pw, at)
     other = to_chan(mine, 0, 0, 1)
     weight = in_weight.reshape(3, 8, 2, 256, 128)
     block, wblock = ((8, ROWS, 256), BF16), ((3, 8, 256, 128), BF16)
     half = far_call(
-        half_kernel, 4.0, at, [((ROWS, 384), F32)], [block, wblock, ((ROWS, 384), F32)], 48, mine, weight
+        half_kernel, 4.0, at, [((ROWS, 384), F32)], [block, wblock, ((ROWS, 384), F32)], 48, mine, weight, pw
     )[0]
     given = lax.ppermute(mine, ("seq", "chan"), joint_pairs("give"))
     ext, prod, gl, st, send = call(

time: 153 us -> 149 us (0.974)
  blocking collectives: 0 us -> 34.1 us
  waiting for transfers between devices: 50.3 us -> 21.5 us
  starting transfers between devices: 43.6 us -> 37 us
  local copies, waits for them, and re-layouts: 4.43 us -> 1.68 us
    all_to_all x0 -> x1, blocking collectives: none -> 34.1 us  [exchange(): lax.all_to_all(x, axis, split_axis=0, concat_axis=0, tiled=True, axis_ind...]
    all_to_all x3 -> x2, waiting for transfers between devices: 36.1 us -> 7.02 us  [exchange(): lax.all_to_all(x, axis, split_axis=0, concat_axis=0, tiled=True, axis_ind...]
    all_to_all x3 -> x2, starting transfers between devices: 21.6 us -> 12.9 us  [exchange(): lax.all_to_all(x, axis, split_axis=0, concat_axis=0, tiled=True, axis_ind...]
    ppermute x3, starting transfers between devices: 5.23 us -> 7.38 us  [to_chan(): return lax.ppermute(x, 'chan', chan_pairs(dx, dy, dc))]
  transfers between devices with their start and end apart: 15 -> 14, of which waited for: 7 -> 6; matrix products, arithmetic and copies ran while one was open for 2% -> 2% of each run, Pallas kernels for 31% -> 32%
where the time goes in v4:
time: 149 us; the launch traced here: 147 us
  Pallas kernels  49.3 us (33%)
  starting transfers between devices  37 us (25%)
  blocking collectives  34.1 us (23%)
  waiting for transfers between devices  21.5 us (14%)
  other arithmetic  2.4 us (2%)
  local copies, waits for them, and re-layouts  1.68 us (1%)
    pallas_call x10, Pallas kernels, raw_call(): pl.pallas_call(kernel, in_specs=in_specs, out_specs=out_specs, out_shape=...  49.3 us
    all_to_all x1, blocking collectives, exchange(): lax.all_to_all(x, axis, split_axis=0, concat_axis=0, tiled=True, axis_ind...  34.1 us
    ppermute x7, waiting for transfers between devices, to_seq(): return lax.ppermute(x, 'seq', seq_pairs(dz, dy))  13.6 us
    all_to_all x2, starting transfers between devices, exchange(): lax.all_to_all(x, axis, split_axis=0, concat_axis=0, tiled=True, axis_ind...  12.9 us
    ppermute x7, starting transfers between devices, to_seq(): return lax.ppermute(x, 'seq', seq_pairs(dz, dy))  11.7 us
    ppermute x3, starting transfers between devices, to_chan(): return lax.ppermute(x, 'chan', chan_pairs(dx, dy, dc))  7.38 us
    all_to_all x2, waiting for transfers between devices, exchange(): lax.all_to_all(x, axis, split_axis=0, concat_axis=0, tiled=True, axis_ind...  7.02 us
    ppermute x1, starting transfers between devices, on_device(): given = lax.ppermute(mine, ('seq', 'chan'), joint_pairs('give'))  3.74 us
  transfers between devices with their start and end apart: 14, of which 6 were waited for; matrix products, arithmetic and copies ran while one was open for 2% of the time, Pallas kernels for 32%

profile of v4, /device:TPU:1, one launch (start us, length us, event | category | flops | bytes accessed | tf_op | source)
XLA Modules:
  0.0 147.0 jit_solution(7437581253465445824)
XLA Ops:
  0.6 1.1 broadcast_in_dim.4
  1.8 34.1 %all_to_all.15.mine_far.mine = bf16[8,512,256]{2,1,0:T(8,128)(2,1)} all-to-all(bf16[8,512,256]{2,1,0:T(8,128)(2,1)S(1)} %broadcast_in_dim.4), channel_id=1, replica_groups={{0,2,4,6,8,10,12,14},{1,3,5,7,9,11,13,15},{16,18,20,22,24,26,28,30},{17..., dimensions={0} | all-to-all | bytes 4194304 | tf_op jit(solution)/shard_map/all_to_all | solution.py:661
  35.8 2.5 %collective-permute-start = (bf16[8,512,256]{2,1,0:T(8,128)(2,1)}, bf16[8,512,256]{2,1,0:T(8,128)(2,1)}, u32[]{:S(2)}, u32[]{:S(2)}) collective-permute-start(bf16[8,512,256]{2,1,0:T(8,128)(2,1)} %all_to_all.15.mine_far.mine), channel_id=1, source_target_pairs={{0,1},{1,0},{2,3},{3,2},{4,5},{5,4},{6,7},{7,6},{8,9},{9,8},{10,11... | collective-permute-start | bytes 6291464 | tf_op jit(solution)/shard_map/ppermute | solution.py:30
  38.5 1.5 %fusion.5 = (f32[24,16,128]{2,1,0:T(8,128)S(1)}, f32[24,16,128]{2,1,0:T(8,128)S(1)}) fusion(f32[16,128]{1,0:T(8,128)S(1)} %get-tuple-element.55, f32[16,128]{1,0:T(8,128)S(1)} %get-tuple-element.54, f32[24]{0:T(128)S(1)} %pad_maximum_fusion.1, f32[16,128]{1,0:T(8,128)S(1)} %neg.4), kind=kLoop, calls=%fused_computation.10 | loop fusion | flops 540672 | bytes 417888 | tf_op jit(solution)/shard_map/mul | solution.py:43
  40.0 3.7 %collective-permute-start.3 = (bf16[8,512,256]{2,1,0:T(8,128)(2,1)}, bf16[8,512,256]{2,1,0:T(8,128)(2,1)}, u32[]{:S(2)}, u32[]{:S(2)}) collective-permute-start(bf16[8,512,256]{2,1,0:T(8,128)(2,1)} %all_to_all.15.mine_far.mine), channel_id=1, source_target_pairs={{1,17},{3,19},{5,21},{7,23},{9,25},{11,27},{13,29},{15,31},{16,0},... | collective-permute-start | bytes 6291464 | tf_op jit(solution)/shard_map/ppermute | solution.py:701
  43.7 0.6 stack.35.at.refs_0_
  44.3 0.8 pad_maximum_fusion._.refs_6_.refs_3_.refs_2_
  45.1 4.7 %shard_map.136.refs_3_ = f32[512,384]{1,0:T(8,128)} custom-call(s32[7]{0:T(128)} %stack.35.at.refs_0_, bf16[8,512,256]{2,1,0:T(8,128)(2,1)} %all_to_all.15.mine_far.mine, bf16[3,8,2,256,128]{4,3,2,1,0:T(8,128)(2,1)} %bitcast.7.weight_far.refs_2_.weight, f32[24,32,128]{2,1,0:T(8,128)} %pad_maximum_fusion._.refs_6_.refs_3_.refs_2_), custom_call_target="tpu_custom_call" | custom-call | flops 4400000000 | tf_op jit(solution)/shard_map/pallas_call | solution.py:569
  49.8 8.0 %shard_map.137 = (f32[528,384]{1,0:T(8,128)}, f32[576,128]{1,0:T(8,128)}, f32[576,128]{1,0:T(8,128)}, f32[64,8,128]{2,1,0:T(8,128)}, f32[16,48,128]{2,1,0:T(8,128)}) custom-call(s32[7]{0:T(128)} %stack.35.at.refs_0_, bf16[8,512,256]{2,1,0:T(8,128)(2,1)} %collective-permute-done.refs_1_.other, bf16[3,8,2,256,128]{4,3,2,1,0:T(8,128)(2,1)} %bitcast.7.weight_far.refs_2_.weight, ...), custom_call_target="tpu_custom_call" | custom-call | flops 8800000000 | tf_op jit(solution)/shard_map/pallas_call | solution.py:569
  57.8 8.3 %all-to-all-start.1 = ((f32[16,48,128]{2,1,0:T(8,128)}), f32[16,48,128]{2,1,0:T(8,128)}, u32[]{:S(2)}, u32[]{:S(2)}) async-start(f32[16,48,128]{2,1,0:T(8,128)} %get-tuple-element.29), calls=%async_computation.1 | async-start | bytes 786432 | tf_op jit(solution)/shard_map/all_to_all | solution.py:661
  66.2 7.3 %shard_map.138 = (f32[64,8,128]{2,1,0:T(8,128)}, f32[64,8,128]{2,1,0:T(8,128)}, f32[96,8,128]{2,1,0:T(8,128)}) custom-call(f32[576,128]{1,0:T(8,128)} %get-tuple-element.30.refs_0_, f32[576,128]{1,0:T(8,128)} %get-tuple-element.31.refs_1_, f32[64,8,128]{2,1,0:T(8,128)} %get-tuple-element.32.refs_2_.refs_8_, ...), custom_call_target="tpu_custom_call" | custom-call | flops 7699999744 | tf_op jit(solution)/shard_map/pallas_call | solution.py:569
  73.5 4.9 %all-to-all-done.1.refs_1_.__1_ = f32[16,48,128]{2,1,0:T(8,128)} async-done(((f32[16,48,128]{2,1,0:T(8,128)}), f32[16,48,128]{2,1,0:T(8,128)}, u32[]{:S(2)}, u32[]{:S(2)}) %all-to-all-start.1) | async-done | bytes 393248 | tf_op jit(solution)/shard_map/all_to_all | solution.py:661
  78.4 1.3 collective-permute-start.4
  79.6 8.1 %shard_map.139 = (f32[128,512]{1,0:T(8,128)}, bf16[544,384]{1,0:T(8,128)(2,1)}) custom-call(s32[7]{0:T(128)} %stack.35.at.refs_0_, f32[16,48,128]{2,1,0:T(8,128)} %all-to-all-done.1.refs_1_.__1_, f32[24,32,128]{2,1,0:T(8,128)} %pad_maximum_fusion._.refs_6_.refs_3_.refs_2_, f32[32,128]{1,0:T(8,128)} %bitcast.13, f32[1,128]{1,0:T(1,128)} %bitcast.14, ...), custom_call_target="tpu_custom_call" | custom-call | flops 8800000000 | tf_op jit(solution)/shard_map/pallas_call | solution.py:569
  87.7 4.9 %collective-permute-start.1 = (bf16[544,384]{1,0:T(8,128)(2,1)}, bf16[544,384]{1,0:T(8,128)(2,1)}, u32[]{:S(2)}, u32[]{:S(2)}) collective-permute-start(bf16[544,384]{1,0:T(8,128)(2,1)} %get-tuple-element.38.low), channel_id=1, source_target_pairs={{0,1},{1,0},{2,3},{3,2},{4,5},{5,4},{6,7},{7,6},{8,9},{9,8},{10,11... | collective-permute-start | bytes 1253384 | tf_op jit(solution)/shard_map/ppermute | solution.py:30
  92.6 0.9 collective-permute-start.5
  93.5 0.8 collective-permute-done.1.low_core
  94.4 5.3 %shard_map.140._ = bf16[8,256,512]{2,1,0:T(8,128)(2,1)} custom-call(s32[7]{0:T(128)} %stack.35.at.refs_0_, bf16[544,384]{1,0:T(8,128)(2,1)} %get-tuple-element.38.low, bf16[544,384]{1,0:T(8,128)(2,1)} %collective-permute-done.1.low_core, bf16[3,8,2,256,128]{4,3,2,1,0:T(8,128)(2,1)} %bitcast.7.weight_far.refs_2_.weight, ...), custom_call_target="tpu_custom_call" | custom-call | flops 6600000000 | tf_op jit(solution)/shard_map/pallas_call | solution.py:569
  99.7 4.5 %all-to-all-start.2 = ((bf16[8,256,512]{2,1,0:T(8,128)(2,1)}), bf16[8,256,512]{2,1,0:T(8,128)(2,1)}, u32[]{:S(2)}, u32[]{:S(2)}) async-start(bf16[8,256,512]{2,1,0:T(8,128)(2,1)} %shard_map.140._), calls=%async_computation.2 | async-start | bytes 4194304 | tf_op jit(solution)/shard_map/all_to_all | solution.py:661
  104.2 6.1 %shard_map.143 = (bf16[544,384]{1,0:T(8,128)(2,1)}, bf16[544,384]{1,0:T(8,128)(2,1)}, bf16[160,384]{1,0:T(8,128)(2,1)}, bf16[160,384]{1,0:T(8,128)(2,1)}, f32[2,...) custom-call(s32[7]{0:T(128)} %stack.35.at.refs_0_, bf16[8,512,256]{2,1,0:T(8,128)(2,1)} %all_to_all.15.mine_far.mine, ...), custom_call_target="tpu_custom_call" | custom-call | flops 44000002048 | tf_op jit(solution)/shard_map/pallas_call | solution.py:569
  110.4 0.4 collective-permute-start.6
  110.8 2.4 %collective-permute-start.7 = (bf16[544,384]{1,0:T(8,128)(2,1)}, bf16[544,384]{1,0:T(8,128)(2,1)}, u32[]{:S(2)}, u32[]{:S(2)}) collective-permute-start(bf16[544,384]{1,0:T(8,128)(2,1)} %get-tuple-element.41), channel_id=1, source_target_pairs={{0,224},{16,240},{32,0},{48,16},{64,32},{80,48},{96,64},{112,80},{... | collective-permute-start | bytes 1253384 | tf_op jit(solution)/shard_map/ppermute | solution.py:34
  113.1 3.6 %collective-permute-start.9 = (bf16[160,384]{1,0:T(8,128)(2,1)}, bf16[160,384]{1,0:T(8,128)(2,1)}, u32[]{:S(2)}, u32[]{:S(2)}) collective-permute-start(bf16[160,384]{1,0:T(8,128)(2,1)} %get-tuple-element.44), channel_id=1, source_target_pairs={{0,192},{16,208},{32,224},{48,240},{64,0},{80,16},{96,32},{112,48}... | collective-permute-start | bytes 368648 | tf_op jit(solution)/shard_map/ppermute | solution.py:34
  116.7 7.3 %collective-permute-done.8.refs_2_.refs_7_ = bf16[160,384]{1,0:T(8,128)(2,1)} collective-permute-done((bf16[160,384]{1,0:T(8,128)(2,1)}, bf16[160,384]{1,0:T(8,128)(2,1)}, u32[]{:S(2)}, u32[]{:S(2)}) %collective-permute-start.8) | collective-permute-done | bytes 122912 | tf_op jit(solution)/shard_map/ppermute | solution.py:34
  124.0 2.5 %collective-permute-done.9.refs_4_.refs_8_ = bf16[160,384]{1,0:T(8,128)(2,1)} collective-permute-done((bf16[160,384]{1,0:T(8,128)(2,1)}, bf16[160,384]{1,0:T(8,128)(2,1)}, u32[]{:S(2)}, u32[]{:S(2)}) %collective-permute-start.9) | collective-permute-done | bytes 122912 | tf_op jit(solution)/shard_map/ppermute | solution.py:34
  126.5 2.3 %shard_map.145 = (bf16[320,384]{1,0:T(8,128)(2,1)}, bf16[288,384]{1,0:T(8,128)(2,1)}) custom-call(f32[2,256,384]{2,1,0:T(8,128)} %get-tuple-element.42.refs_0_, bf16[544,384]{1,0:T(8,128)(2,1)} %collective-permute-done.6.refs_1_.refs_5_, bf16[160,384]{1,0:T(8,128)(2,1)} %collective-permute-done.8.refs_2_.refs_7_, ...), custom_call_target="tpu_custom_call" | custom-call | flops 2200000000 | tf_op jit(solution)/shard_map/pallas_call | solution.py:569
  128.8 4.5 %collective-permute-start.10 = (bf16[320,384]{1,0:T(8,128)(2,1)}, bf16[320,384]{1,0:T(8,128)(2,1)}, u32[]{:S(2)}, u32[]{:S(2)}) collective-permute-start(bf16[320,384]{1,0:T(8,128)(2,1)} %get-tuple-element.45), channel_id=1, source_target_pairs={{0,192},{16,208},{32,224},{48,240},{64,0},{80,16},{96,32},{112,48}... | collective-permute-start | bytes 737288 | tf_op jit(solution)/shard_map/ppermute | solution.py:34
  133.3 2.1 %all-to-all-done.2.refs_0_ = bf16[8,256,512]{2,1,0:T(8,128)(2,1)} async-done(((bf16[8,256,512]{2,1,0:T(8,128)(2,1)}), bf16[8,256,512]{2,1,0:T(8,128)(2,1)}, u32[]{:S(2)}, u32[]{:S(2)}) %all-to-all-start.2) | async-done | bytes 2097184 | tf_op jit(solution)/shard_map/all_to_all | solution.py:661
  135.4 2.7 %shard_map.141.refs_9_ = f32[512,256]{1,0:T(8,128)} custom-call(bf16[8,256,512]{2,1,0:T(8,128)(2,1)} %all-to-all-done.2.refs_0_), custom_call_target="tpu_custom_call" | custom-call | flops 2750000128 | tf_op jit(solution)/shard_map/pallas_call | solution.py:569
  138.1 2.1 %shard_map.144.refs_1_ = f32[256,384]{1,0:T(8,128)} custom-call(f32[256,384]{1,0:T(8,128)} %get-tuple-element.39.refs_0_, bf16[544,384]{1,0:T(8,128)(2,1)} %collective-permute-done.6.refs_1_.refs_5_, bf16[544,384]{1,0:T(8,128)(2,1)} %collective-permute-done.7.refs_2_.refs_3_.refs_6_), custom_call_target="tpu_custom_call" | custom-call | flops 2200000000 | tf_op jit(solution)/shard_map/pallas_call | solution.py:569
  140.2 3.9 %collective-permute-done.11.refs_3_ = bf16[288,384]{1,0:T(8,128)(2,1)} collective-permute-done((bf16[288,384]{1,0:T(8,128)(2,1)}, bf16[288,384]{1,0:T(8,128)(2,1)}, u32[]{:S(2)}, u32[]{:S(2)}) %collective-permute-start.11) | collective-permute-done | bytes 221216 | tf_op jit(solution)/shard_map/ppermute | solution.py:34
  144.1 2.7 %shard_map.146 = (f32[3,256,128]{2,1,0:T(8,128)}, f32[2,16,128]{2,1,0:T(8,128)}, f32[3,3,128]{2,1,0:T(4,128)}, f32[1,128]{1,0:T(1,128)}) custom-call(s32[7]{0:T(128)} %stack.35.at.refs_0_, f32[256,384]{1,0:T(8,128)} %shard_map.144.refs_1_, bf16[320,384]{1,0:T(8,128)(2,1)} %collective-permute-done.10.refs_2_, ...), custom_call_target="tpu_custom_call" | custom-call | flops 2750000128 | tf_op jit(solution)/shard_map/pallas_call | solution.py:569
  (22 shorter events, 0.1 us)
Async XLA Ops:
  1.7 36.6 %copy-start.1 = (f32[16,128]{1,0:T(8,128)S(1)}, f32[16,128]{1,0:T(8,128)}, u32[]{:S(2)}) copy-start(f32[16,128]{1,0:T(8,128)} %param.12) | copy-start | bytes 24580
  1.7 36.6 %copy-start.2 = (f32[8]{0:T(128)S(1)}, f32[8]{0:T(128)}, u32[]{:S(2)}) copy-start(f32[8]{0:T(128)} %constant.69.clone) | copy-start | bytes 100
  1.7 36.7 %copy-start = (f32[16,128]{1,0:T(8,128)S(1)}, f32[16,128]{1,0:T(8,128)}, u32[]{:S(2)}) copy-start(f32[16,128]{1,0:T(8,128)} %param.13) | copy-start | bytes 24580
  35.8 13.9 %collective-permute-start = (bf16[8,512,256]{2,1,0:T(8,128)(2,1)}, bf16[8,512,256]{2,1,0:T(8,128)(2,1)}, u32[]{:S(2)}, u32[]{:S(2)}) collective-permute-start(bf16[8,512,256]{2,1,0:T(8,128)(2,1)} %all_to_all.15.mine_far.mine), channel_id=1, source_target_pairs={{0,1},{1,0},{2,3},{3,2},{4,5},{5,4},{6,7},{7,6},{8,9},{9,8},{10,11... | collective-permute-start | bytes 6291464 | tf_op jit(solution)/shard_map/ppermute | solution.py:30
  38.3 55.2 %collective-permute-start.2 = (bf16[3,4096,128]{2,1,0:T(8,128)(2,1)}, bf16[3,4096,128]{2,1,0:T(8,128)(2,1)}, u32[]{:S(2)}, u32[]{:S(2)}) collective-permute-start(bf16[3,4096,128]{2,1,0:T(8,128)(2,1)} %param.10), channel_id=1, source_target_pairs={{0,1},{1,0},{2,3},{3,2},{4,5},{5,4},{6,7},{7,6},{8,9},{9,8},{10,11... | collective-permute-start | bytes 9437192 | tf_op jit(solution)/shard_map/ppermute | solution.py:30
  40.0 33.5 %collective-permute-start.3 = (bf16[8,512,256]{2,1,0:T(8,128)(2,1)}, bf16[8,512,256]{2,1,0:T(8,128)(2,1)}, u32[]{:S(2)}, u32[]{:S(2)}) collective-permute-start(bf16[8,512,256]{2,1,0:T(8,128)(2,1)} %all_to_all.15.mine_far.mine), channel_id=1, source_target_pairs={{1,17},{3,19},{5,21},{7,23},{9,25},{11,27},{13,29},{15,31},{16,0},... | collective-permute-start | bytes 6291464 | tf_op jit(solution)/shard_map/ppermute | solution.py:701
  57.8 20.5 %all-to-all-start.1 = ((f32[16,48,128]{2,1,0:T(8,128)}), f32[16,48,128]{2,1,0:T(8,128)}, u32[]{:S(2)}, u32[]{:S(2)}) async-start(f32[16,48,128]{2,1,0:T(8,128)} %get-tuple-element.29), calls=%async_computation.1 | async-start | bytes 786432 | tf_op jit(solution)/shard_map/all_to_all | solution.py:661
  78.4 25.9 %collective-permute-start.4 = (bf16[8,512,256]{2,1,0:T(8,128)(2,1)}, bf16[8,512,256]{2,1,0:T(8,128)(2,1)}, u32[]{:S(2)}, u32[]{:S(2)}) collective-permute-start(bf16[8,512,256]{2,1,0:T(8,128)(2,1)} %shard_map.142.given), channel_id=1, source_target_pairs={{0,1},{2,3},{4,5},{6,7},{8,9},{10,11},{12,13},{14,15},{17,16},{19,... | collective-permute-start | bytes 6291464 | tf_op jit(solution)/shard_map/ppermute | solution.py:723
  87.7 6.6 %collective-permute-start.1 = (bf16[544,384]{1,0:T(8,128)(2,1)}, bf16[544,384]{1,0:T(8,128)(2,1)}, u32[]{:S(2)}, u32[]{:S(2)}) collective-permute-start(bf16[544,384]{1,0:T(8,128)(2,1)} %get-tuple-element.38.low), channel_id=1, source_target_pairs={{0,1},{1,0},{2,3},{3,2},{4,5},{5,4},{6,7},{7,6},{8,9},{9,8},{10,11... | collective-permute-start | bytes 1253384 | tf_op jit(solution)/shard_map/ppermute | solution.py:30
  92.6 11.6 %collective-permute-start.5 = (bf16[544,384]{1,0:T(8,128)(2,1)}, bf16[544,384]{1,0:T(8,128)(2,1)}, u32[]{:S(2)}, u32[]{:S(2)}) collective-permute-start(bf16[544,384]{1,0:T(8,128)(2,1)} %get-tuple-element.38.low), channel_id=1, source_target_pairs={{0,16},{16,0},{32,48},{48,32},{64,80},{80,64},{96,112},{112,96},{1... | collective-permute-start | bytes 1253384 | tf_op jit(solution)/shard_map/ppermute | solution.py:34
  99.7 35.7 %all-to-all-start.2 = ((bf16[8,256,512]{2,1,0:T(8,128)(2,1)}), bf16[8,256,512]{2,1,0:T(8,128)(2,1)}, u32[]{:S(2)}, u32[]{:S(2)}) async-start(bf16[8,256,512]{2,1,0:T(8,128)(2,1)} %shard_map.140._), calls=%async_computation.2 | async-start | bytes 4194304 | tf_op jit(solution)/shard_map/all_to_all | solution.py:661
  110.4 16.1 %collective-permute-start.6 = (bf16[544,384]{1,0:T(8,128)(2,1)}, bf16[544,384]{1,0:T(8,128)(2,1)}, u32[]{:S(2)}, u32[]{:S(2)}) collective-permute-start(bf16[544,384]{1,0:T(8,128)(2,1)} %get-tuple-element.40), channel_id=1, source_target_pairs={{0,32},{16,48},{32,64},{48,80},{64,96},{80,112},{96,128},{112,144}... | collective-permute-start | bytes 1253384 | tf_op jit(solution)/shard_map/ppermute | solution.py:34
  110.8 15.7 %collective-permute-start.7 = (bf16[544,384]{1,0:T(8,128)(2,1)}, bf16[544,384]{1,0:T(8,128)(2,1)}, u32[]{:S(2)}, u32[]{:S(2)}) collective-permute-start(bf16[544,384]{1,0:T(8,128)(2,1)} %get-tuple-element.41), channel_id=1, source_target_pairs={{0,224},{16,240},{32,0},{48,16},{64,32},{80,48},{96,64},{112,80},{... | collective-permute-start | bytes 1253384 | tf_op jit(solution)/shard_map/ppermute | solution.py:34
  113.1 10.8 %collective-permute-start.8 = (bf16[160,384]{1,0:T(8,128)(2,1)}, bf16[160,384]{1,0:T(8,128)(2,1)}, u32[]{:S(2)}, u32[]{:S(2)}) collective-permute-start(bf16[160,384]{1,0:T(8,128)(2,1)} %get-tuple-element.43), channel_id=1, source_target_pairs={{0,64},{16,80},{32,96},{48,112},{64,128},{80,144},{96,160},{112,17... | collective-permute-start | bytes 368648 | tf_op jit(solution)/shard_map/ppermute | solution.py:34
  113.1 13.3 %collective-permute-start.9 = (bf16[160,384]{1,0:T(8,128)(2,1)}, bf16[160,384]{1,0:T(8,128)(2,1)}, u32[]{:S(2)}, u32[]{:S(2)}) collective-permute-start(bf16[160,384]{1,0:T(8,128)(2,1)} %get-tuple-element.44), channel_id=1, source_target_pairs={{0,192},{16,208},{32,224},{48,240},{64,0},{80,16},{96,32},{112,48}... | collective-permute-start | bytes 368648 | tf_op jit(solution)/shard_map/ppermute | solution.py:34
  128.8 15.3 %collective-permute-start.10 = (bf16[320,384]{1,0:T(8,128)(2,1)}, bf16[320,384]{1,0:T(8,128)(2,1)}, u32[]{:S(2)}, u32[]{:S(2)}) collective-permute-start(bf16[320,384]{1,0:T(8,128)(2,1)} %get-tuple-element.45), channel_id=1, source_target_pairs={{0,192},{16,208},{32,224},{48,240},{64,0},{80,16},{96,32},{112,48}... | collective-permute-start | bytes 737288 | tf_op jit(solution)/shard_map/ppermute | solution.py:34
  133.3 10.8 %collective-permute-start.11 = (bf16[288,384]{1,0:T(8,128)(2,1)}, bf16[288,384]{1,0:T(8,128)(2,1)}, u32[]{:S(2)}, u32[]{:S(2)}) collective-permute-start(bf16[288,384]{1,0:T(8,128)(2,1)} %get-tuple-element.46), channel_id=1, source_target_pairs={{0,64},{16,80},{32,96},{48,112},{64,128},{80,144},{96,160},{112,17... | collective-permute-start | bytes 663560 | tf_op jit(solution)/shard_map/ppermute | solution.py:34

commit v5 on v4

--- a/solution.py
+++ b/solution.py
@@ -434,15 +434,15 @@
     wait_all(copies)
     lturn[...] = jnp.concatenate([left[0].T, left[1].T], axis=0)
     sent = []
-    for n in range(0, 8, 2):
-        wait_all(far[2 * n : 2 * n + 4])
+    for n in range(0, 8, 4):
+        wait_all(far[2 * n : 2 * n + 8])
         cols = [
             jnp.concatenate([right[i, s, k] for s in range(2) for k in range(3)], axis=1)
-            for i in (n, n + 1)
+            for i in range(n, n + 4)
         ]
         cols = jnp.concatenate(cols, axis=0)
         total = jnp.dot(cols, lturn[...], preferred_element_type=F32).astype(BF16)
-        for i in range(2):
+        for i in range(4):
             parts[n + i] = total[256 * i : 256 * i + 256]
             c = pltpu.make_async_copy(parts.at[n + i], out.at[n + i], sems.at[18 + n + i])
             c.start()

time: 149 us -> 149 us (level)
  no operation moved by 1% of the time
where the time goes in v5:
time: 149 us; the launch traced here: 147 us
  Pallas kernels  49.3 us (33%)
  starting transfers between devices  37 us (25%)
  blocking collectives  34.1 us (23%)
  waiting for transfers between devices  21.5 us (14%)
  other arithmetic  2.4 us (2%)
  local copies, waits for them, and re-layouts  1.68 us (1%)
    pallas_call x10, Pallas kernels, raw_call(): pl.pallas_call(kernel, in_specs=in_specs, out_specs=out_specs, out_shape=...  49.3 us
    all_to_all x1, blocking collectives, exchange(): lax.all_to_all(x, axis, split_axis=0, concat_axis=0, tiled=True, axis_ind...  34.1 us
    ppermute x7, waiting for transfers between devices, to_seq(): return lax.ppermute(x, 'seq', seq_pairs(dz, dy))  13.6 us
    all_to_all x2, starting transfers between devices, exchange(): lax.all_to_all(x, axis, split_axis=0, concat_axis=0, tiled=True, axis_ind...  12.9 us
    ppermute x7, starting transfers between devices, to_seq(): return lax.ppermute(x, 'seq', seq_pairs(dz, dy))  11.7 us
    ppermute x3, starting transfers between devices, to_chan(): return lax.ppermute(x, 'chan', chan_pairs(dx, dy, dc))  7.38 us
    all_to_all x2, waiting for transfers between devices, exchange(): lax.all_to_all(x, axis, split_axis=0, concat_axis=0, tiled=True, axis_ind...  7.02 us
    ppermute x1, starting transfers between devices, on_device(): given = lax.ppermute(mine, ('seq', 'chan'), joint_pairs('give'))  3.74 us
  transfers between devices with their start and end apart: 14, of which 6 were waited for; matrix products, arithmetic and copies ran while one was open for 2% of the time, Pallas kernels for 32%

profile of v5, /device:TPU:1, one launch (start us, length us, event | category | flops | bytes accessed | tf_op | source)
XLA Modules:
  0.0 147.0 jit_solution(2967695184474181602)
XLA Ops:
  0.6 1.1 broadcast_in_dim.4
  1.8 34.1 %all_to_all.15.mine_far.mine = bf16[8,512,256]{2,1,0:T(8,128)(2,1)} all-to-all(bf16[8,512,256]{2,1,0:T(8,128)(2,1)S(1)} %broadcast_in_dim.4), channel_id=1, replica_groups={{0,2,4,6,8,10,12,14},{1,3,5,7,9,11,13,15},{16,18,20,22,24,26,28,30},{17..., dimensions={0} | all-to-all | bytes 4194304 | tf_op jit(solution)/shard_map/all_to_all | solution.py:661
  35.8 2.5 %collective-permute-start = (bf16[8,512,256]{2,1,0:T(8,128)(2,1)}, bf16[8,512,256]{2,1,0:T(8,128)(2,1)}, u32[]{:S(2)}, u32[]{:S(2)}) collective-permute-start(bf16[8,512,256]{2,1,0:T(8,128)(2,1)} %all_to_all.15.mine_far.mine), channel_id=1, source_target_pairs={{0,1},{1,0},{2,3},{3,2},{4,5},{5,4},{6,7},{7,6},{8,9},{9,8},{10,11... | collective-permute-start | bytes 6291464 | tf_op jit(solution)/shard_map/ppermute | solution.py:30
  38.5 1.5 %fusion.5 = (f32[24,16,128]{2,1,0:T(8,128)S(1)}, f32[24,16,128]{2,1,0:T(8,128)S(1)}) fusion(f32[16,128]{1,0:T(8,128)S(1)} %get-tuple-element.55, f32[16,128]{1,0:T(8,128)S(1)} %get-tuple-element.54, f32[24]{0:T(128)S(1)} %pad_maximum_fusion.1, f32[16,128]{1,0:T(8,128)S(1)} %neg.4), kind=kLoop, calls=%fused_computation.10 | loop fusion | flops 540672 | bytes 417888 | tf_op jit(solution)/shard_map/mul | solution.py:43
  40.0 3.7 %collective-permute-start.3 = (bf16[8,512,256]{2,1,0:T(8,128)(2,1)}, bf16[8,512,256]{2,1,0:T(8,128)(2,1)}, u32[]{:S(2)}, u32[]{:S(2)}) collective-permute-start(bf16[8,512,256]{2,1,0:T(8,128)(2,1)} %all_to_all.15.mine_far.mine), channel_id=1, source_target_pairs={{1,17},{3,19},{5,21},{7,23},{9,25},{11,27},{13,29},{15,31},{16,0},... | collective-permute-start | bytes 6291464 | tf_op jit(solution)/shard_map/ppermute | solution.py:701
  43.7 0.6 stack.35.at.refs_0_
  44.3 0.8 pad_maximum_fusion._.refs_6_.refs_3_.refs_2_
  45.1 4.7 %shard_map.136.refs_3_ = f32[512,384]{1,0:T(8,128)} custom-call(s32[7]{0:T(128)} %stack.35.at.refs_0_, bf16[8,512,256]{2,1,0:T(8,128)(2,1)} %all_to_all.15.mine_far.mine, bf16[3,8,2,256,128]{4,3,2,1,0:T(8,128)(2,1)} %bitcast.7.weight_far.refs_2_.weight, f32[24,32,128]{2,1,0:T(8,128)} %pad_maximum_fusion._.refs_6_.refs_3_.refs_2_), custom_call_target="tpu_custom_call" | custom-call | flops 4400000000 | tf_op jit(solution)/shard_map/pallas_call | solution.py:569
  49.8 8.0 %shard_map.137 = (f32[528,384]{1,0:T(8,128)}, f32[576,128]{1,0:T(8,128)}, f32[576,128]{1,0:T(8,128)}, f32[64,8,128]{2,1,0:T(8,128)}, f32[16,48,128]{2,1,0:T(8,128)}) custom-call(s32[7]{0:T(128)} %stack.35.at.refs_0_, bf16[8,512,256]{2,1,0:T(8,128)(2,1)} %collective-permute-done.refs_1_.other, bf16[3,8,2,256,128]{4,3,2,1,0:T(8,128)(2,1)} %bitcast.7.weight_far.refs_2_.weight, ...), custom_call_target="tpu_custom_call" | custom-call | flops 8800000000 | tf_op jit(solution)/shard_map/pallas_call | solution.py:569
  57.8 8.3 %all-to-all-start.1 = ((f32[16,48,128]{2,1,0:T(8,128)}), f32[16,48,128]{2,1,0:T(8,128)}, u32[]{:S(2)}, u32[]{:S(2)}) async-start(f32[16,48,128]{2,1,0:T(8,128)} %get-tuple-element.29), calls=%async_computation.1 | async-start | bytes 786432 | tf_op jit(solution)/shard_map/all_to_all | solution.py:661
  66.2 7.3 %shard_map.138 = (f32[64,8,128]{2,1,0:T(8,128)}, f32[64,8,128]{2,1,0:T(8,128)}, f32[96,8,128]{2,1,0:T(8,128)}) custom-call(f32[576,128]{1,0:T(8,128)} %get-tuple-element.30.refs_0_, f32[576,128]{1,0:T(8,128)} %get-tuple-element.31.refs_1_, f32[64,8,128]{2,1,0:T(8,128)} %get-tuple-element.32.refs_2_.refs_8_, ...), custom_call_target="tpu_custom_call" | custom-call | flops 7699999744 | tf_op jit(solution)/shard_map/pallas_call | solution.py:569
  73.5 4.9 %all-to-all-done.1.refs_1_.__1_ = f32[16,48,128]{2,1,0:T(8,128)} async-done(((f32[16,48,128]{2,1,0:T(8,128)}), f32[16,48,128]{2,1,0:T(8,128)}, u32[]{:S(2)}, u32[]{:S(2)}) %all-to-all-start.1) | async-done | bytes 393248 | tf_op jit(solution)/shard_map/all_to_all | solution.py:661
  78.4 1.3 collective-permute-start.4
  79.6 8.1 %shard_map.139 = (f32[128,512]{1,0:T(8,128)}, bf16[544,384]{1,0:T(8,128)(2,1)}) custom-call(s32[7]{0:T(128)} %stack.35.at.refs_0_, f32[16,48,128]{2,1,0:T(8,128)} %all-to-all-done.1.refs_1_.__1_, f32[24,32,128]{2,1,0:T(8,128)} %pad_maximum_fusion._.refs_6_.refs_3_.refs_2_, f32[32,128]{1,0:T(8,128)} %bitcast.13, f32[1,128]{1,0:T(1,128)} %bitcast.14, ...), custom_call_target="tpu_custom_call" | custom-call | flops 8800000000 | tf_op jit(solution)/shard_map/pallas_call | solution.py:569
  87.7 4.9 %collective-permute-start.1 = (bf16[544,384]{1,0:T(8,128)(2,1)}, bf16[544,384]{1,0:T(8,128)(2,1)}, u32[]{:S(2)}, u32[]{:S(2)}) collective-permute-start(bf16[544,384]{1,0:T(8,128)(2,1)} %get-tuple-element.38.low), channel_id=1, source_target_pairs={{0,1},{1,0},{2,3},{3,2},{4,5},{5,4},{6,7},{7,6},{8,9},{9,8},{10,11... | collective-permute-start | bytes 1253384 | tf_op jit(solution)/shard_map/ppermute | solution.py:30
  92.6 0.9 collective-permute-start.5
  93.5 0.8 collective-permute-done.1.low_core
  94.4 5.3 %shard_map.140._ = bf16[8,256,512]{2,1,0:T(8,128)(2,1)} custom-call(s32[7]{0:T(128)} %stack.35.at.refs_0_, bf16[544,384]{1,0:T(8,128)(2,1)} %get-tuple-element.38.low, bf16[544,384]{1,0:T(8,128)(2,1)} %collective-permute-done.1.low_core, bf16[3,8,2,256,128]{4,3,2,1,0:T(8,128)(2,1)} %bitcast.7.weight_far.refs_2_.weight, ...), custom_call_target="tpu_custom_call" | custom-call | flops 6600000000 | tf_op jit(solution)/shard_map/pallas_call | solution.py:569
  99.7 4.5 %all-to-all-start.2 = ((bf16[8,256,512]{2,1,0:T(8,128)(2,1)}), bf16[8,256,512]{2,1,0:T(8,128)(2,1)}, u32[]{:S(2)}, u32[]{:S(2)}) async-start(bf16[8,256,512]{2,1,0:T(8,128)(2,1)} %shard_map.140._), calls=%async_computation.2 | async-start | bytes 4194304 | tf_op jit(solution)/shard_map/all_to_all | solution.py:661
  104.2 6.1 %shard_map.143 = (bf16[544,384]{1,0:T(8,128)(2,1)}, bf16[544,384]{1,0:T(8,128)(2,1)}, bf16[160,384]{1,0:T(8,128)(2,1)}, bf16[160,384]{1,0:T(8,128)(2,1)}, f32[2,...) custom-call(s32[7]{0:T(128)} %stack.35.at.refs_0_, bf16[8,512,256]{2,1,0:T(8,128)(2,1)} %all_to_all.15.mine_far.mine, ...), custom_call_target="tpu_custom_call" | custom-call | flops 44000002048 | tf_op jit(solution)/shard_map/pallas_call | solution.py:569
  110.4 0.4 collective-permute-start.6
  110.8 2.4 %collective-permute-start.7 = (bf16[544,384]{1,0:T(8,128)(2,1)}, bf16[544,384]{1,0:T(8,128)(2,1)}, u32[]{:S(2)}, u32[]{:S(2)}) collective-permute-start(bf16[544,384]{1,0:T(8,128)(2,1)} %get-tuple-element.41), channel_id=1, source_target_pairs={{0,224},{16,240},{32,0},{48,16},{64,32},{80,48},{96,64},{112,80},{... | collective-permute-start | bytes 1253384 | tf_op jit(solution)/shard_map/ppermute | solution.py:34
  113.1 3.6 %collective-permute-start.9 = (bf16[160,384]{1,0:T(8,128)(2,1)}, bf16[160,384]{1,0:T(8,128)(2,1)}, u32[]{:S(2)}, u32[]{:S(2)}) collective-permute-start(bf16[160,384]{1,0:T(8,128)(2,1)} %get-tuple-element.44), channel_id=1, source_target_pairs={{0,192},{16,208},{32,224},{48,240},{64,0},{80,16},{96,32},{112,48}... | collective-permute-start | bytes 368648 | tf_op jit(solution)/shard_map/ppermute | solution.py:34
  116.7 7.3 %collective-permute-done.8.refs_2_.refs_7_ = bf16[160,384]{1,0:T(8,128)(2,1)} collective-permute-done((bf16[160,384]{1,0:T(8,128)(2,1)}, bf16[160,384]{1,0:T(8,128)(2,1)}, u32[]{:S(2)}, u32[]{:S(2)}) %collective-permute-start.8) | collective-permute-done | bytes 122912 | tf_op jit(solution)/shard_map/ppermute | solution.py:34
  124.0 2.5 %collective-permute-done.9.refs_4_.refs_8_ = bf16[160,384]{1,0:T(8,128)(2,1)} collective-permute-done((bf16[160,384]{1,0:T(8,128)(2,1)}, bf16[160,384]{1,0:T(8,128)(2,1)}, u32[]{:S(2)}, u32[]{:S(2)}) %collective-permute-start.9) | collective-permute-done | bytes 122912 | tf_op jit(solution)/shard_map/ppermute | solution.py:34
  126.4 2.3 %shard_map.145 = (bf16[320,384]{1,0:T(8,128)(2,1)}, bf16[288,384]{1,0:T(8,128)(2,1)}) custom-call(f32[2,256,384]{2,1,0:T(8,128)} %get-tuple-element.42.refs_0_, bf16[544,384]{1,0:T(8,128)(2,1)} %collective-permute-done.6.refs_1_.refs_5_, bf16[160,384]{1,0:T(8,128)(2,1)} %collective-permute-done.8.refs_2_.refs_7_, ...), custom_call_target="tpu_custom_call" | custom-call | flops 2200000000 | tf_op jit(solution)/shard_map/pallas_call | solution.py:569
  128.8 4.5 %collective-permute-start.10 = (bf16[320,384]{1,0:T(8,128)(2,1)}, bf16[320,384]{1,0:T(8,128)(2,1)}, u32[]{:S(2)}, u32[]{:S(2)}) collective-permute-start(bf16[320,384]{1,0:T(8,128)(2,1)} %get-tuple-element.45), channel_id=1, source_target_pairs={{0,192},{16,208},{32,224},{48,240},{64,0},{80,16},{96,32},{112,48}... | collective-permute-start | bytes 737288 | tf_op jit(solution)/shard_map/ppermute | solution.py:34
  133.3 2.1 %all-to-all-done.2.refs_0_ = bf16[8,256,512]{2,1,0:T(8,128)(2,1)} async-done(((bf16[8,256,512]{2,1,0:T(8,128)(2,1)}), bf16[8,256,512]{2,1,0:T(8,128)(2,1)}, u32[]{:S(2)}, u32[]{:S(2)}) %all-to-all-start.2) | async-done | bytes 2097184 | tf_op jit(solution)/shard_map/all_to_all | solution.py:661
  135.4 2.7 %shard_map.141.refs_9_ = f32[512,256]{1,0:T(8,128)} custom-call(bf16[8,256,512]{2,1,0:T(8,128)(2,1)} %all-to-all-done.2.refs_0_), custom_call_target="tpu_custom_call" | custom-call | flops 2750000128 | tf_op jit(solution)/shard_map/pallas_call | solution.py:569
  138.1 2.1 %shard_map.144.refs_1_ = f32[256,384]{1,0:T(8,128)} custom-call(f32[256,384]{1,0:T(8,128)} %get-tuple-element.39.refs_0_, bf16[544,384]{1,0:T(8,128)(2,1)} %collective-permute-done.6.refs_1_.refs_5_, bf16[544,384]{1,0:T(8,128)(2,1)} %collective-permute-done.7.refs_2_.refs_3_.refs_6_), custom_call_target="tpu_custom_call" | custom-call | flops 2200000000 | tf_op jit(solution)/shard_map/pallas_call | solution.py:569
  140.2 3.9 %collective-permute-done.11.refs_3_ = bf16[288,384]{1,0:T(8,128)(2,1)} collective-permute-done((bf16[288,384]{1,0:T(8,128)(2,1)}, bf16[288,384]{1,0:T(8,128)(2,1)}, u32[]{:S(2)}, u32[]{:S(2)}) %collective-permute-start.11) | collective-permute-done | bytes 221216 | tf_op jit(solution)/shard_map/ppermute | solution.py:34
  144.1 2.7 %shard_map.146 = (f32[3,256,128]{2,1,0:T(8,128)}, f32[2,16,128]{2,1,0:T(8,128)}, f32[3,3,128]{2,1,0:T(4,128)}, f32[1,128]{1,0:T(1,128)}) custom-call(s32[7]{0:T(128)} %stack.35.at.refs_0_, f32[256,384]{1,0:T(8,128)} %shard_map.144.refs_1_, bf16[320,384]{1,0:T(8,128)(2,1)} %collective-permute-done.10.refs_2_, ...), custom_call_target="tpu_custom_call" | custom-call | flops 2750000128 | tf_op jit(solution)/shard_map/pallas_call | solution.py:569
  (22 shorter events, 0.1 us)
Async XLA Ops:
  1.7 36.6 %copy-start.1 = (f32[16,128]{1,0:T(8,128)S(1)}, f32[16,128]{1,0:T(8,128)}, u32[]{:S(2)}) copy-start(f32[16,128]{1,0:T(8,128)} %param.12) | copy-start | bytes 24580
  1.7 36.6 %copy-start.2 = (f32[8]{0:T(128)S(1)}, f32[8]{0:T(128)}, u32[]{:S(2)}) copy-start(f32[8]{0:T(128)} %constant.69.clone) | copy-start | bytes 100
  1.7 36.7 %copy-start = (f32[16,128]{1,0:T(8,128)S(1)}, f32[16,128]{1,0:T(8,128)}, u32[]{:S(2)}) copy-start(f32[16,128]{1,0:T(8,128)} %param.13) | copy-start | bytes 24580
  35.8 13.9 %collective-permute-start = (bf16[8,512,256]{2,1,0:T(8,128)(2,1)}, bf16[8,512,256]{2,1,0:T(8,128)(2,1)}, u32[]{:S(2)}, u32[]{:S(2)}) collective-permute-start(bf16[8,512,256]{2,1,0:T(8,128)(2,1)} %all_to_all.15.mine_far.mine), channel_id=1, source_target_pairs={{0,1},{1,0},{2,3},{3,2},{4,5},{5,4},{6,7},{7,6},{8,9},{9,8},{10,11... | collective-permute-start | bytes 6291464 | tf_op jit(solution)/shard_map/ppermute | solution.py:30
  38.3 55.2 %collective-permute-start.2 = (bf16[3,4096,128]{2,1,0:T(8,128)(2,1)}, bf16[3,4096,128]{2,1,0:T(8,128)(2,1)}, u32[]{:S(2)}, u32[]{:S(2)}) collective-permute-start(bf16[3,4096,128]{2,1,0:T(8,128)(2,1)} %param.10), channel_id=1, source_target_pairs={{0,1},{1,0},{2,3},{3,2},{4,5},{5,4},{6,7},{7,6},{8,9},{9,8},{10,11... | collective-permute-start | bytes 9437192 | tf_op jit(solution)/shard_map/ppermute | solution.py:30
  40.0 33.5 %collective-permute-start.3 = (bf16[8,512,256]{2,1,0:T(8,128)(2,1)}, bf16[8,512,256]{2,1,0:T(8,128)(2,1)}, u32[]{:S(2)}, u32[]{:S(2)}) collective-permute-start(bf16[8,512,256]{2,1,0:T(8,128)(2,1)} %all_to_all.15.mine_far.mine), channel_id=1, source_target_pairs={{1,17},{3,19},{5,21},{7,23},{9,25},{11,27},{13,29},{15,31},{16,0},... | collective-permute-start | bytes 6291464 | tf_op jit(solution)/shard_map/ppermute | solution.py:701
  57.8 20.5 %all-to-all-start.1 = ((f32[16,48,128]{2,1,0:T(8,128)}), f32[16,48,128]{2,1,0:T(8,128)}, u32[]{:S(2)}, u32[]{:S(2)}) async-start(f32[16,48,128]{2,1,0:T(8,128)} %get-tuple-element.29), calls=%async_computation.1 | async-start | bytes 786432 | tf_op jit(solution)/shard_map/all_to_all | solution.py:661
  78.4 25.9 %collective-permute-start.4 = (bf16[8,512,256]{2,1,0:T(8,128)(2,1)}, bf16[8,512,256]{2,1,0:T(8,128)(2,1)}, u32[]{:S(2)}, u32[]{:S(2)}) collective-permute-start(bf16[8,512,256]{2,1,0:T(8,128)(2,1)} %shard_map.142.given), channel_id=1, source_target_pairs={{0,1},{2,3},{4,5},{6,7},{8,9},{10,11},{12,13},{14,15},{17,16},{19,... | collective-permute-start | bytes 6291464 | tf_op jit(solution)/shard_map/ppermute | solution.py:723
  87.7 6.6 %collective-permute-start.1 = (bf16[544,384]{1,0:T(8,128)(2,1)}, bf16[544,384]{1,0:T(8,128)(2,1)}, u32[]{:S(2)}, u32[]{:S(2)}) collective-permute-start(bf16[544,384]{1,0:T(8,128)(2,1)} %get-tuple-element.38.low), channel_id=1, source_target_pairs={{0,1},{1,0},{2,3},{3,2},{4,5},{5,4},{6,7},{7,6},{8,9},{9,8},{10,11... | collective-permute-start | bytes 1253384 | tf_op jit(solution)/shard_map/ppermute | solution.py:30
  92.6 11.6 %collective-permute-start.5 = (bf16[544,384]{1,0:T(8,128)(2,1)}, bf16[544,384]{1,0:T(8,128)(2,1)}, u32[]{:S(2)}, u32[]{:S(2)}) collective-permute-start(bf16[544,384]{1,0:T(8,128)(2,1)} %get-tuple-element.38.low), channel_id=1, source_target_pairs={{0,16},{16,0},{32,48},{48,32},{64,80},{80,64},{96,112},{112,96},{1... | collective-permute-start | bytes 1253384 | tf_op jit(solution)/shard_map/ppermute | solution.py:34
  99.7 35.7 %all-to-all-start.2 = ((bf16[8,256,512]{2,1,0:T(8,128)(2,1)}), bf16[8,256,512]{2,1,0:T(8,128)(2,1)}, u32[]{:S(2)}, u32[]{:S(2)}) async-start(bf16[8,256,512]{2,1,0:T(8,128)(2,1)} %shard_map.140._), calls=%async_computation.2 | async-start | bytes 4194304 | tf_op jit(solution)/shard_map/all_to_all | solution.py:661
  110.4 16.1 %collective-permute-start.6 = (bf16[544,384]{1,0:T(8,128)(2,1)}, bf16[544,384]{1,0:T(8,128)(2,1)}, u32[]{:S(2)}, u32[]{:S(2)}) collective-permute-start(bf16[544,384]{1,0:T(8,128)(2,1)} %get-tuple-element.40), channel_id=1, source_target_pairs={{0,32},{16,48},{32,64},{48,80},{64,96},{80,112},{96,128},{112,144}... | collective-permute-start | bytes 1253384 | tf_op jit(solution)/shard_map/ppermute | solution.py:34
  110.8 15.7 %collective-permute-start.7 = (bf16[544,384]{1,0:T(8,128)(2,1)}, bf16[544,384]{1,0:T(8,128)(2,1)}, u32[]{:S(2)}, u32[]{:S(2)}) collective-permute-start(bf16[544,384]{1,0:T(8,128)(2,1)} %get-tuple-element.41), channel_id=1, source_target_pairs={{0,224},{16,240},{32,0},{48,16},{64,32},{80,48},{96,64},{112,80},{... | collective-permute-start | bytes 1253384 | tf_op jit(solution)/shard_map/ppermute | solution.py:34
  113.1 10.8 %collective-permute-start.8 = (bf16[160,384]{1,0:T(8,128)(2,1)}, bf16[160,384]{1,0:T(8,128)(2,1)}, u32[]{:S(2)}, u32[]{:S(2)}) collective-permute-start(bf16[160,384]{1,0:T(8,128)(2,1)} %get-tuple-element.43), channel_id=1, source_target_pairs={{0,64},{16,80},{32,96},{48,112},{64,128},{80,144},{96,160},{112,17... | collective-permute-start | bytes 368648 | tf_op jit(solution)/shard_map/ppermute | solution.py:34
  113.1 13.3 %collective-permute-start.9 = (bf16[160,384]{1,0:T(8,128)(2,1)}, bf16[160,384]{1,0:T(8,128)(2,1)}, u32[]{:S(2)}, u32[]{:S(2)}) collective-permute-start(bf16[160,384]{1,0:T(8,128)(2,1)} %get-tuple-element.44), channel_id=1, source_target_pairs={{0,192},{16,208},{32,224},{48,240},{64,0},{80,16},{96,32},{112,48}... | collective-permute-start | bytes 368648 | tf_op jit(solution)/shard_map/ppermute | solution.py:34
  128.8 15.3 %collective-permute-start.10 = (bf16[320,384]{1,0:T(8,128)(2,1)}, bf16[320,384]{1,0:T(8,128)(2,1)}, u32[]{:S(2)}, u32[]{:S(2)}) collective-permute-start(bf16[320,384]{1,0:T(8,128)(2,1)} %get-tuple-element.45), channel_id=1, source_target_pairs={{0,192},{16,208},{32,224},{48,240},{64,0},{80,16},{96,32},{112,48}... | collective-permute-start | bytes 737288 | tf_op jit(solution)/shard_map/ppermute | solution.py:34
  133.3 10.8 %collective-permute-start.11 = (bf16[288,384]{1,0:T(8,128)(2,1)}, bf16[288,384]{1,0:T(8,128)(2,1)}, u32[]{:S(2)}, u32[]{:S(2)}) collective-permute-start(bf16[288,384]{1,0:T(8,128)(2,1)} %get-tuple-element.46), channel_id=1, source_target_pairs={{0,64},{16,80},{32,96},{48,112},{64,128},{80,144},{96,160},{112,17... | collective-permute-start | bytes 663560 | tf_op jit(solution)/shard_map/ppermute | solution.py:34
